TPU v7x, 512 devices: a whole 4x8x8 slice. The times are simulated.
512 devices in a mesh: dp: 32 (over y, x), mp: 16 (over z, core).
Axes of the slice: x: 4, y: 8, z: 8, core: 2. Of those that a mesh axis runs over, the one named last changes fastest.
Arguments:
- tokens: bfloat16 [4096, 4096], P('dp', 'mp'), may hold values from -6 to 6
- cotangent: bfloat16 [4096, 4096], P('dp', 'mp'), may hold values from -6 to 6
- block_mask: int32 [128, 32], P('mp'), may hold values from 0 to 1, as said below
- up_tiles: bfloat16 [512, 128, 128], P('mp'), may hold values from -0.25 to 0.25
- down_tiles: bfloat16 [512, 128, 128], P('mp'), may hold values from -0.25 to 0.25
Outputs:
- output: bfloat16 [4096, 4096], P('dp', 'mp')
- grad_tokens: bfloat16 [4096, 4096], P('dp', 'mp')
- grad_up: bfloat16 [512, 128, 128], P('mp')
- grad_down: bfloat16 [512, 128, 128], P('mp')
Inputs may be any that keep to these rules, and one draw needn't show every extreme that they name: `block_mask`: entries are 0 or 1. Every row block has 2 or more active tiles; each group of 8 row blocks has at most 32 active tiles, some group exactly 32; groups g and g + 8 together hold exactly 48 active tiles.
All inputs are finite; a program needn't handle non-finite values.
Results may differ from a plain program's by a relative error of at most 0.02.
Values may be sent and summed in bfloat16 or wider, within the bound.
No kernel may reach another device: no remote copies, remote signals or barrier semaphores. Data moves between devices by JAX's collectives and lax.ppermute only.
A program may use at most 64 MiB of HBM per device.

v0:
```python
import jax
import jax.numpy as jnp
from jax import lax
from jax.sharding import PartitionSpec as P


def gelu_value(hidden):
    argument = 0.7978845608 * (hidden + 0.044715 * hidden * hidden * hidden)
    return 0.5 * hidden * (1.0 + jnp.tanh(argument))


def gelu_slope(hidden):
    argument = 0.7978845608 * (hidden + 0.044715 * hidden * hidden * hidden)
    tangent = jnp.tanh(argument)
    inner_slope = 0.7978845608 * (1.0 + 3.0 * 0.044715 * hidden * hidden)
    return 0.5 * (1.0 + tangent) + 0.5 * hidden * (1.0 - tangent * tangent) * inner_slope


def slot_table(local_mask, capacity):
    flattened = local_mask.reshape(-1)
    position = jnp.cumsum(flattened) - 1
    slot_ids = jnp.arange(capacity, dtype=jnp.int32)
    cell_ids = jnp.arange(flattened.shape[0], dtype=jnp.int32)
    matches = (flattened[None, :] == 1) & (position[None, :] == slot_ids[:, None])
    chosen = jnp.sum(jnp.where(matches, cell_ids[None, :], 0), axis=1)
    in_use = slot_ids < jnp.sum(flattened)
    col_count = local_mask.shape[1]
    return (chosen // col_count, chosen % col_count, in_use)


def first_section(
    panels_in, panels_back, slot_rows, slot_cols, weight_use, up_work, down_work, row_count
):
    in_picked = jnp.take(panels_in, slot_cols, axis=1)
    back_picked = jnp.take(panels_back, slot_cols, axis=1)
    row_hot = (slot_rows[:, None] == jnp.arange(row_count, dtype=jnp.int32)[None, :]).astype(
        jnp.float32
    ) * weight_use[:, None]
    hidden_part = jnp.einsum("tsi,sio->tso", in_picked, up_work, preferred_element_type=jnp.float32)
    dact_part = jnp.einsum(
        "tsc,shc->tsh", back_picked, down_work, preferred_element_type=jnp.float32
    )
    hidden_rows = jnp.einsum("tso,sr->tro", hidden_part, row_hot, precision=lax.Precision.HIGHEST)
    dact_rows = jnp.einsum("tsh,sr->trh", dact_part, row_hot, precision=lax.Precision.HIGHEST)
    return (in_picked, back_picked, hidden_rows, dact_rows)


def activate(hidden, dact):
    return (
        gelu_value(hidden).astype(jnp.bfloat16),
        (dact * gelu_slope(hidden)).astype(jnp.bfloat16),
    )


def second_section(
    in_picked,
    back_picked,
    act_all,
    pre_all,
    slot_rows,
    slot_cols,
    weight_use,
    up_work,
    down_work,
    col_blocks,
):
    act_picked = jnp.take(act_all, slot_rows, axis=1)
    pre_picked = jnp.take(pre_all, slot_rows, axis=1)
    column_hot = (slot_cols[:, None] == jnp.arange(col_blocks, dtype=jnp.int32)[None, :]).astype(
        jnp.float32
    ) * weight_use[:, None]
    out_part = jnp.einsum("tsh,shc->tsc", act_picked, down_work, preferred_element_type=jnp.float32)
    out_cols = jnp.einsum("tsc,sk->tkc", out_part, column_hot, precision=lax.Precision.HIGHEST)
    grad_part = jnp.einsum("tsh,sih->tsi", pre_picked, up_work, preferred_element_type=jnp.float32)
    grad_cols = jnp.einsum("tsc,sk->tkc", grad_part, column_hot, precision=lax.Precision.HIGHEST)
    grad_down = (
        jnp.einsum("tsh,tsc->shc", act_picked, back_picked, preferred_element_type=jnp.float32)
        * weight_use[:, None, None]
    )
    grad_up = (
        jnp.einsum("tsi,tsh->sih", in_picked, pre_picked, preferred_element_type=jnp.float32)
        * weight_use[:, None, None]
    )
    return (out_cols, grad_cols, grad_up, grad_down)


def reduce_tiles(grad_up, grad_down):
    summed_up, summed_down = (
        lax.psum(grad_up.astype(jnp.bfloat16), "dp").astype(jnp.float32),
        lax.psum(grad_down.astype(jnp.bfloat16), "dp").astype(jnp.float32),
    )
    return (summed_up.astype(jnp.bfloat16), summed_down.astype(jnp.bfloat16))


def body(tokens, cotangent, block_mask, up_tiles, down_tiles):
    capacity = up_tiles.shape[0]
    block_size = up_tiles.shape[1]
    row_blocks = block_mask.shape[0]
    col_blocks = block_mask.shape[1]
    gathered_in, gathered_back = (
        lax.all_gather(tokens, "mp", axis=1, tiled=True),
        lax.all_gather(cotangent, "mp", axis=1, tiled=True),
    )
    tok_rows = gathered_in.shape[0]
    panels_in = gathered_in.reshape(tok_rows, col_blocks, block_size)
    panels_back = gathered_back.reshape(tok_rows, col_blocks, block_size)
    own_table = slot_table(block_mask, capacity)
    own_use = own_table[2].astype(jnp.float32)
    in_picked, back_picked, hidden_rows, dact_rows = first_section(
        panels_in,
        panels_back,
        own_table[0],
        own_table[1],
        own_use,
        up_tiles,
        down_tiles,
        row_blocks,
    )
    activated, pre_grad = activate(hidden_rows, dact_rows)
    out_cols, grad_cols, grad_up, grad_down = second_section(
        in_picked,
        back_picked,
        activated,
        pre_grad,
        own_table[0],
        own_table[1],
        own_use,
        up_tiles,
        down_tiles,
        col_blocks,
    )
    final_up, final_down = reduce_tiles(grad_up, grad_down)
    output, grad_tokens = (
        lax.psum_scatter(
            out_cols.reshape(tok_rows, col_blocks * block_size).astype(jnp.bfloat16),
            "mp",
            scatter_dimension=1,
            tiled=True,
        ).astype(jnp.float32),
        lax.psum_scatter(
            grad_cols.reshape(tok_rows, col_blocks * block_size).astype(jnp.bfloat16),
            "mp",
            scatter_dimension=1,
            tiled=True,
        ).astype(jnp.float32),
    )
    return (output.astype(jnp.bfloat16), grad_tokens.astype(jnp.bfloat16), final_up, final_down)


def solution(mesh):
    in_specs = (
        P("dp", "mp"),
        P("dp", "mp"),
        P("mp", None),
        P("mp", None, None),
        P("mp", None, None),
    )
    out_specs = (P("dp", "mp"), P("dp", "mp"), P("mp", None, None), P("mp", None, None))
    return jax.shard_map(body, mesh=mesh, in_specs=in_specs, out_specs=out_specs, check_vma=False)
```

profile of v0, /device:TPU:6, one launch (start us, length us, event | category | flops | bytes accessed | tf_op | source)
XLA Modules:
  0.0 416.9 jit_solution(8813385863941740147)
XLA Ops:
  7.2 0.0 copy-start
  7.2 0.0 all-gather.3.cloned.1.call-start
  7.2 1.7 copy.27
  8.9 0.0 all-gather.3.cloned.1.call-update
  8.9 0.0 all-gather.5.cloned.1.call-start
  9.0 1.6 copy.32
  10.5 0.0 all-gather.5.cloned.1.call-update
  10.6 0.0 all-reduce.3.cloned.1.call-start
  10.6 0.8 reshape.105
  11.4 1.3 reduce_sum.19
  12.7 0.3 reduce-window.9
  13.0 0.1 slice.7
  13.1 0.7 broadcast_compare_fusion
  13.8 0.1 eq.57
  13.9 0.6 compare_convert_fusion
  14.5 0.1 slice_reduce_fusion
  14.7 0.1 add_bitcast_fusion
  14.7 0.1 select_reduce_fusion
  14.9 42.3 %all-gather.3.cloned.1.call-done = bf16[128,4096]{0,1:T(8,128)(2,1)} async-done(((bf16[128,256]{0,1:T(8,128)(2,1)}), bf16[128,4096]{0,1:T(8,128)(2,1)}) %all-gather.3.cloned.1.call-update) | async-done | bytes 1048592 | tf_op jit(solution)/shard_map/all_gather | solution.py:101
  57.3 1.6 copy.28
  58.9 41.2 %all-gather.5.cloned.1.call-done = bf16[128,4096]{0,1:T(8,128)(2,1)} async-done(((bf16[128,256]{0,1:T(8,128)(2,1)}), bf16[128,4096]{0,1:T(8,128)(2,1)}) %all-gather.5.cloned.1.call-update) | async-done | bytes 1048592 | tf_op jit(solution)/shard_map/all_gather | solution.py:102
  100.1 2.3 copy.33
  102.3 0.7 gather_fusion
  103.1 2.4 gather_fusion.2
  105.5 0.5 convolution_bitcast_fusion.3
  106.0 2.3 multiply_convert_fusion.2
  108.3 0.9 convolution_bitcast_fusion.1
  109.2 2.4 fusion.23
  111.7 1.7 gather_fusion.3
  113.4 1.6 gather_fusion.1
  115.0 3.3 multiply_convert_fusion.1
  118.4 1.7 multiply_convert_fusion
  120.0 0.0 all-reduce.3.cloned.1.call-update
  120.0 0.2 reduce-scatter.5.cloned.1.call-start
  120.3 2.1 convolution_bitcast_fusion
  122.4 3.0 fusion.11
  125.4 1.4 copy.67
  126.8 0.0 reduce-scatter.5.cloned.1.call-update
  126.8 0.0 reduce-scatter.3.cloned.1.call-start
  126.9 0.5 convolution_bitcast_fusion.2
  127.4 3.0 fusion.8
  130.4 1.4 copy.68
  131.8 0.0 reduce-scatter.3.cloned.1.call-update
  131.8 149.9 %all-reduce.3.cloned.1.call-done = (bf16[32,128,128]{2,1,0:T(8,128)(2,1)}, bf16[32,128,128]{2,1,0:T(8,128)(2,1)}) async-done(((bf16[32,128,128]{2,1,0:T(8,128)(2,1)}, bf16[32,128,128]{2,1,0:T(8,128)(2,1)}), (bf16[32,128,128]{2,1,0:T(8,128)(2,1)}, bf16[32,128,128]{2,1,0:T(8,128)(2,1)})) %all-reduce.3.cloned.1.call-update) | async-done | bytes 2097168 | tf_op jit(solution)/shard_map/psum | solution.py:89
  281.7 63.5 %reduce-scatter.5.cloned.1.call-done = bf16[128,256]{1,0:T(8,128)(2,1)} async-done(((bf16[128,4096]{1,0:T(8,128)(2,1)}), bf16[128,256]{1,0:T(8,128)(2,1)}) %reduce-scatter.5.cloned.1.call-update) | async-done | bytes 65552 | tf_op jit(solution)/shard_map/reduce_scatter | solution.py:140
  345.3 61.8 %reduce-scatter.3.cloned.1.call-done = bf16[128,256]{1,0:T(8,128)(2,1)} async-done(((bf16[128,4096]{1,0:T(8,128)(2,1)}), bf16[128,256]{1,0:T(8,128)(2,1)}) %reduce-scatter.3.cloned.1.call-update) | async-done | bytes 65552 | tf_op jit(solution)/shard_map/reduce_scatter | solution.py:134
  407.1 2.3 copy.71
  409.4 1.0 copy.72
  (21 shorter events, 0.2 us)
Async XLA Ops:
  7.2 98.3 %copy-start = (bf16[32,128,128]{2,1,0:T(8,128)(2,1)S(1)}, bf16[32,128,128]{2,1,0:T(8,128)(2,1)}, u32[]{:S(2)}) copy-start(bf16[32,128,128]{2,1,0:T(8,128)(2,1)} %param.12) | copy-start | bytes 3145732
  7.2 50.1 %all-gather.3.cloned.1.call-start = ((), (), s32[]{:S(2)}) async-start(), calls=%async_computation.2 | async-start | bytes 1114112 | tf_op jit(solution)/shard_map/all_gather | solution.py:101
  8.9 91.2 %all-gather.5.cloned.1.call-start = ((), (), s32[]{:S(2)}) async-start(), calls=%async_computation.4 | async-start | bytes 1114112 | tf_op jit(solution)/shard_map/all_gather | solution.py:102
  10.6 271.2 %all-reduce.3.cloned.1.call-start = ((), (), s32[]{:S(2)}) async-start(), calls=%async_computation.6 | async-start | bytes 4194304 | tf_op jit(solution)/shard_map/psum | solution.py:89
  103.1 2.4 copy-start.5
  105.5 2.8 copy-start.3
  106.0 2.3 copy-start.1
  115.0 3.3 copy-start.2
  115.0 3.3 copy-start.4
  120.0 225.2 %reduce-scatter.5.cloned.1.call-start = ((), (), s32[]{:S(2)}) async-start(), calls=%async_computation.5 | async-start | bytes 1114112 | tf_op jit(solution)/shard_map/reduce_scatter | solution.py:140
  126.8 280.3 %reduce-scatter.3.cloned.1.call-start = ((), (), s32[]{:S(2)}) async-start(), calls=%async_computation.3 | async-start | bytes 1114112 | tf_op jit(solution)/shard_map/reduce_scatter | solution.py:134
  281.7 127.7 %copy-start.6 = (bf16[32,128,128]{2,1,0:T(8,128)(2,1)S(1)}, bf16[32,128,128]{2,1,0:T(8,128)(2,1)}, u32[]{:S(2)}) copy-start(bf16[32,128,128]{2,1,0:T(8,128)(2,1)} %get-tuple-element.19) | copy-start | bytes 3145732
Sparse Core Ops, SparseCore 0:
  10.7 46.5 all-gather.2
  60.0 40.0 all-gather.4
  120.2 161.5 all-reduce.2
  285.2 60.0 reduce-scatter.4
  348.5 58.5 reduce-scatter.2
where the time goes:
time: 417 us
  waiting for transfers between devices  359 us (86%)
  local copies, waits for them, and re-layouts  20.8 us (5%)
  matrix products  19.7 us (5%)
  between operations  14 us (3%)
    psum x1, waiting for transfers between devices, reduce_tiles(): lax.psum(grad_up.astype(jnp.bfloat16), 'dp').astype(jnp.float32)  150 us
    reduce_scatter x1, waiting for transfers between devices, body(): lax.psum_scatter(grad_cols.reshape(tok_rows, col_blocks * block_size).ast...  63.5 us
    reduce_scatter x1, waiting for transfers between devices, body(): lax.psum_scatter(out_cols.reshape(tok_rows, col_blocks * block_size).asty...  61.8 us
    all_gather x1, waiting for transfers between devices, body(): lax.all_gather(tokens, 'mp', axis=1, tiled=True)  42.3 us
    all_gather x1, waiting for transfers between devices, body(): lax.all_gather(cotangent, 'mp', axis=1, tiled=True)  41.2 us
    unnamed x20, local copies, waits for them, and re-layouts  9.36 us
  transfers between devices with their start and end apart: 5, of which 5 were waited for; matrix products, arithmetic and copies ran while one was open for 5% of the time, Pallas kernels for 0%

commit v1 on v0

v1 whole, which is shorter than its diff:
```python
import jax
import jax.numpy as jnp
from jax import lax
from jax.experimental import pallas as pl
from jax.experimental.pallas import tpu as pltpu
from jax.sharding import PartitionSpec as P

BF = jnp.bfloat16
F32 = jnp.float32
VM = pltpu.CompilerParams(vmem_limit_bytes=48 * 1024 * 1024)
NX, NY, NZ = 4, 8, 8
X_GROUPS = [[NX * y + x for x in range(NX)] for y in range(NY)]
Y_GROUPS = [[NX * y + x for y in range(NY)] for x in range(NX)]
Z_GROUPS = [[2 * z + c for z in range(NZ)] for c in range(2)]
CORE_SWAP = [(i, i ^ 1) for i in range(2 * NZ)]
SLOTS, ROWS, COLS, BLK = 32, 8, 32, 128


def gelu_pair(hidden, dact):
    inner = 0.7978845608 * (hidden + 0.044715 * hidden * hidden * hidden)
    tangent = jnp.tanh(inner)
    inner_slope = 0.7978845608 * (1.0 + 3.0 * 0.044715 * hidden * hidden)
    value = 0.5 * hidden * (1.0 + tangent)
    slope = 0.5 * (1.0 + tangent) + 0.5 * hidden * (1.0 - tangent * tangent) * inner_slope
    return value.astype(BF), (dact * slope).astype(BF)


def nn(a, b):
    return lax.dot_general(a, b, (((1,), (0,)), ((), ())), preferred_element_type=F32)


def nt(a, b):
    return lax.dot_general(a, b, (((1,), (1,)), ((), ())), preferred_element_type=F32)


def prep_kernel(tok_ref, cot_ref, out_ref):
    for j in range(2):
        tok_t = tok_ref[:, j * BLK : (j + 1) * BLK].T
        cot = cot_ref[:, j * BLK : (j + 1) * BLK]
        for z in range(NZ):
            out_ref[z, j] = tok_t
            out_ref[z, 2 + j] = cot


def table_kernel(mask_ref, out_ref, cells):
    count = jnp.int32(0)
    for cell in range(ROWS * COLS):
        cells[count] = jnp.int32(cell)
        count = count + mask_ref[cell // COLS, cell % COLS]
    last_row = jnp.int32(-1)
    for s in range(SLOTS):
        used = jnp.int32(s) < count
        cell = jnp.where(used, cells[s], ROWS * COLS - 1)
        row = cell >> 5
        out_ref[s] = cell & 31
        out_ref[SLOTS + s] = row
        out_ref[2 * SLOTS + s] = jnp.where(row == last_row, 0, 1)
        out_ref[3 * SLOTS + s] = jnp.where(used, 1, 0)
        last_row = row


def weights_kernel(up_ref, down_ref, up_t_ref, down_t_ref):
    for s in range(SLOTS):
        up_t_ref[s] = up_ref[s].T
        down_t_ref[s] = down_ref[s].T


def first_kernel(
    table_ref, core_ref, own_ref, other_ref, up_t_ref, down_ref, grads_ref, act_ref, pre_ref, panels, hid, dac
):
    core = core_ref[0]
    panels[0] = own_ref[...]
    panels[1] = other_ref[...]

    def place(s):
        col = table_ref[s]
        return ((col >> 1) & 1) ^ core, col >> 2, col & 1

    hid_sum = jnp.zeros((BLK, BLK), F32)
    dac_sum = jnp.zeros((BLK, BLK), F32)
    for s in range(SLOTS):
        side, z, j = place(s)
        row = table_ref[SLOTS + s]
        fresh = table_ref[2 * SLOTS + s] == 1
        used = table_ref[3 * SLOTS + s] == 1
        hid_part = nn(up_t_ref[s], panels[side, z, j])
        dac_part = nt(down_ref[s], panels[side, z, 2 + j])
        hid_sum = jnp.where(fresh, 0.0, hid_sum) + jnp.where(used, hid_part, 0.0)
        dac_sum = jnp.where(fresh, 0.0, dac_sum) + jnp.where(used, dac_part, 0.0)
        hid[row] = hid_sum
        dac[row] = dac_sum
    for r in range(ROWS):
        act, pre = gelu_pair(hid[r], dac[r])
        act_ref[r] = act
        pre_ref[r] = pre
    for s in range(SLOTS):
        side, z, j = place(s)
        row = table_ref[SLOTS + s]
        used = table_ref[3 * SLOTS + s] == 1
        up_part = nt(panels[side, z, j], pre_ref[row])
        down_part = nn(act_ref[row], panels[side, z, 2 + j])
        grads_ref[s // 8, 0, s % 8] = jnp.where(used, up_part, 0.0).astype(BF)
        grads_ref[s // 8, 1, s % 8] = jnp.where(used, down_part, 0.0).astype(BF)


def second_kernel(table_ref, core_ref, act_ref, pre_ref, down_t_ref, up_ref, own_ref, send_ref, out_sum, grad_sum):
    core = core_ref[0]
    out_sum[...] = jnp.zeros_like(out_sum)
    grad_sum[...] = jnp.zeros_like(grad_sum)
    for s in range(SLOTS):
        col = table_ref[s]
        row = table_ref[SLOTS + s]
        used = table_ref[3 * SLOTS + s] == 1
        out_part = nn(down_t_ref[s], act_ref[row])
        grad_part = nn(up_ref[s], pre_ref[row])
        out_sum[col] += jnp.where(used, out_part, 0.0)
        grad_sum[col] += jnp.where(used, grad_part, 0.0)
    for z in range(NZ):
        for j in range(2):
            own = 4 * z + 2 * core + j
            other = 4 * z + 2 * (1 - core) + j
            own_ref[z, j] = out_sum[own].astype(BF)
            own_ref[z, 2 + j] = grad_sum[own].astype(BF)
            send_ref[z, j] = out_sum[other].astype(BF)
            send_ref[z, 2 + j] = grad_sum[other].astype(BF)


def add_kernel(a_ref, b_ref, out_ref):
    out_ref[...] = (a_ref[...].astype(F32) + b_ref[...].astype(F32)).astype(BF)


def x_sum_kernel(in_ref, out_ref):
    for y in range(NY):
        for k in range(2):
            total = in_ref[0, k, y].astype(F32)
            for x in range(1, NX):
                total = total + in_ref[x, k, y].astype(F32)
            out_ref[y, k] = total.astype(BF)


def y_sum_kernel(in_ref, out_ref):
    for k in range(2):
        total = in_ref[0, k].astype(F32)
        for y in range(1, NY):
            total = total + in_ref[y, k].astype(F32)
        total = total.astype(BF)
        for y in range(NY):
            out_ref[y, k] = total


def spread_kernel(in_ref, out_ref):
    for y in range(NY):
        for k in range(2):
            tile = in_ref[y, k]
            for x in range(NX):
                out_ref[x, k, y] = tile


def split_kernel(in_ref, up_ref, down_ref):
    for x in range(NX):
        up_ref[x * 8 : (x + 1) * 8] = in_ref[x, 0]
        down_ref[x * 8 : (x + 1) * 8] = in_ref[x, 1]


def final_kernel(in_ref, out_ref, grad_ref):
    for j in range(2):
        out_ref[:, j * BLK : (j + 1) * BLK] = in_ref[j].T
        grad_ref[:, j * BLK : (j + 1) * BLK] = in_ref[2 + j].T


def whole(count):
    return [pl.BlockSpec(memory_space=pltpu.VMEM)] * count


def smem(count):
    return [pl.BlockSpec(memory_space=pltpu.SMEM)] * count


def shape(*dims, dtype=BF):
    return jax.ShapeDtypeStruct(dims, dtype)


def call(kernel, outs, operands, n_smem=0, scratch=(), flops=0, moved=0, out_smem=False):
    many = isinstance(outs, (list, tuple))
    n_out = len(outs) if many else 1
    out_specs = smem(n_out) if out_smem else whole(n_out)
    return pl.pallas_call(
        kernel,
        out_shape=outs,
        in_specs=smem(n_smem) + whole(len(operands) - n_smem),
        out_specs=out_specs if many else out_specs[0],
        scratch_shapes=list(scratch),
        compiler_params=VM,
        cost_estimate=pl.CostEstimate(flops=flops, bytes_accessed=moved, transcendentals=0),
    )(*operands)


def exchange(x, axis, groups):
    return lax.all_to_all(x, axis, 0, 0, tiled=True, axis_index_groups=groups)


def body(tokens, cotangent, block_mask, up_tiles, down_tiles):
    mib = 1 << 20
    core = (lax.axis_index("mp") % 2).astype(jnp.int32).reshape(1)
    sent = call(prep_kernel, shape(NZ, 4, BLK, BLK), (tokens, cotangent), moved=mib)
    own_panels = exchange(sent, "mp", Z_GROUPS)
    table = call(
        table_kernel,
        shape(4 * SLOTS, dtype=jnp.int32),
        (block_mask,),
        n_smem=1,
        scratch=[pltpu.SMEM((ROWS * COLS + 8,), jnp.int32)],
        out_smem=True,
        flops=mib,
        moved=1024,
    )
    up_t, down_t = call(
        weights_kernel,
        [shape(SLOTS, BLK, BLK), shape(SLOTS, BLK, BLK)],
        (up_tiles, down_tiles),
        moved=4 * mib,
    )
    other_panels = lax.ppermute(own_panels, "mp", CORE_SWAP)
    product = 2 * SLOTS * BLK * BLK * BLK
    grads, act, pre = call(
        first_kernel,
        [shape(NX, 2, 8, BLK, BLK), shape(ROWS, BLK, BLK), shape(ROWS, BLK, BLK)],
        (table, core, own_panels, other_panels, up_t, down_tiles),
        n_smem=2,
        scratch=[
            pltpu.VMEM((2, NZ, 4, BLK, BLK), BF),
            pltpu.VMEM((ROWS, BLK, BLK), F32),
            pltpu.VMEM((ROWS, BLK, BLK), F32),
        ],
        flops=4 * product,
        moved=6 * mib,
    )
    own_part, other_part = call(
        second_kernel,
        [shape(NZ, 4, BLK, BLK), shape(NZ, 4, BLK, BLK)],
        (table, core, act, pre, down_t, up_tiles),
        n_smem=2,
        scratch=[pltpu.VMEM((COLS, BLK, BLK), F32), pltpu.VMEM((COLS, BLK, BLK), F32)],
        flops=2 * product,
        moved=5 * mib,
    )
    from_other = lax.ppermute(other_part, "mp", CORE_SWAP)
    chip_part = call(add_kernel, shape(NZ, 4, BLK, BLK), (own_part, from_other), moved=3 * mib)
    by_x = exchange(grads, "dp", X_GROUPS)
    x_done = call(x_sum_kernel, shape(NY, 2, BLK, BLK), (by_x,), moved=3 * mib)
    x_done, chip_part = lax.optimization_barrier((x_done, chip_part))
    columns = lax.psum_scatter(
        chip_part.reshape(NZ * 4, BLK, BLK), "mp", scatter_dimension=0, axis_index_groups=Z_GROUPS, tiled=True
    )
    output, grad_tokens = call(
        final_kernel, [shape(BLK, 2 * BLK), shape(BLK, 2 * BLK)], (columns,), moved=mib // 4
    )
    by_y = exchange(x_done, "dp", Y_GROUPS)
    y_done = call(y_sum_kernel, shape(NY, 2, BLK, BLK), (by_y,), moved=mib)
    all_y = exchange(y_done, "dp", Y_GROUPS)
    spread = call(spread_kernel, shape(NX, 2, NY, BLK, BLK), (all_y,), moved=3 * mib)
    all_x = exchange(spread, "dp", X_GROUPS)
    grad_up, grad_down = call(
        split_kernel, [shape(SLOTS, BLK, BLK), shape(SLOTS, BLK, BLK)], (all_x,), moved=4 * mib
    )
    return output, grad_tokens, grad_up, grad_down


def solution(mesh):
    in_specs = (
        P("dp", "mp"),
        P("dp", "mp"),
        P("mp", None),
        P("mp", None, None),
        P("mp", None, None),
    )
    out_specs = (P("dp", "mp"), P("dp", "mp"), P("mp", None, None), P("mp", None, None))
    return jax.shard_map(body, mesh=mesh, in_specs=in_specs, out_specs=out_specs, check_vma=False)
```

time: 417 us -> 171 us (0.41)
  waiting for transfers between devices: 359 us -> 52.9 us
  blocking collectives: 0 us -> 62.8 us
  matrix products: 19.7 us -> 0 us
  starting transfers between devices: 0.39 us -> 17.8 us
  Pallas kernels: 0 us -> 15.5 us
  local copies, waits for them, and re-layouts: 20.8 us -> 6.58 us
    psum x1 -> x0, waiting for transfers between devices: 150 us -> none  [reduce_tiles(): lax.psum(grad_up.astype(jnp.bfloat16), 'dp').astype(jnp.float32)]
    reduce_scatter x2 -> x1, waiting for transfers between devices: 125 us -> 19.7 us  [body(): lax.psum_scatter(chip_part.reshape(NZ * 4, BLK, BLK), 'mp', scatter_dimen...]
    all_gather x2 -> x0, waiting for transfers between devices: 83.5 us -> none  [the longest x1 42.3 us: body(): lax.all_gather(tokens, 'mp', axis=1, tiled=True)]
    all_to_all x0 -> x2, blocking collectives: none -> 62.8 us  [exchange(): return lax.all_to_all(x, axis, 0, 0, tiled=True, axis_index_groups=groups)]
    all_to_all x0 -> x3, waiting for transfers between devices: none -> 29.9 us  [exchange(): return lax.all_to_all(x, axis, 0, 0, tiled=True, axis_index_groups=groups)]
    dot_general x10 -> x0, matrix products: 19.7 us -> none  [the longest x1 3.33 us: second_section(): jnp.einsum('tsi,tsh->sih', in_picked, pre_picked, preferred_element_type=...]
    pallas_call x0 -> x11, Pallas kernels: none -> 15.5 us  [call(): pl.pallas_call(kernel, out_shape=outs, in_specs=smem(n_smem) + whole(len(...]
    all_to_all x0 -> x3, starting transfers between devices: none -> 13.9 us  [exchange(): return lax.all_to_all(x, axis, 0, 0, tiled=True, axis_index_groups=groups)]
  transfers between devices with their start and end apart: 5 -> 6, of which waited for: 5 -> 4; matrix products, arithmetic and copies ran while one was open for 5% -> 0% of each run, Pallas kernels for 0% -> 4%
where the time goes in v1:
time: 171 us; the launch traced here: 170 us
  blocking collectives  62.8 us (37%)
  waiting for transfers between devices  52.9 us (31%)
  starting transfers between devices  17.8 us (10%)
  Pallas kernels  15.5 us (9%)
  between operations  14.2 us (8%)
  local copies, waits for them, and re-layouts  6.58 us (4%)
    all_to_all x2, blocking collectives, exchange(): return lax.all_to_all(x, axis, 0, 0, tiled=True, axis_index_groups=groups)  62.8 us
    all_to_all x3, waiting for transfers between devices, exchange(): return lax.all_to_all(x, axis, 0, 0, tiled=True, axis_index_groups=groups)  29.9 us
    reduce_scatter x1, waiting for transfers between devices, body(): lax.psum_scatter(chip_part.reshape(NZ * 4, BLK, BLK), 'mp', scatter_dimen...  19.7 us
    pallas_call x11, Pallas kernels, call(): pl.pallas_call(kernel, out_shape=outs, in_specs=smem(n_smem) + whole(len(...  15.5 us
    all_to_all x3, starting transfers between devices, exchange(): return lax.all_to_all(x, axis, 0, 0, tiled=True, axis_index_groups=groups)  13.9 us
    unnamed x20, local copies, waits for them, and re-layouts  6.58 us
  transfers between devices with their start and end apart: 6, of which 4 were waited for; matrix products, arithmetic and copies ran while one was open for 0% of the time, Pallas kernels for 4%

profile of v1, /device:TPU:6, one launch (start us, length us, event | category | flops | bytes accessed | tf_op | source)
XLA Modules:
  0.0 169.8 jit_solution(9900888770069602085)
XLA Ops:
  7.2 0.0 copy-start
  7.2 0.0 copy-start.1
  7.2 0.0 copy-start.7
  7.2 1.0 copy-done.7
  8.2 0.0 copy-start.8
  8.2 0.8 copy-done.8
  9.0 0.1 shard_map.85
  9.2 0.0 copy-start.9
  9.2 38.8 %all_to_all.25.own_ref = bf16[8,4,128,128]{3,2,1,0:T(8,128)(2,1)S(1)} all-to-all(bf16[8,4,128,128]{3,2,1,0:T(8,128)(2,1)S(1)} %shard_map.85), channel_id=1, replica_groups={{0,2,4,6,8,10,12,14},{1,3,5,7,9,11,13,15},{16,18,20,22,24,26,28,30},{17..., dimensions={0} | all-to-all | bytes 2097152 | tf_op jit(solution)/shard_map/all_to_all | solution.py:199
  48.0 1.9 %collective-permute-start = (bf16[8,4,128,128]{3,2,1,0:T(8,128)(2,1)S(1)}, bf16[8,4,128,128]{3,2,1,0:T(8,128)(2,1)}, u32[]{:S(2)}, u32[]{:S(2)}) collective-permute-start(bf16[8,4,128,128]{3,2,1,0:T(8,128)(2,1)S(1)} %all_to_all.25.own_ref), channel_id=1, source_target_pairs={{0,1},{1,0},{2,3},{3,2},{4,5},{5,4},{6,7},{7,6},{8,9},{9,8},{10,11... | collective-permute-start | bytes 3145736 | tf_op jit(solution)/shard_map/ppermute | solution.py:223
  49.9 0.0 copy-done
  49.9 0.0 copy-done.1
  50.0 0.6 shard_map.86
  50.6 0.0 copy-start.2
  50.6 1.0 copy-done.2
  51.5 0.0 copy-done.9
  51.5 1.6 shard_map.84.table_ref
  53.2 0.0 collective-permute-done.other_ref
  53.2 5.4 %shard_map.87 = (bf16[4,2,8,128,128]{4,3,2,1,0:T(8,128)(2,1)}, bf16[8,128,128]{2,1,0:T(8,128)(2,1)S(1)}, bf16[8,128,128]{2,1,0:T(8,128)(2,1)S(1)}) custom-call(s32[128]{0:T(128)S(1)} %shard_map.84.table_ref, s32[1]{0:T(128)} %bitcast.core_ref, bf16[8,4,128,128]{3,2,1,0:T(8,128)(2,1)S(1)} %all_to_all.25.own_ref, ...), custom_call_target="tpu_custom_call" | custom-call | flops 536870912 | bytes 6291456 | tf_op jit(solution)/shard_map/pallas_call | solution.py:187
  58.6 0.0 copy-start.4
  58.6 0.7 copy-done.4
  59.3 4.8 %all-to-all-start.1 = ((bf16[4,2,8,128,128]{4,3,2,1,0:T(8,128)(2,1)}), bf16[4,2,8,128,128]{4,3,2,1,0:T(8,128)(2,1)S(1)}, u32[]{:S(2)}, u32[]{:S(2)}) async-start(bf16[4,2,8,128,128]{4,3,2,1,0:T(8,128)(2,1)} %get-tuple-element.18), calls=%async_computation.1 | async-start | bytes 4194304 | tf_op jit(solution)/shard_map/all_to_all | solution.py:199
  64.0 0.0 copy-start.3
  64.0 1.2 copy-done.3
  65.3 0.0 copy-start.5
  65.3 0.9 copy-done.5
  66.2 1.7 %shard_map.89 = (bf16[8,4,128,128]{3,2,1,0:T(8,128)(2,1)S(1)}, bf16[8,4,128,128]{3,2,1,0:T(8,128)(2,1)S(1)}) custom-call(s32[128]{0:T(128)S(1)} %shard_map.84.table_ref, s32[1]{0:T(128)} %bitcast.core_ref, bf16[8,128,128]{2,1,0:T(8,128)(2,1)S(1)} %get-tuple-element.19.act_ref, bf16[8,128,128]{2,1,0:T(8,128)(2,1)S(1)} %copy-done.5, ...), custom_call_target="tpu_custom_call" | custom-call | flops 268435456 | bytes 5242880 | tf_op jit(solution)/shard_map/pallas_call | solution.py:187
  67.9 1.9 %collective-permute-start.1 = (bf16[8,4,128,128]{3,2,1,0:T(8,128)(2,1)S(1)}, bf16[8,4,128,128]{3,2,1,0:T(8,128)(2,1)S(1)}, u32[]{:S(2)}, u32[]{:S(2)}) collective-permute-start(bf16[8,4,128,128]{3,2,1,0:T(8,128)(2,1)S(1)} %get-tuple-element.23), channel_id=1, source_target_pairs={{0,1},{1,0},{2,3},{3,2},{4,5},{5,4},{6,7},{7,6},{8,9},{9,8},{10,11... | collective-permute-start | bytes 3145736 | tf_op jit(solution)/shard_map/ppermute | solution.py:247
  69.8 2.6 %collective-permute-done.1.b_ref = bf16[8,4,128,128]{3,2,1,0:T(8,128)(2,1)S(1)} collective-permute-done((bf16[8,4,128,128]{3,2,1,0:T(8,128)(2,1)S(1)}, bf16[8,4,128,128]{3,2,1,0:T(8,128)(2,1)S(1)}, u32[]{:S(2)}, u32[]{:S(2)}) %collective-permute-start.1) | collective-permute-done | bytes 1048608 | tf_op jit(solution)/shard_map/ppermute | solution.py:247
  72.5 1.2 shard_map.90
  73.7 15.3 %all-to-all-done.1.in_ref = bf16[4,2,8,128,128]{4,3,2,1,0:T(8,128)(2,1)S(1)} async-done(((bf16[4,2,8,128,128]{4,3,2,1,0:T(8,128)(2,1)}), bf16[4,2,8,128,128]{4,3,2,1,0:T(8,128)(2,1)S(1)}, u32[]{:S(2)}, u32[]{:S(2)}) %all-to-all-start.1) | async-done | bytes 2097184 | tf_op jit(solution)/shard_map/all_to_all | solution.py:199
  89.0 0.3 shard_map.88
  89.2 24.0 %all_to_all.26.in_ref = bf16[8,2,128,128]{3,2,1,0:T(8,128)(2,1)S(1)} all-to-all(bf16[8,2,128,128]{3,2,1,0:T(8,128)(2,1)S(1)} %shard_map.88), channel_id=1, replica_groups={{0,64,128,192,256,320,384,448},{16,80,144,208,272,336,400,464},{32,96,1..., dimensions={0} | all-to-all | bytes 1048576 | tf_op jit(solution)/shard_map/all_to_all | solution.py:199
  113.2 0.9 shard_map.92
  114.0 3.5 %all-to-all-start.3 = ((bf16[8,2,128,128]{3,2,1,0:T(8,128)(2,1)}), bf16[8,2,128,128]{3,2,1,0:T(8,128)(2,1)S(1)}, u32[]{:S(2)}, u32[]{:S(2)}) async-start(bf16[8,2,128,128]{3,2,1,0:T(8,128)(2,1)} %shard_map.92), calls=%async_computation.4 | async-start | bytes 1048576 | tf_op jit(solution)/shard_map/all_to_all | solution.py:199
  117.5 0.0 reduce-scatter.2.cloned.1.call-start
  117.6 0.7 reduce-scatter.2.cloned.1.call-update
  118.3 14.6 %all-to-all-done.3.in_ref = bf16[8,2,128,128]{3,2,1,0:T(8,128)(2,1)S(1)} async-done(((bf16[8,2,128,128]{3,2,1,0:T(8,128)(2,1)}), bf16[8,2,128,128]{3,2,1,0:T(8,128)(2,1)S(1)}, u32[]{:S(2)}, u32[]{:S(2)}) %all-to-all-start.3) | async-done | bytes 524320 | tf_op jit(solution)/shard_map/all_to_all | solution.py:199
  132.9 1.6 shard_map.93
  134.5 5.7 %all-to-all-start.4 = ((bf16[4,2,8,128,128]{4,3,2,1,0:T(8,128)(2,1)}), bf16[4,2,8,128,128]{4,3,2,1,0:T(8,128)(2,1)S(1)}, u32[]{:S(2)}, u32[]{:S(2)}) async-start(bf16[4,2,8,128,128]{4,3,2,1,0:T(8,128)(2,1)} %shard_map.93), calls=%async_computation.5 | async-start | bytes 4194304 | tf_op jit(solution)/shard_map/all_to_all | solution.py:199
  140.1 19.7 %reduce-scatter.2.cloned.1.call-done.in_ref = bf16[4,128,128]{2,1,0:T(8,128)(2,1)} async-done(((bf16[32,128,128]{2,1,0:T(8,128)(2,1)}), bf16[4,128,128]{2,1,0:T(8,128)(2,1)}) %reduce-scatter.2.cloned.1.call-update) | async-done | bytes 131088 | tf_op jit(solution)/shard_map/reduce_scatter | solution.py:252
  159.9 0.0 copy-start.6
  159.9 0.9 copy-done.6
  160.8 0.7 shard_map.91
  161.5 0.0 all-to-all-done.4.in_ref
  161.5 1.5 shard_map.94
Async XLA Ops:
  7.2 42.8 %copy-start = (bf16[32,128,128]{2,1,0:T(8,128)(2,1)S(1)}, bf16[32,128,128]{2,1,0:T(8,128)(2,1)}, u32[]{:S(2)}) copy-start(bf16[32,128,128]{2,1,0:T(8,128)(2,1)} %down_ref.3) | copy-start | bytes 3145732
  7.2 42.8 %copy-start.1 = (bf16[32,128,128]{2,1,0:T(8,128)(2,1)S(1)}, bf16[32,128,128]{2,1,0:T(8,128)(2,1)}, u32[]{:S(2)}) copy-start(bf16[32,128,128]{2,1,0:T(8,128)(2,1)} %up_ref.3) | copy-start | bytes 3145732
  7.2 1.0 copy-start.7
  8.2 0.8 copy-start.8
  9.2 42.4 %copy-start.9 = (s32[8,32]{1,0:T(8,128)S(1)}, s32[8,32]{1,0:T(8,128)}, u32[]{:S(2)}) copy-start(s32[8,32]{1,0:T(8,128)} %mask_ref.1) | copy-start | bytes 3076
  48.0 5.2 %collective-permute-start = (bf16[8,4,128,128]{3,2,1,0:T(8,128)(2,1)S(1)}, bf16[8,4,128,128]{3,2,1,0:T(8,128)(2,1)}, u32[]{:S(2)}, u32[]{:S(2)}) collective-permute-start(bf16[8,4,128,128]{3,2,1,0:T(8,128)(2,1)S(1)} %all_to_all.25.own_ref), channel_id=1, source_target_pairs={{0,1},{1,0},{2,3},{3,2},{4,5},{5,4},{6,7},{7,6},{8,9},{9,8},{10,11... | collective-permute-start | bytes 3145736 | tf_op jit(solution)/shard_map/ppermute | solution.py:223
  50.6 1.0 copy-start.2
  58.6 0.7 copy-start.4
  59.3 29.7 %all-to-all-start.1 = ((bf16[4,2,8,128,128]{4,3,2,1,0:T(8,128)(2,1)}), bf16[4,2,8,128,128]{4,3,2,1,0:T(8,128)(2,1)S(1)}, u32[]{:S(2)}, u32[]{:S(2)}) async-start(bf16[4,2,8,128,128]{4,3,2,1,0:T(8,128)(2,1)} %get-tuple-element.18), calls=%async_computation.1 | async-start | bytes 4194304 | tf_op jit(solution)/shard_map/all_to_all | solution.py:199
  64.0 1.2 copy-start.3
  65.3 0.9 copy-start.5
  67.9 4.6 %collective-permute-start.1 = (bf16[8,4,128,128]{3,2,1,0:T(8,128)(2,1)S(1)}, bf16[8,4,128,128]{3,2,1,0:T(8,128)(2,1)S(1)}, u32[]{:S(2)}, u32[]{:S(2)}) collective-permute-start(bf16[8,4,128,128]{3,2,1,0:T(8,128)(2,1)S(1)} %get-tuple-element.23), channel_id=1, source_target_pairs={{0,1},{1,0},{2,3},{3,2},{4,5},{5,4},{6,7},{7,6},{8,9},{9,8},{10,11... | collective-permute-start | bytes 3145736 | tf_op jit(solution)/shard_map/ppermute | solution.py:247
  114.0 18.9 %all-to-all-start.3 = ((bf16[8,2,128,128]{3,2,1,0:T(8,128)(2,1)}), bf16[8,2,128,128]{3,2,1,0:T(8,128)(2,1)S(1)}, u32[]{:S(2)}, u32[]{:S(2)}) async-start(bf16[8,2,128,128]{3,2,1,0:T(8,128)(2,1)} %shard_map.92), calls=%async_computation.4 | async-start | bytes 1048576 | tf_op jit(solution)/shard_map/all_to_all | solution.py:199
  117.5 42.3 %reduce-scatter.2.cloned.1.call-start = ((), (), s32[]{:S(2)}) async-start(), calls=%async_computation.6 | async-start | bytes 1179648 | tf_op jit(solution)/shard_map/reduce_scatter | solution.py:252
  134.5 27.0 %all-to-all-start.4 = ((bf16[4,2,8,128,128]{4,3,2,1,0:T(8,128)(2,1)}), bf16[4,2,8,128,128]{4,3,2,1,0:T(8,128)(2,1)S(1)}, u32[]{:S(2)}, u32[]{:S(2)}) async-start(bf16[4,2,8,128,128]{4,3,2,1,0:T(8,128)(2,1)} %shard_map.93), calls=%async_computation.5 | async-start | bytes 4194304 | tf_op jit(solution)/shard_map/all_to_all | solution.py:199
  159.9 0.9 copy-start.6
Sparse Core Ops, SparseCore 0:
  121.8 38.0 reduce-scatter.1

commit v2 on v1

--- a/solution.py
+++ b/solution.py
@@ -13,6 +13,7 @@
 Y_GROUPS = [[NX * y + x for y in range(NY)] for x in range(NX)]
 Z_GROUPS = [[2 * z + c for z in range(NZ)] for c in range(2)]
 CORE_SWAP = [(i, i ^ 1) for i in range(2 * NZ)]
+PAIR_SWAP = [(i, i ^ 2) for i in range(2 * NZ)]
 SLOTS, ROWS, COLS, BLK = 32, 8, 32, 128
 
 
@@ -66,9 +67,9 @@
 
 
 def first_kernel(
-    table_ref, core_ref, own_ref, other_ref, up_t_ref, down_ref, grads_ref, act_ref, pre_ref, panels, hid, dac
+    table_ref, place_ref, own_ref, other_ref, up_t_ref, down_ref, grads_ref, act_ref, pre_ref, panels, hid, dac
 ):
-    core = core_ref[0]
+    core = place_ref[0]
     panels[0] = own_ref[...]
     panels[1] = other_ref[...]
 
@@ -103,8 +104,8 @@
         grads_ref[s // 8, 1, s % 8] = jnp.where(used, down_part, 0.0).astype(BF)
 
 
-def second_kernel(table_ref, core_ref, act_ref, pre_ref, down_t_ref, up_ref, own_ref, send_ref, out_sum, grad_sum):
-    core = core_ref[0]
+def second_kernel(table_ref, place_ref, act_ref, pre_ref, down_t_ref, up_ref, own_ref, send_ref, out_sum, grad_sum):
+    core = place_ref[0]
     out_sum[...] = jnp.zeros_like(out_sum)
     grad_sum[...] = jnp.zeros_like(grad_sum)
     for s in range(SLOTS):
@@ -125,8 +126,20 @@
             send_ref[z, 2 + j] = grad_sum[other].astype(BF)
 
 
-def add_kernel(a_ref, b_ref, out_ref):
-    out_ref[...] = (a_ref[...].astype(F32) + b_ref[...].astype(F32)).astype(BF)
+def chip_add_kernel(place_ref, a_ref, b_ref, keep_ref, send_ref):
+    odd = place_ref[1] & 1
+    for half in range(NZ // 2):
+        near = 2 * half + odd
+        far = 2 * half + 1 - odd
+        keep_ref[half] = (a_ref[near].astype(F32) + b_ref[near].astype(F32)).astype(BF)
+        send_ref[half] = (a_ref[far].astype(F32) + b_ref[far].astype(F32)).astype(BF)
+
+
+def pair_add_kernel(place_ref, a_ref, b_ref, *out_refs):
+    mine = place_ref[1] >> 1
+    for hop in range(NZ // 2):
+        there = (mine + hop) & (NZ // 2 - 1)
+        out_refs[hop][...] = (a_ref[there].astype(F32) + b_ref[there].astype(F32)).astype(BF)
 
 
 def x_sum_kernel(in_ref, out_ref):
@@ -162,10 +175,14 @@
         down_ref[x * 8 : (x + 1) * 8] = in_ref[x, 1]
 
 
-def final_kernel(in_ref, out_ref, grad_ref):
-    for j in range(2):
-        out_ref[:, j * BLK : (j + 1) * BLK] = in_ref[j].T
-        grad_ref[:, j * BLK : (j + 1) * BLK] = in_ref[2 + j].T
+def final_kernel(*refs):
+    in_refs, out_ref, grad_ref = refs[:-2], refs[-2], refs[-1]
+    for j in range(4):
+        total = in_refs[0][j].astype(F32)
+        for in_ref in in_refs[1:]:
+            total = total + in_ref[j].astype(F32)
+        goal = out_ref if j < 2 else grad_ref
+        goal[:, (j % 2) * BLK : (j % 2 + 1) * BLK] = total.T.astype(BF)
 
 
 def whole(count):
@@ -201,7 +218,8 @@
 
 def body(tokens, cotangent, block_mask, up_tiles, down_tiles):
     mib = 1 << 20
-    core = (lax.axis_index("mp") % 2).astype(jnp.int32).reshape(1)
+    position = lax.axis_index("mp")
+    place = jnp.stack([position & 1, position >> 1]).astype(jnp.int32)
     sent = call(prep_kernel, shape(NZ, 4, BLK, BLK), (tokens, cotangent), moved=mib)
     own_panels = exchange(sent, "mp", Z_GROUPS)
     table = call(
@@ -225,7 +243,7 @@
     grads, act, pre = call(
         first_kernel,
         [shape(NX, 2, 8, BLK, BLK), shape(ROWS, BLK, BLK), shape(ROWS, BLK, BLK)],
-        (table, core, own_panels, other_panels, up_t, down_tiles),
+        (table, place, own_panels, other_panels, up_t, down_tiles),
         n_smem=2,
         scratch=[
             pltpu.VMEM((2, NZ, 4, BLK, BLK), BF),
@@ -238,26 +256,42 @@
     own_part, other_part = call(
         second_kernel,
         [shape(NZ, 4, BLK, BLK), shape(NZ, 4, BLK, BLK)],
-        (table, core, act, pre, down_t, up_tiles),
+        (table, place, act, pre, down_t, up_tiles),
         n_smem=2,
         scratch=[pltpu.VMEM((COLS, BLK, BLK), F32), pltpu.VMEM((COLS, BLK, BLK), F32)],
         flops=2 * product,
         moved=5 * mib,
     )
     from_other = lax.ppermute(other_part, "mp", CORE_SWAP)
-    chip_part = call(add_kernel, shape(NZ, 4, BLK, BLK), (own_part, from_other), moved=3 * mib)
+    chip_keep, chip_send = call(
+        chip_add_kernel,
+        [shape(NZ // 2, 4, BLK, BLK)] * 2,
+        (place, own_part, from_other),
+        n_smem=1,
+        moved=3 * mib,
+    )
     by_x = exchange(grads, "dp", X_GROUPS)
+    by_x, chip_keep, chip_send = lax.optimization_barrier((by_x, chip_keep, chip_send))
+    from_pair = lax.ppermute(chip_send, "mp", PAIR_SWAP)
     x_done = call(x_sum_kernel, shape(NY, 2, BLK, BLK), (by_x,), moved=3 * mib)
-    x_done, chip_part = lax.optimization_barrier((x_done, chip_part))
-    columns = lax.psum_scatter(
-        chip_part.reshape(NZ * 4, BLK, BLK), "mp", scatter_dimension=0, axis_index_groups=Z_GROUPS, tiled=True
-    )
-    output, grad_tokens = call(
-        final_kernel, [shape(BLK, 2 * BLK), shape(BLK, 2 * BLK)], (columns,), moved=mib // 4
-    )
     by_y = exchange(x_done, "dp", Y_GROUPS)
+    hops = call(
+        pair_add_kernel,
+        [shape(4, BLK, BLK)] * (NZ // 2),
+        (place, chip_keep, from_pair),
+        n_smem=1,
+        moved=3 * mib // 2,
+    )
+    by_y, hops = lax.optimization_barrier((by_y, hops))
+    columns = [hops[0]]
+    for hop in range(1, NZ // 2):
+        pairs = [(2 * z + c, 2 * ((z + 2 * hop) % NZ) + c) for z in range(NZ) for c in range(2)]
+        columns.append(lax.ppermute(hops[hop], "mp", pairs))
     y_done = call(y_sum_kernel, shape(NY, 2, BLK, BLK), (by_y,), moved=mib)
     all_y = exchange(y_done, "dp", Y_GROUPS)
+    output, grad_tokens = call(
+        final_kernel, [shape(BLK, 2 * BLK), shape(BLK, 2 * BLK)], columns, moved=mib
+    )
     spread = call(spread_kernel, shape(NX, 2, NY, BLK, BLK), (all_y,), moved=3 * mib)
     all_x = exchange(spread, "dp", X_GROUPS)
     grad_up, grad_down = call(

time: 171 us -> 160 us (0.936)
  starting transfers between devices: 17.8 us -> 34.2 us
  between operations: 14.2 us -> 0.8 us
  waiting for transfers between devices: 52.9 us -> 42 us
  blocking collectives: 62.8 us -> 59.6 us
    ppermute x0 -> x4, waiting for transfers between devices: none -> 20.2 us  [the longest x1 12.4 us: body(): from_pair = lax.ppermute(chip_send, 'mp', PAIR_SWAP)]
    reduce_scatter x1 -> x0, waiting for transfers between devices: 19.7 us -> none  [body(): lax.psum_scatter(chip_part.reshape(NZ * 4, BLK, BLK), 'mp', scatter_dimen...]
    ppermute x0 -> x4, starting transfers between devices: none -> 12.9 us  [the longest x3 10.4 us: body(): columns.append(lax.ppermute(hops[hop], 'mp', pairs))]
    all_to_all x3, waiting for transfers between devices: 29.9 us -> 19.2 us  [exchange(): return lax.all_to_all(x, axis, 0, 0, tiled=True, axis_index_groups=groups)]
    all_to_all x3, starting transfers between devices: 13.9 us -> 17.5 us  [exchange(): return lax.all_to_all(x, axis, 0, 0, tiled=True, axis_index_groups=groups)]
    all_to_all x2, blocking collectives: 62.8 us -> 59.6 us  [exchange(): return lax.all_to_all(x, axis, 0, 0, tiled=True, axis_index_groups=groups)]
    unnamed x20 -> x18, local copies, waits for them, and re-layouts: 6.58 us -> 5.67 us
    pallas_call x11 -> x12, Pallas kernels: 15.5 us -> 15.9 us  [call(): pl.pallas_call(kernel, out_shape=outs, in_specs=smem(n_smem) + whole(len(...]
  transfers between devices with their start and end apart: 6 -> 9, of which waited for: 4 -> 7; matrix products, arithmetic and copies ran while one was open for 0% -> 0% of each run, Pallas kernels for 4% -> 4%
where the time goes in v2:
time: 160 us; the launch traced here: 158 us
  blocking collectives  59.6 us (37%)
  waiting for transfers between devices  42 us (26%)
  starting transfers between devices  34.2 us (21%)
  Pallas kernels  15.9 us (10%)
  local copies, waits for them, and re-layouts  5.67 us (4%)
    all_to_all x2, blocking collectives, exchange(): return lax.all_to_all(x, axis, 0, 0, tiled=True, axis_index_groups=groups)  59.6 us
    all_to_all x3, waiting for transfers between devices, exchange(): return lax.all_to_all(x, axis, 0, 0, tiled=True, axis_index_groups=groups)  19.2 us
    all_to_all x3, starting transfers between devices, exchange(): return lax.all_to_all(x, axis, 0, 0, tiled=True, axis_index_groups=groups)  17.5 us
    pallas_call x12, Pallas kernels, call(): pl.pallas_call(kernel, out_shape=outs, in_specs=smem(n_smem) + whole(len(...  15.9 us
    ppermute x1, waiting for transfers between devices, body(): from_pair = lax.ppermute(chip_send, 'mp', PAIR_SWAP)  12.4 us
    ppermute x3, starting transfers between devices, body(): columns.append(lax.ppermute(hops[hop], 'mp', pairs))  10.4 us
    ppermute x3, waiting for transfers between devices, body(): columns.append(lax.ppermute(hops[hop], 'mp', pairs))  7.8 us
    unnamed x18, local copies, waits for them, and re-layouts  5.67 us
  transfers between devices with their start and end apart: 9, of which 7 were waited for; matrix products, arithmetic and copies ran while one was open for 0% of the time, Pallas kernels for 4%

profile of v2, /device:TPU:6, one launch (start us, length us, event | category | flops | bytes accessed | tf_op | source)
XLA Modules:
  0.0 158.2 jit_solution(12970256454844846771)
XLA Ops:
  0.6 0.0 copy-start
  0.6 0.0 copy-start.1
  0.7 0.0 copy-start.6
  0.7 1.0 copy-done.6
  1.6 0.0 copy-start.7
  1.6 0.8 copy-done.7
  2.5 0.1 shard_map.85
  2.6 0.0 copy-start.8
  2.6 38.8 %all_to_all.25.own_ref = bf16[8,4,128,128]{3,2,1,0:T(8,128)(2,1)S(1)} all-to-all(bf16[8,4,128,128]{3,2,1,0:T(8,128)(2,1)S(1)} %shard_map.85), channel_id=1, replica_groups={{0,2,4,6,8,10,12,14},{1,3,5,7,9,11,13,15},{16,18,20,22,24,26,28,30},{17..., dimensions={0} | all-to-all | bytes 2097152 | tf_op jit(solution)/shard_map/all_to_all | solution.py:216
  41.5 1.9 %collective-permute-start = (bf16[8,4,128,128]{3,2,1,0:T(8,128)(2,1)S(1)}, bf16[8,4,128,128]{3,2,1,0:T(8,128)(2,1)}, u32[]{:S(2)}, u32[]{:S(2)}) collective-permute-start(bf16[8,4,128,128]{3,2,1,0:T(8,128)(2,1)S(1)} %all_to_all.25.own_ref), channel_id=1, source_target_pairs={{0,1},{1,0},{2,3},{3,2},{4,5},{5,4},{6,7},{7,6},{8,9},{9,8},{10,11... | collective-permute-start | bytes 3145736 | tf_op jit(solution)/shard_map/ppermute | solution.py:241
  43.4 0.0 copy-done
  43.4 0.0 copy-done.1
  43.4 0.6 shard_map.86
  44.0 0.0 copy-start.2
  44.0 1.0 copy-done.2
  45.0 0.0 copy-done.8
  45.0 1.6 %shard_map.84.table_ref = s32[128]{0:T(128)S(1)} custom-call(s32[8,32]{1,0:T(8,128)S(1)} %copy-done.8), custom_call_target="tpu_custom_call" | custom-call | flops 1048576 | bytes 1024 | tf_op jit(solution)/shard_map/pallas_call | solution.py:204
  46.6 0.1 pad_add_fusion.place_ref
  46.7 0.0 collective-permute-done.other_ref
  46.7 5.4 %shard_map.87 = (bf16[4,2,8,128,128]{4,3,2,1,0:T(8,128)(2,1)}, bf16[8,128,128]{2,1,0:T(8,128)(2,1)S(1)}, bf16[8,128,128]{2,1,0:T(8,128)(2,1)S(1)}) custom-call(s32[128]{0:T(128)S(1)} %shard_map.84.table_ref, s32[2]{0:T(128)S(1)} %pad_add_fusion.place_ref, bf16[8,4,128,128]{3,2,1,0:T(8,128)(2,1)S(1)} %all_to_all.25.own_ref, ...), custom_call_target="tpu_custom_call" | custom-call | flops 536870912 | bytes 6291456 | tf_op jit(solution)/shard_map/pallas_call | solution.py:204
  52.1 0.7 copy-done.4
  52.8 4.8 %all-to-all-start.1 = ((bf16[4,2,8,128,128]{4,3,2,1,0:T(8,128)(2,1)}), bf16[4,2,8,128,128]{4,3,2,1,0:T(8,128)(2,1)S(1)}, u32[]{:S(2)}, u32[]{:S(2)}) async-start(bf16[4,2,8,128,128]{4,3,2,1,0:T(8,128)(2,1)} %get-tuple-element.30), calls=%async_computation.1 | async-start | bytes 4194304 | tf_op jit(solution)/shard_map/all_to_all | solution.py:216
  57.6 1.2 copy-done.3
  58.8 0.9 copy-done.5
  59.8 1.7 %shard_map.88 = (bf16[8,4,128,128]{3,2,1,0:T(8,128)(2,1)S(1)}, bf16[8,4,128,128]{3,2,1,0:T(8,128)(2,1)S(1)}) custom-call(s32[128]{0:T(128)S(1)} %shard_map.84.table_ref, s32[2]{0:T(128)S(1)} %pad_add_fusion.place_ref, bf16[8,128,128]{2,1,0:T(8,128)(2,1)S(1)} %get-tuple-element.31.act_ref, bf16[8,128,128]{2,1,0:T(8,128)(2,1)S(1)} %copy-done.5, ...), custom_call_target="tpu_custom_call" | custom-call | flops 268435456 | bytes 5242880 | tf_op jit(solution)/shard_map/pallas_call | solution.py:204
  61.5 1.9 %collective-permute-start.1 = (bf16[8,4,128,128]{3,2,1,0:T(8,128)(2,1)S(1)}, bf16[8,4,128,128]{3,2,1,0:T(8,128)(2,1)S(1)}, u32[]{:S(2)}, u32[]{:S(2)}) collective-permute-start(bf16[8,4,128,128]{3,2,1,0:T(8,128)(2,1)S(1)} %get-tuple-element.35), channel_id=1, source_target_pairs={{0,1},{1,0},{2,3},{3,2},{4,5},{5,4},{6,7},{7,6},{8,9},{9,8},{10,11... | collective-permute-start | bytes 3145736 | tf_op jit(solution)/shard_map/ppermute | solution.py:265
  63.4 2.6 %collective-permute-done.1.b_ref = bf16[8,4,128,128]{3,2,1,0:T(8,128)(2,1)S(1)} collective-permute-done((bf16[8,4,128,128]{3,2,1,0:T(8,128)(2,1)S(1)}, bf16[8,4,128,128]{3,2,1,0:T(8,128)(2,1)S(1)}, u32[]{:S(2)}, u32[]{:S(2)}) %collective-permute-start.1) | collective-permute-done | bytes 1048608 | tf_op jit(solution)/shard_map/ppermute | solution.py:265
  66.0 0.8 shard_map.89
  66.8 15.7 %all-to-all-done.1.in_ref = bf16[4,2,8,128,128]{4,3,2,1,0:T(8,128)(2,1)S(1)} async-done(((bf16[4,2,8,128,128]{4,3,2,1,0:T(8,128)(2,1)}), bf16[4,2,8,128,128]{4,3,2,1,0:T(8,128)(2,1)S(1)}, u32[]{:S(2)}, u32[]{:S(2)}) %all-to-all-start.1) | async-done | bytes 2097184 | tf_op jit(solution)/shard_map/all_to_all | solution.py:216
  82.5 1.0 shard_map.90
  83.5 7.1 %all-to-all-start.2 = ((bf16[8,2,128,128]{3,2,1,0:T(8,128)(2,1)}), bf16[8,2,128,128]{3,2,1,0:T(8,128)(2,1)S(1)}, u32[]{:S(2)}, u32[]{:S(2)}) async-start(bf16[8,2,128,128]{3,2,1,0:T(8,128)(2,1)} %shard_map.90), calls=%async_computation.2 | async-start | bytes 1048576 | tf_op jit(solution)/shard_map/all_to_all | solution.py:216
  90.7 2.5 %collective-permute-start.2 = (bf16[4,4,128,128]{3,2,1,0:T(8,128)(2,1)S(1)}, bf16[4,4,128,128]{3,2,1,0:T(8,128)(2,1)S(1)}, u32[]{:S(2)}, u32[]{:S(2)}) collective-permute-start(bf16[4,4,128,128]{3,2,1,0:T(8,128)(2,1)S(1)} %get-tuple-element.40), channel_id=1, source_target_pairs={{0,2},{1,3},{2,0},{3,1},{4,6},{5,7},{6,4},{7,5},{8,10},{9,11},{10,... | collective-permute-start | bytes 1572872 | tf_op jit(solution)/shard_map/ppermute | solution.py:275
  93.1 12.4 %collective-permute-done.2.b_ref = bf16[4,4,128,128]{3,2,1,0:T(8,128)(2,1)S(1)} collective-permute-done((bf16[4,4,128,128]{3,2,1,0:T(8,128)(2,1)S(1)}, bf16[4,4,128,128]{3,2,1,0:T(8,128)(2,1)S(1)}, u32[]{:S(2)}, u32[]{:S(2)}) %collective-permute-start.2) | collective-permute-done | bytes 524320 | tf_op jit(solution)/shard_map/ppermute | solution.py:275
  105.5 0.7 shard_map.91
  106.2 1.6 all-to-all-done.2.in_ref
  107.7 0.1 shard_map.93
  107.8 20.8 %all_to_all.26.in_ref = bf16[8,2,128,128]{3,2,1,0:T(8,128)(2,1)S(1)} all-to-all(bf16[8,2,128,128]{3,2,1,0:T(8,128)(2,1)S(1)} %shard_map.93), channel_id=1, replica_groups={{0,64,128,192,256,320,384,448},{16,80,144,208,272,336,400,464},{32,96,1..., dimensions={0} | all-to-all | bytes 1048576 | tf_op jit(solution)/shard_map/all_to_all | solution.py:216
  128.6 1.6 %shard_map.94 = bf16[4,2,8,128,128]{4,3,2,1,0:T(8,128)(2,1)} custom-call(bf16[8,2,128,128]{3,2,1,0:T(8,128)(2,1)S(1)} %all_to_all.26.in_ref), custom_call_target="tpu_custom_call" | custom-call | bytes 3145728 | tf_op jit(solution)/shard_map/pallas_call | solution.py:204
  130.2 5.6 %all-to-all-start.4 = ((bf16[4,2,8,128,128]{4,3,2,1,0:T(8,128)(2,1)}), bf16[4,2,8,128,128]{4,3,2,1,0:T(8,128)(2,1)S(1)}, u32[]{:S(2)}, u32[]{:S(2)}) async-start(bf16[4,2,8,128,128]{4,3,2,1,0:T(8,128)(2,1)} %shard_map.94), calls=%async_computation.4 | async-start | bytes 4194304 | tf_op jit(solution)/shard_map/all_to_all | solution.py:216
  135.8 2.0 %collective-permute-start.3 = (bf16[4,128,128]{2,1,0:T(8,128)(2,1)S(1)}, bf16[4,128,128]{2,1,0:T(8,128)(2,1)S(1)}, u32[]{:S(2)}, u32[]{:S(2)}) collective-permute-start(bf16[4,128,128]{2,1,0:T(8,128)(2,1)S(1)} %get-tuple-element.46), channel_id=1, source_target_pairs={{0,4},{1,5},{2,6},{3,7},{4,8},{5,9},{6,10},{7,11},{8,12},{9,13},{1... | collective-permute-start | bytes 393224 | tf_op jit(solution)/shard_map/ppermute | solution.py:289
  137.8 4.5 %collective-permute-start.4 = (bf16[4,128,128]{2,1,0:T(8,128)(2,1)S(1)}, bf16[4,128,128]{2,1,0:T(8,128)(2,1)S(1)}, u32[]{:S(2)}, u32[]{:S(2)}) collective-permute-start(bf16[4,128,128]{2,1,0:T(8,128)(2,1)S(1)} %get-tuple-element.47), channel_id=1, source_target_pairs={{0,8},{1,9},{2,10},{3,11},{4,12},{5,13},{6,14},{7,15},{8,0},{9,1},... | collective-permute-start | bytes 393224 | tf_op jit(solution)/shard_map/ppermute | solution.py:289
  142.3 3.9 %collective-permute-start.5 = (bf16[4,128,128]{2,1,0:T(8,128)(2,1)S(1)}, bf16[4,128,128]{2,1,0:T(8,128)(2,1)S(1)}, u32[]{:S(2)}, u32[]{:S(2)}) collective-permute-start(bf16[4,128,128]{2,1,0:T(8,128)(2,1)S(1)} %get-tuple-element.48), channel_id=1, source_target_pairs={{0,12},{1,13},{2,14},{3,15},{4,0},{5,1},{6,2},{7,3},{8,4},{9,5},{1... | collective-permute-start | bytes 393224 | tf_op jit(solution)/shard_map/ppermute | solution.py:289
  146.2 0.0 collective-permute-done.3.refs_1_
  146.2 4.1 %collective-permute-done.4.refs_2_ = bf16[4,128,128]{2,1,0:T(8,128)(2,1)S(1)} collective-permute-done((bf16[4,128,128]{2,1,0:T(8,128)(2,1)S(1)}, bf16[4,128,128]{2,1,0:T(8,128)(2,1)S(1)}, u32[]{:S(2)}, u32[]{:S(2)}) %collective-permute-start.4) | collective-permute-done | bytes 131104 | tf_op jit(solution)/shard_map/ppermute | solution.py:289
  150.4 3.7 %collective-permute-done.5.refs_3_ = bf16[4,128,128]{2,1,0:T(8,128)(2,1)S(1)} collective-permute-done((bf16[4,128,128]{2,1,0:T(8,128)(2,1)S(1)}, bf16[4,128,128]{2,1,0:T(8,128)(2,1)S(1)}, u32[]{:S(2)}, u32[]{:S(2)}) %collective-permute-start.5) | collective-permute-done | bytes 131104 | tf_op jit(solution)/shard_map/ppermute | solution.py:289
  154.0 0.8 shard_map.92
  154.8 1.9 %all-to-all-done.4.in_ref = bf16[4,2,8,128,128]{4,3,2,1,0:T(8,128)(2,1)S(1)} async-done(((bf16[4,2,8,128,128]{4,3,2,1,0:T(8,128)(2,1)}), bf16[4,2,8,128,128]{4,3,2,1,0:T(8,128)(2,1)S(1)}, u32[]{:S(2)}, u32[]{:S(2)}) %all-to-all-start.4) | async-done | bytes 2097184 | tf_op jit(solution)/shard_map/all_to_all | solution.py:216
  156.8 1.5 shard_map.95
  (3 shorter events, 0.0 us)
Async XLA Ops:
  0.6 42.8 %copy-start = (bf16[32,128,128]{2,1,0:T(8,128)(2,1)S(1)}, bf16[32,128,128]{2,1,0:T(8,128)(2,1)}, u32[]{:S(2)}) copy-start(bf16[32,128,128]{2,1,0:T(8,128)(2,1)} %down_ref.3) | copy-start | bytes 3145732
  0.6 42.8 %copy-start.1 = (bf16[32,128,128]{2,1,0:T(8,128)(2,1)S(1)}, bf16[32,128,128]{2,1,0:T(8,128)(2,1)}, u32[]{:S(2)}) copy-start(bf16[32,128,128]{2,1,0:T(8,128)(2,1)} %up_ref.3) | copy-start | bytes 3145732
  0.7 1.0 copy-start.6
  1.6 0.8 copy-start.7
  2.6 42.4 %copy-start.8 = (s32[8,32]{1,0:T(8,128)S(1)}, s32[8,32]{1,0:T(8,128)}, u32[]{:S(2)}) copy-start(s32[8,32]{1,0:T(8,128)} %mask_ref.1) | copy-start | bytes 3076
  41.5 5.3 %collective-permute-start = (bf16[8,4,128,128]{3,2,1,0:T(8,128)(2,1)S(1)}, bf16[8,4,128,128]{3,2,1,0:T(8,128)(2,1)}, u32[]{:S(2)}, u32[]{:S(2)}) collective-permute-start(bf16[8,4,128,128]{3,2,1,0:T(8,128)(2,1)S(1)} %all_to_all.25.own_ref), channel_id=1, source_target_pairs={{0,1},{1,0},{2,3},{3,2},{4,5},{5,4},{6,7},{7,6},{8,9},{9,8},{10,11... | collective-permute-start | bytes 3145736 | tf_op jit(solution)/shard_map/ppermute | solution.py:241
  44.0 1.0 copy-start.2
  52.1 0.7 copy-start.4
  52.8 29.7 %all-to-all-start.1 = ((bf16[4,2,8,128,128]{4,3,2,1,0:T(8,128)(2,1)}), bf16[4,2,8,128,128]{4,3,2,1,0:T(8,128)(2,1)S(1)}, u32[]{:S(2)}, u32[]{:S(2)}) async-start(bf16[4,2,8,128,128]{4,3,2,1,0:T(8,128)(2,1)} %get-tuple-element.30), calls=%async_computation.1 | async-start | bytes 4194304 | tf_op jit(solution)/shard_map/all_to_all | solution.py:216
  57.6 1.2 copy-start.3
  58.8 0.9 copy-start.5
  61.5 4.6 %collective-permute-start.1 = (bf16[8,4,128,128]{3,2,1,0:T(8,128)(2,1)S(1)}, bf16[8,4,128,128]{3,2,1,0:T(8,128)(2,1)S(1)}, u32[]{:S(2)}, u32[]{:S(2)}) collective-permute-start(bf16[8,4,128,128]{3,2,1,0:T(8,128)(2,1)S(1)} %get-tuple-element.35), channel_id=1, source_target_pairs={{0,1},{1,0},{2,3},{3,2},{4,5},{5,4},{6,7},{7,6},{8,9},{9,8},{10,11... | collective-permute-start | bytes 3145736 | tf_op jit(solution)/shard_map/ppermute | solution.py:265
  83.5 24.2 %all-to-all-start.2 = ((bf16[8,2,128,128]{3,2,1,0:T(8,128)(2,1)}), bf16[8,2,128,128]{3,2,1,0:T(8,128)(2,1)S(1)}, u32[]{:S(2)}, u32[]{:S(2)}) async-start(bf16[8,2,128,128]{3,2,1,0:T(8,128)(2,1)} %shard_map.90), calls=%async_computation.2 | async-start | bytes 1048576 | tf_op jit(solution)/shard_map/all_to_all | solution.py:216
  90.7 14.8 %collective-permute-start.2 = (bf16[4,4,128,128]{3,2,1,0:T(8,128)(2,1)S(1)}, bf16[4,4,128,128]{3,2,1,0:T(8,128)(2,1)S(1)}, u32[]{:S(2)}, u32[]{:S(2)}) collective-permute-start(bf16[4,4,128,128]{3,2,1,0:T(8,128)(2,1)S(1)} %get-tuple-element.40), channel_id=1, source_target_pairs={{0,2},{1,3},{2,0},{3,1},{4,6},{5,7},{6,4},{7,5},{8,10},{9,11},{10,... | collective-permute-start | bytes 1572872 | tf_op jit(solution)/shard_map/ppermute | solution.py:275
  130.2 26.6 %all-to-all-start.4 = ((bf16[4,2,8,128,128]{4,3,2,1,0:T(8,128)(2,1)}), bf16[4,2,8,128,128]{4,3,2,1,0:T(8,128)(2,1)S(1)}, u32[]{:S(2)}, u32[]{:S(2)}) async-start(bf16[4,2,8,128,128]{4,3,2,1,0:T(8,128)(2,1)} %shard_map.94), calls=%async_computation.4 | async-start | bytes 4194304 | tf_op jit(solution)/shard_map/all_to_all | solution.py:216
  135.8 10.4 %collective-permute-start.3 = (bf16[4,128,128]{2,1,0:T(8,128)(2,1)S(1)}, bf16[4,128,128]{2,1,0:T(8,128)(2,1)S(1)}, u32[]{:S(2)}, u32[]{:S(2)}) collective-permute-start(bf16[4,128,128]{2,1,0:T(8,128)(2,1)S(1)} %get-tuple-element.46), channel_id=1, source_target_pairs={{0,4},{1,5},{2,6},{3,7},{4,8},{5,9},{6,10},{7,11},{8,12},{9,13},{1... | collective-permute-start | bytes 393224 | tf_op jit(solution)/shard_map/ppermute | solution.py:289
  137.8 12.6 %collective-permute-start.4 = (bf16[4,128,128]{2,1,0:T(8,128)(2,1)S(1)}, bf16[4,128,128]{2,1,0:T(8,128)(2,1)S(1)}, u32[]{:S(2)}, u32[]{:S(2)}) collective-permute-start(bf16[4,128,128]{2,1,0:T(8,128)(2,1)S(1)} %get-tuple-element.47), channel_id=1, source_target_pairs={{0,8},{1,9},{2,10},{3,11},{4,12},{5,13},{6,14},{7,15},{8,0},{9,1},... | collective-permute-start | bytes 393224 | tf_op jit(solution)/shard_map/ppermute | solution.py:289
  142.3 11.7 %collective-permute-start.5 = (bf16[4,128,128]{2,1,0:T(8,128)(2,1)S(1)}, bf16[4,128,128]{2,1,0:T(8,128)(2,1)S(1)}, u32[]{:S(2)}, u32[]{:S(2)}) collective-permute-start(bf16[4,128,128]{2,1,0:T(8,128)(2,1)S(1)} %get-tuple-element.48), channel_id=1, source_target_pairs={{0,12},{1,13},{2,14},{3,15},{4,0},{5,1},{6,2},{7,3},{8,4},{9,5},{1... | collective-permute-start | bytes 393224 | tf_op jit(solution)/shard_map/ppermute | solution.py:289

commit v3 on v1

--- a/solution.py
+++ b/solution.py
@@ -1,3 +1,5 @@
+import functools
+
 import jax
 import jax.numpy as jnp
 from jax import lax
@@ -9,10 +11,38 @@
 F32 = jnp.float32
 VM = pltpu.CompilerParams(vmem_limit_bytes=48 * 1024 * 1024)
 NX, NY, NZ = 4, 8, 8
-X_GROUPS = [[NX * y + x for x in range(NX)] for y in range(NY)]
-Y_GROUPS = [[NX * y + x for y in range(NY)] for x in range(NX)]
+N_MP = 2 * NZ
+
+
+def flat(x, y, mp):
+    return ((y % NY) * NX + x % NX) * N_MP + mp
+
+
+NEAR_GROUPS = [
+    [flat(2 * bx + mp % 2 + i, 2 * by + mp % 2 + j, mp) for j in range(2) for i in range(2)]
+    for mp in range(N_MP)
+    for by in range(NY // 2)
+    for bx in range(NX // 2)
+]
+FAR_GROUPS = [
+    [flat(2 * bx + mp % 2 + i, 2 * by + mp % 2 + j, mp) for by in range(NY // 2) for bx in range(NX // 2)]
+    for mp in range(N_MP)
+    for j in range(2)
+    for i in range(2)
+]
 Z_GROUPS = [[2 * z + c for z in range(NZ)] for c in range(2)]
 CORE_SWAP = [(i, i ^ 1) for i in range(2 * NZ)]
+
+
+def z_swap(level):
+    step = 1 << level
+    return [
+        (2 * z + c, 2 * ((z + (step if ((z >> level) + c) % 2 == 0 else -step)) % NZ) + c)
+        for z in range(NZ)
+        for c in range(2)
+    ]
+
+
 SLOTS, ROWS, COLS, BLK = 32, 8, 32, 128
 
 
@@ -66,9 +96,9 @@
 
 
 def first_kernel(
-    table_ref, core_ref, own_ref, other_ref, up_t_ref, down_ref, grads_ref, act_ref, pre_ref, panels, hid, dac
+    table_ref, place_ref, own_ref, other_ref, up_t_ref, down_ref, grads_ref, act_ref, pre_ref, panels, hid, dac
 ):
-    core = core_ref[0]
+    core = place_ref[0]
     panels[0] = own_ref[...]
     panels[1] = other_ref[...]
 
@@ -103,8 +133,8 @@
         grads_ref[s // 8, 1, s % 8] = jnp.where(used, down_part, 0.0).astype(BF)
 
 
-def second_kernel(table_ref, core_ref, act_ref, pre_ref, down_t_ref, up_ref, own_ref, send_ref, out_sum, grad_sum):
-    core = core_ref[0]
+def second_kernel(table_ref, place_ref, act_ref, pre_ref, down_t_ref, up_ref, own_ref, send_ref, out_sum, grad_sum):
+    core = place_ref[0]
     out_sum[...] = jnp.zeros_like(out_sum)
     grad_sum[...] = jnp.zeros_like(grad_sum)
     for s in range(SLOTS):
@@ -125,8 +155,13 @@
             send_ref[z, 2 + j] = grad_sum[other].astype(BF)
 
 
-def add_kernel(a_ref, b_ref, out_ref):
-    out_ref[...] = (a_ref[...].astype(F32) + b_ref[...].astype(F32)).astype(BF)
+def halve_kernel(level, place_ref, a_ref, b_ref, keep_ref, send_ref):
+    bit = (place_ref[1] >> level) & 1
+    for half in range(NZ >> (level + 1)):
+        near = 2 * half + bit
+        far = 2 * half + 1 - bit
+        keep_ref[half] = (a_ref[near].astype(F32) + b_ref[near].astype(F32)).astype(BF)
+        send_ref[half] = (a_ref[far].astype(F32) + b_ref[far].astype(F32)).astype(BF)
 
 
 def x_sum_kernel(in_ref, out_ref):
@@ -162,10 +197,11 @@
         down_ref[x * 8 : (x + 1) * 8] = in_ref[x, 1]
 
 
-def final_kernel(in_ref, out_ref, grad_ref):
-    for j in range(2):
-        out_ref[:, j * BLK : (j + 1) * BLK] = in_ref[j].T
-        grad_ref[:, j * BLK : (j + 1) * BLK] = in_ref[2 + j].T
+def final_kernel(a_ref, b_ref, out_ref, grad_ref):
+    for j in range(4):
+        total = a_ref[0, j].astype(F32) + b_ref[0, j].astype(F32)
+        goal = out_ref if j < 2 else grad_ref
+        goal[:, (j % 2) * BLK : (j % 2 + 1) * BLK] = total.T.astype(BF)
 
 
 def whole(count):
@@ -201,7 +237,8 @@
 
 def body(tokens, cotangent, block_mask, up_tiles, down_tiles):
     mib = 1 << 20
-    core = (lax.axis_index("mp") % 2).astype(jnp.int32).reshape(1)
+    position = lax.axis_index("mp")
+    place = jnp.stack([position & 1, position >> 1]).astype(jnp.int32)
     sent = call(prep_kernel, shape(NZ, 4, BLK, BLK), (tokens, cotangent), moved=mib)
     own_panels = exchange(sent, "mp", Z_GROUPS)
     table = call(
@@ -225,7 +262,7 @@
     grads, act, pre = call(
         first_kernel,
         [shape(NX, 2, 8, BLK, BLK), shape(ROWS, BLK, BLK), shape(ROWS, BLK, BLK)],
-        (table, core, own_panels, other_panels, up_t, down_tiles),
+        (table, place, own_panels, other_panels, up_t, down_tiles),
         n_smem=2,
         scratch=[
             pltpu.VMEM((2, NZ, 4, BLK, BLK), BF),
@@ -238,28 +275,43 @@
     own_part, other_part = call(
         second_kernel,
         [shape(NZ, 4, BLK, BLK), shape(NZ, 4, BLK, BLK)],
-        (table, core, act, pre, down_t, up_tiles),
+        (table, place, act, pre, down_t, up_tiles),
         n_smem=2,
         scratch=[pltpu.VMEM((COLS, BLK, BLK), F32), pltpu.VMEM((COLS, BLK, BLK), F32)],
         flops=2 * product,
         moved=5 * mib,
     )
     from_other = lax.ppermute(other_part, "mp", CORE_SWAP)
-    chip_part = call(add_kernel, shape(NZ, 4, BLK, BLK), (own_part, from_other), moved=3 * mib)
-    by_x = exchange(grads, "dp", X_GROUPS)
+
+    def halve(level, a, b):
+        count = NZ >> (level + 1)
+        return call(
+            functools.partial(halve_kernel, level),
+            [shape(count, 4, BLK, BLK)] * 2,
+            (place, a, b),
+            n_smem=1,
+            moved=count * mib // 2,
+        )
+
+    keep, send = halve(0, own_part, from_other)
+    by_x = exchange(grads, ("dp", "mp"), NEAR_GROUPS)
+    by_x, keep, send = lax.optimization_barrier((by_x, keep, send))
     x_done = call(x_sum_kernel, shape(NY, 2, BLK, BLK), (by_x,), moved=3 * mib)
-    x_done, chip_part = lax.optimization_barrier((x_done, chip_part))
-    columns = lax.psum_scatter(
-        chip_part.reshape(NZ * 4, BLK, BLK), "mp", scatter_dimension=0, axis_index_groups=Z_GROUPS, tiled=True
-    )
+    keep, send = halve(1, keep, lax.ppermute(send, "mp", z_swap(0)))
+    by_y = exchange(x_done, ("dp", "mp"), FAR_GROUPS)
+    by_y, keep, send = lax.optimization_barrier((by_y, keep, send))
+    y_done = call(y_sum_kernel, shape(NY, 2, BLK, BLK), (by_y,), moved=mib)
+    keep, send = halve(2, keep, lax.ppermute(send, "mp", z_swap(1)))
+    all_y = exchange(y_done, ("dp", "mp"), FAR_GROUPS)
+    all_y, keep, send = lax.optimization_barrier((all_y, keep, send))
+    spread = call(spread_kernel, shape(NX, 2, NY, BLK, BLK), (all_y,), moved=3 * mib)
     output, grad_tokens = call(
-        final_kernel, [shape(BLK, 2 * BLK), shape(BLK, 2 * BLK)], (columns,), moved=mib // 4
-    )
-    by_y = exchange(x_done, "dp", Y_GROUPS)
-    y_done = call(y_sum_kernel, shape(NY, 2, BLK, BLK), (by_y,), moved=mib)
-    all_y = exchange(y_done, "dp", Y_GROUPS)
-    spread = call(spread_kernel, shape(NX, 2, NY, BLK, BLK), (all_y,), moved=3 * mib)
-    all_x = exchange(spread, "dp", X_GROUPS)
+        final_kernel,
+        [shape(BLK, 2 * BLK), shape(BLK, 2 * BLK)],
+        (keep, lax.ppermute(send, "mp", z_swap(2))),
+        moved=mib // 2,
+    )
+    all_x = exchange(spread, ("dp", "mp"), NEAR_GROUPS)
     grad_up, grad_down = call(
         split_kernel, [shape(SLOTS, BLK, BLK), shape(SLOTS, BLK, BLK)], (all_x,), moved=4 * mib
     )

time: 171 us -> 146 us (0.85)
  blocking collectives: 62.8 us -> 38.8 us
  starting transfers between devices: 17.8 us -> 37.3 us
  between operations: 14.2 us -> 0.8 us
  waiting for transfers between devices: 52.9 us -> 43.7 us
  Pallas kernels: 15.5 us -> 17.3 us
    ppermute x0 -> x3, waiting for transfers between devices: none -> 30.1 us  [the longest x1 11.6 us: body(): lax.ppermute(send, 'mp', z_swap(2))]
    all_to_all x2 -> x1, blocking collectives: 62.8 us -> 38.8 us  [exchange(): return lax.all_to_all(x, axis, 0, 0, tiled=True, axis_index_groups=groups)]
    reduce_scatter x1 -> x0, waiting for transfers between devices: 19.7 us -> none  [body(): lax.psum_scatter(chip_part.reshape(NZ * 4, BLK, BLK), 'mp', scatter_dimen...]
    all_to_all x3 -> x4, waiting for transfers between devices: 29.9 us -> 11.3 us  [exchange(): return lax.all_to_all(x, axis, 0, 0, tiled=True, axis_index_groups=groups)]
    all_to_all x3 -> x4, starting transfers between devices: 13.9 us -> 23.7 us  [exchange(): return lax.all_to_all(x, axis, 0, 0, tiled=True, axis_index_groups=groups)]
    ppermute x0 -> x3, starting transfers between devices: none -> 6.91 us  [the longest x1 2.49 us: body(): lax.ppermute(send, 'mp', z_swap(2))]
    ppermute x1, starting transfers between devices: 1.92 us -> 4.77 us  [body(): from_other = lax.ppermute(other_part, 'mp', CORE_SWAP)]
    pallas_call x11 -> x13, Pallas kernels: 15.5 us -> 17.3 us  [call(): pl.pallas_call(kernel, out_shape=outs, in_specs=smem(n_smem) + whole(len(...]
  transfers between devices with their start and end apart: 6 -> 9, of which waited for: 4 -> 7; matrix products, arithmetic and copies ran while one was open for 0% -> 0% of each run, Pallas kernels for 4% -> 5%
where the time goes in v3:
time: 146 us; the launch traced here: 144 us
  waiting for transfers between devices  43.7 us (30%)
  blocking collectives  38.8 us (27%)
  starting transfers between devices  37.3 us (26%)
  Pallas kernels  17.3 us (12%)
  local copies, waits for them, and re-layouts  5.67 us (4%)
    all_to_all x1, blocking collectives, exchange(): return lax.all_to_all(x, axis, 0, 0, tiled=True, axis_index_groups=groups)  38.8 us
    all_to_all x4, starting transfers between devices, exchange(): return lax.all_to_all(x, axis, 0, 0, tiled=True, axis_index_groups=groups)  23.7 us
    pallas_call x13, Pallas kernels, call(): pl.pallas_call(kernel, out_shape=outs, in_specs=smem(n_smem) + whole(len(...  17.3 us
    ppermute x1, waiting for transfers between devices, body(): lax.ppermute(send, 'mp', z_swap(2))  11.6 us
    all_to_all x4, waiting for transfers between devices, exchange(): return lax.all_to_all(x, axis, 0, 0, tiled=True, axis_index_groups=groups)  11.3 us
    ppermute x1, waiting for transfers between devices, body(): keep, send = halve(2, keep, lax.ppermute(send, 'mp', z_swap(1)))  9.99 us
    ppermute x1, waiting for transfers between devices, body(): keep, send = halve(1, keep, lax.ppermute(send, 'mp', z_swap(0)))  8.59 us
    unnamed x18, local copies, waits for them, and re-layouts  5.67 us
  transfers between devices with their start and end apart: 9, of which 7 were waited for; matrix products, arithmetic and copies ran while one was open for 0% of the time, Pallas kernels for 5%

profile of v3, /device:TPU:6, one launch (start us, length us, event | category | flops | bytes accessed | tf_op | source)
XLA Modules:
  0.0 143.7 jit_solution(513260945601913266)
XLA Ops:
  0.6 0.0 copy-start
  0.6 0.0 copy-start.1
  0.7 0.0 copy-start.6
  0.7 1.0 copy-done.6
  1.6 0.0 copy-start.7
  1.6 0.8 copy-done.7
  2.5 0.1 shard_map.85
  2.6 0.0 copy-start.8
  2.6 38.8 %all_to_all.25.own_ref = bf16[8,4,128,128]{3,2,1,0:T(8,128)(2,1)S(1)} all-to-all(bf16[8,4,128,128]{3,2,1,0:T(8,128)(2,1)S(1)} %shard_map.85), channel_id=1, replica_groups={{0,2,4,6,8,10,12,14},{1,3,5,7,9,11,13,15},{16,18,20,22,24,26,28,30},{17..., dimensions={0} | all-to-all | bytes 2097152 | tf_op jit(solution)/shard_map/all_to_all | solution.py:235
  41.5 1.9 %collective-permute-start = (bf16[8,4,128,128]{3,2,1,0:T(8,128)(2,1)S(1)}, bf16[8,4,128,128]{3,2,1,0:T(8,128)(2,1)}, u32[]{:S(2)}, u32[]{:S(2)}) collective-permute-start(bf16[8,4,128,128]{3,2,1,0:T(8,128)(2,1)S(1)} %all_to_all.25.own_ref), channel_id=1, source_target_pairs={{0,1},{1,0},{2,3},{3,2},{4,5},{5,4},{6,7},{7,6},{8,9},{9,8},{10,11... | collective-permute-start | bytes 3145736 | tf_op jit(solution)/shard_map/ppermute | solution.py:260
  43.4 0.0 copy-done
  43.4 0.0 copy-done.1
  43.4 0.6 shard_map.86
  44.0 0.0 copy-start.2
  44.0 1.0 copy-done.2
  45.0 0.0 copy-done.8
  45.0 1.6 %shard_map.84.table_ref = s32[128]{0:T(128)S(1)} custom-call(s32[8,32]{1,0:T(8,128)S(1)} %copy-done.8), custom_call_target="tpu_custom_call" | custom-call | flops 1048576 | bytes 1024 | tf_op jit(solution)/shard_map/pallas_call | solution.py:223
  46.6 0.1 pad_add_fusion.place_ref
  46.7 0.0 collective-permute-done.other_ref
  46.7 5.4 %shard_map.87 = (bf16[4,2,8,128,128]{4,3,2,1,0:T(8,128)(2,1)}, bf16[8,128,128]{2,1,0:T(8,128)(2,1)S(1)}, bf16[8,128,128]{2,1,0:T(8,128)(2,1)S(1)}) custom-call(s32[128]{0:T(128)S(1)} %shard_map.84.table_ref, s32[2]{0:T(128)S(1)} %pad_add_fusion.place_ref, bf16[8,4,128,128]{3,2,1,0:T(8,128)(2,1)S(1)} %all_to_all.25.own_ref, ...), custom_call_target="tpu_custom_call" | custom-call | flops 536870912 | bytes 6291456 | tf_op jit(solution)/shard_map/pallas_call | solution.py:223
  52.1 0.7 copy-done.4
  52.8 4.4 %all-to-all-start.1 = ((bf16[4,2,8,128,128]{4,3,2,1,0:T(8,128)(2,1)}), bf16[4,2,8,128,128]{4,3,2,1,0:T(8,128)(2,1)S(1)}, u32[]{:S(2)}, u32[]{:S(2)}) async-start(bf16[4,2,8,128,128]{4,3,2,1,0:T(8,128)(2,1)} %get-tuple-element.31), calls=%async_computation.1 | async-start | bytes 4194304 | tf_op jit(solution)/shard_map/all_to_all | solution.py:235
  57.2 1.2 copy-done.3
  58.4 0.9 copy-done.5
  59.4 1.7 %shard_map.88 = (bf16[8,4,128,128]{3,2,1,0:T(8,128)(2,1)S(1)}, bf16[8,4,128,128]{3,2,1,0:T(8,128)(2,1)S(1)}) custom-call(s32[128]{0:T(128)S(1)} %shard_map.84.table_ref, s32[2]{0:T(128)S(1)} %pad_add_fusion.place_ref, bf16[8,128,128]{2,1,0:T(8,128)(2,1)S(1)} %get-tuple-element.32.act_ref, bf16[8,128,128]{2,1,0:T(8,128)(2,1)S(1)} %copy-done.5, ...), custom_call_target="tpu_custom_call" | custom-call | flops 268435456 | bytes 5242880 | tf_op jit(solution)/shard_map/pallas_call | solution.py:223
  61.1 4.8 %collective-permute-start.1 = (bf16[8,4,128,128]{3,2,1,0:T(8,128)(2,1)S(1)}, bf16[8,4,128,128]{3,2,1,0:T(8,128)(2,1)S(1)}, u32[]{:S(2)}, u32[]{:S(2)}) collective-permute-start(bf16[8,4,128,128]{3,2,1,0:T(8,128)(2,1)S(1)} %get-tuple-element.36), channel_id=1, source_target_pairs={{0,1},{1,0},{2,3},{3,2},{4,5},{5,4},{6,7},{7,6},{8,9},{9,8},{10,11... | collective-permute-start | bytes 3145736 | tf_op jit(solution)/shard_map/ppermute | solution.py:284
  65.9 2.3 %collective-permute-done.1.b_ref = bf16[8,4,128,128]{3,2,1,0:T(8,128)(2,1)S(1)} collective-permute-done((bf16[8,4,128,128]{3,2,1,0:T(8,128)(2,1)S(1)}, bf16[8,4,128,128]{3,2,1,0:T(8,128)(2,1)S(1)}, u32[]{:S(2)}, u32[]{:S(2)}) %collective-permute-start.1) | collective-permute-done | bytes 1048608 | tf_op jit(solution)/shard_map/ppermute | solution.py:284
  68.2 0.8 shard_map.89
  69.0 2.8 %all-to-all-done.1.in_ref = bf16[4,2,8,128,128]{4,3,2,1,0:T(8,128)(2,1)S(1)} async-done(((bf16[4,2,8,128,128]{4,3,2,1,0:T(8,128)(2,1)}), bf16[4,2,8,128,128]{4,3,2,1,0:T(8,128)(2,1)S(1)}, u32[]{:S(2)}, u32[]{:S(2)}) %all-to-all-start.1) | async-done | bytes 2097184 | tf_op jit(solution)/shard_map/all_to_all | solution.py:235
  71.7 1.0 shard_map.90
  72.8 10.1 %all-to-all-start.2 = ((bf16[8,2,128,128]{3,2,1,0:T(8,128)(2,1)}), bf16[8,2,128,128]{3,2,1,0:T(8,128)(2,1)S(1)}, u32[]{:S(2)}, u32[]{:S(2)}) async-start(bf16[8,2,128,128]{3,2,1,0:T(8,128)(2,1)} %shard_map.90), calls=%async_computation.2 | async-start | bytes 1048576 | tf_op jit(solution)/shard_map/all_to_all | solution.py:235
  82.8 2.5 %collective-permute-start.2 = (bf16[4,4,128,128]{3,2,1,0:T(8,128)(2,1)S(1)}, bf16[4,4,128,128]{3,2,1,0:T(8,128)(2,1)S(1)}, u32[]{:S(2)}, u32[]{:S(2)}) collective-permute-start(bf16[4,4,128,128]{3,2,1,0:T(8,128)(2,1)S(1)} %get-tuple-element.41), channel_id=1, source_target_pairs={{0,2},{1,15},{2,0},{3,5},{4,6},{5,3},{6,4},{7,9},{8,10},{9,7},{10,... | collective-permute-start | bytes 1572872 | tf_op jit(solution)/shard_map/ppermute | solution.py:300
  85.3 8.6 %collective-permute-done.2.b_ref = bf16[4,4,128,128]{3,2,1,0:T(8,128)(2,1)S(1)} collective-permute-done((bf16[4,4,128,128]{3,2,1,0:T(8,128)(2,1)S(1)}, bf16[4,4,128,128]{3,2,1,0:T(8,128)(2,1)S(1)}, u32[]{:S(2)}, u32[]{:S(2)}) %collective-permute-start.2) | collective-permute-done | bytes 524320 | tf_op jit(solution)/shard_map/ppermute | solution.py:300
  93.9 0.7 shard_map.91
  94.6 4.9 %all-to-all-done.2.in_ref = bf16[8,2,128,128]{3,2,1,0:T(8,128)(2,1)S(1)} async-done(((bf16[8,2,128,128]{3,2,1,0:T(8,128)(2,1)}), bf16[8,2,128,128]{3,2,1,0:T(8,128)(2,1)S(1)}, u32[]{:S(2)}, u32[]{:S(2)}) %all-to-all-start.2) | async-done | bytes 524320 | tf_op jit(solution)/shard_map/all_to_all | solution.py:235
  99.4 0.9 shard_map.92
  100.3 5.6 %all-to-all-start.3 = ((bf16[8,2,128,128]{3,2,1,0:T(8,128)(2,1)}), bf16[8,2,128,128]{3,2,1,0:T(8,128)(2,1)S(1)}, u32[]{:S(2)}, u32[]{:S(2)}) async-start(bf16[8,2,128,128]{3,2,1,0:T(8,128)(2,1)} %shard_map.92), calls=%async_computation.3 | async-start | bytes 1048576 | tf_op jit(solution)/shard_map/all_to_all | solution.py:235
  105.9 2.0 %collective-permute-start.3 = (bf16[2,4,128,128]{3,2,1,0:T(8,128)(2,1)S(1)}, bf16[2,4,128,128]{3,2,1,0:T(8,128)(2,1)S(1)}, u32[]{:S(2)}, u32[]{:S(2)}) collective-permute-start(bf16[2,4,128,128]{3,2,1,0:T(8,128)(2,1)S(1)} %get-tuple-element.46), channel_id=1, source_target_pairs={{0,4},{1,13},{2,6},{3,15},{4,0},{5,9},{6,2},{7,11},{8,12},{9,5},{1... | collective-permute-start | bytes 786440 | tf_op jit(solution)/shard_map/ppermute | solution.py:304
  107.9 10.0 %collective-permute-done.3.b_ref = bf16[2,4,128,128]{3,2,1,0:T(8,128)(2,1)S(1)} collective-permute-done((bf16[2,4,128,128]{3,2,1,0:T(8,128)(2,1)S(1)}, bf16[2,4,128,128]{3,2,1,0:T(8,128)(2,1)S(1)}, u32[]{:S(2)}, u32[]{:S(2)}) %collective-permute-start.3) | collective-permute-done | bytes 262176 | tf_op jit(solution)/shard_map/ppermute | solution.py:304
  117.9 0.6 shard_map.93
  118.5 3.7 %all-to-all-done.3.in_ref = bf16[8,2,128,128]{3,2,1,0:T(8,128)(2,1)S(1)} async-done(((bf16[8,2,128,128]{3,2,1,0:T(8,128)(2,1)}), bf16[8,2,128,128]{3,2,1,0:T(8,128)(2,1)S(1)}, u32[]{:S(2)}, u32[]{:S(2)}) %all-to-all-start.3) | async-done | bytes 524320 | tf_op jit(solution)/shard_map/all_to_all | solution.py:235
  122.2 1.6 %shard_map.95 = bf16[4,2,8,128,128]{4,3,2,1,0:T(8,128)(2,1)} custom-call(bf16[8,2,128,128]{3,2,1,0:T(8,128)(2,1)S(1)} %all-to-all-done.3.in_ref), custom_call_target="tpu_custom_call" | custom-call | bytes 3145728 | tf_op jit(solution)/shard_map/pallas_call | solution.py:223
  123.8 3.6 %all-to-all-start.4 = ((bf16[4,2,8,128,128]{4,3,2,1,0:T(8,128)(2,1)}), bf16[4,2,8,128,128]{4,3,2,1,0:T(8,128)(2,1)S(1)}, u32[]{:S(2)}, u32[]{:S(2)}) async-start(bf16[4,2,8,128,128]{4,3,2,1,0:T(8,128)(2,1)} %shard_map.95), calls=%async_computation.4 | async-start | bytes 4194304 | tf_op jit(solution)/shard_map/all_to_all | solution.py:235
  127.4 2.5 %collective-permute-start.4 = (bf16[1,4,128,128]{3,2,1,0:T(8,128)(2,1)S(1)}, bf16[1,4,128,128]{3,2,1,0:T(8,128)(2,1)S(1)}, u32[]{:S(2)}, u32[]{:S(2)}) collective-permute-start(bf16[1,4,128,128]{3,2,1,0:T(8,128)(2,1)S(1)} %get-tuple-element.50), channel_id=1, source_target_pairs={{0,8},{1,9},{2,10},{3,11},{4,12},{5,13},{6,14},{7,15},{8,0},{9,1},... | collective-permute-start | bytes 393224 | tf_op jit(solution)/shard_map/ppermute | solution.py:311
  129.9 11.6 %collective-permute-done.4.b_ref = bf16[1,4,128,128]{3,2,1,0:T(8,128)(2,1)S(1)} collective-permute-done((bf16[1,4,128,128]{3,2,1,0:T(8,128)(2,1)S(1)}, bf16[1,4,128,128]{3,2,1,0:T(8,128)(2,1)S(1)}, u32[]{:S(2)}, u32[]{:S(2)}) %collective-permute-start.4) | collective-permute-done | bytes 131104 | tf_op jit(solution)/shard_map/ppermute | solution.py:311
  141.5 0.8 shard_map.94
  142.2 0.0 all-to-all-done.4.in_ref
  142.2 1.5 %shard_map.96 = (bf16[32,128,128]{2,1,0:T(8,128)(2,1)}, bf16[32,128,128]{2,1,0:T(8,128)(2,1)}) custom-call(bf16[4,2,8,128,128]{4,3,2,1,0:T(8,128)(2,1)S(1)} %all-to-all-done.4.in_ref), custom_call_target="tpu_custom_call" | custom-call | bytes 4194304 | tf_op jit(solution)/shard_map/pallas_call | solution.py:223
  (3 shorter events, 0.0 us)
Async XLA Ops:
  0.6 42.8 %copy-start = (bf16[32,128,128]{2,1,0:T(8,128)(2,1)S(1)}, bf16[32,128,128]{2,1,0:T(8,128)(2,1)}, u32[]{:S(2)}) copy-start(bf16[32,128,128]{2,1,0:T(8,128)(2,1)} %down_ref.3) | copy-start | bytes 3145732
  0.6 42.8 %copy-start.1 = (bf16[32,128,128]{2,1,0:T(8,128)(2,1)S(1)}, bf16[32,128,128]{2,1,0:T(8,128)(2,1)}, u32[]{:S(2)}) copy-start(bf16[32,128,128]{2,1,0:T(8,128)(2,1)} %up_ref.3) | copy-start | bytes 3145732
  0.7 1.0 copy-start.6
  1.6 0.8 copy-start.7
  2.6 42.4 %copy-start.8 = (s32[8,32]{1,0:T(8,128)S(1)}, s32[8,32]{1,0:T(8,128)}, u32[]{:S(2)}) copy-start(s32[8,32]{1,0:T(8,128)} %mask_ref.1) | copy-start | bytes 3076
  41.5 5.3 %collective-permute-start = (bf16[8,4,128,128]{3,2,1,0:T(8,128)(2,1)S(1)}, bf16[8,4,128,128]{3,2,1,0:T(8,128)(2,1)}, u32[]{:S(2)}, u32[]{:S(2)}) collective-permute-start(bf16[8,4,128,128]{3,2,1,0:T(8,128)(2,1)S(1)} %all_to_all.25.own_ref), channel_id=1, source_target_pairs={{0,1},{1,0},{2,3},{3,2},{4,5},{5,4},{6,7},{7,6},{8,9},{9,8},{10,11... | collective-permute-start | bytes 3145736 | tf_op jit(solution)/shard_map/ppermute | solution.py:260
  44.0 1.0 copy-start.2
  52.1 0.7 copy-start.4
  52.8 18.9 %all-to-all-start.1 = ((bf16[4,2,8,128,128]{4,3,2,1,0:T(8,128)(2,1)}), bf16[4,2,8,128,128]{4,3,2,1,0:T(8,128)(2,1)S(1)}, u32[]{:S(2)}, u32[]{:S(2)}) async-start(bf16[4,2,8,128,128]{4,3,2,1,0:T(8,128)(2,1)} %get-tuple-element.31), calls=%async_computation.1 | async-start | bytes 4194304 | tf_op jit(solution)/shard_map/all_to_all | solution.py:235
  57.2 1.2 copy-start.3
  58.4 0.9 copy-start.5
  61.1 7.0 %collective-permute-start.1 = (bf16[8,4,128,128]{3,2,1,0:T(8,128)(2,1)S(1)}, bf16[8,4,128,128]{3,2,1,0:T(8,128)(2,1)S(1)}, u32[]{:S(2)}, u32[]{:S(2)}) collective-permute-start(bf16[8,4,128,128]{3,2,1,0:T(8,128)(2,1)S(1)} %get-tuple-element.36), channel_id=1, source_target_pairs={{0,1},{1,0},{2,3},{3,2},{4,5},{5,4},{6,7},{7,6},{8,9},{9,8},{10,11... | collective-permute-start | bytes 3145736 | tf_op jit(solution)/shard_map/ppermute | solution.py:284
  72.8 26.7 %all-to-all-start.2 = ((bf16[8,2,128,128]{3,2,1,0:T(8,128)(2,1)}), bf16[8,2,128,128]{3,2,1,0:T(8,128)(2,1)S(1)}, u32[]{:S(2)}, u32[]{:S(2)}) async-start(bf16[8,2,128,128]{3,2,1,0:T(8,128)(2,1)} %shard_map.90), calls=%async_computation.2 | async-start | bytes 1048576 | tf_op jit(solution)/shard_map/all_to_all | solution.py:235
  82.8 11.1 %collective-permute-start.2 = (bf16[4,4,128,128]{3,2,1,0:T(8,128)(2,1)S(1)}, bf16[4,4,128,128]{3,2,1,0:T(8,128)(2,1)S(1)}, u32[]{:S(2)}, u32[]{:S(2)}) collective-permute-start(bf16[4,4,128,128]{3,2,1,0:T(8,128)(2,1)S(1)} %get-tuple-element.41), channel_id=1, source_target_pairs={{0,2},{1,15},{2,0},{3,5},{4,6},{5,3},{6,4},{7,9},{8,10},{9,7},{10,... | collective-permute-start | bytes 1572872 | tf_op jit(solution)/shard_map/ppermute | solution.py:300
  100.3 21.9 %all-to-all-start.3 = ((bf16[8,2,128,128]{3,2,1,0:T(8,128)(2,1)}), bf16[8,2,128,128]{3,2,1,0:T(8,128)(2,1)S(1)}, u32[]{:S(2)}, u32[]{:S(2)}) async-start(bf16[8,2,128,128]{3,2,1,0:T(8,128)(2,1)} %shard_map.92), calls=%async_computation.3 | async-start | bytes 1048576 | tf_op jit(solution)/shard_map/all_to_all | solution.py:235
  105.9 12.0 %collective-permute-start.3 = (bf16[2,4,128,128]{3,2,1,0:T(8,128)(2,1)S(1)}, bf16[2,4,128,128]{3,2,1,0:T(8,128)(2,1)S(1)}, u32[]{:S(2)}, u32[]{:S(2)}) collective-permute-start(bf16[2,4,128,128]{3,2,1,0:T(8,128)(2,1)S(1)} %get-tuple-element.46), channel_id=1, source_target_pairs={{0,4},{1,13},{2,6},{3,15},{4,0},{5,9},{6,2},{7,11},{8,12},{9,5},{1... | collective-permute-start | bytes 786440 | tf_op jit(solution)/shard_map/ppermute | solution.py:304
  123.8 18.4 %all-to-all-start.4 = ((bf16[4,2,8,128,128]{4,3,2,1,0:T(8,128)(2,1)}), bf16[4,2,8,128,128]{4,3,2,1,0:T(8,128)(2,1)S(1)}, u32[]{:S(2)}, u32[]{:S(2)}) async-start(bf16[4,2,8,128,128]{4,3,2,1,0:T(8,128)(2,1)} %shard_map.95), calls=%async_computation.4 | async-start | bytes 4194304 | tf_op jit(solution)/shard_map/all_to_all | solution.py:235
  127.4 14.0 %collective-permute-start.4 = (bf16[1,4,128,128]{3,2,1,0:T(8,128)(2,1)S(1)}, bf16[1,4,128,128]{3,2,1,0:T(8,128)(2,1)S(1)}, u32[]{:S(2)}, u32[]{:S(2)}) collective-permute-start(bf16[1,4,128,128]{3,2,1,0:T(8,128)(2,1)S(1)} %get-tuple-element.50), channel_id=1, source_target_pairs={{0,8},{1,9},{2,10},{3,11},{4,12},{5,13},{6,14},{7,15},{8,0},{9,1},... | collective-permute-start | bytes 393224 | tf_op jit(solution)/shard_map/ppermute | solution.py:311

commit v4 on v3

--- a/solution.py
+++ b/solution.py
@@ -30,7 +30,7 @@
     for j in range(2)
     for i in range(2)
 ]
-Z_GROUPS = [[2 * z + c for z in range(NZ)] for c in range(2)]
+Z_GROUPS = [[2 * (2 * half + odd) + c for half in range(NZ // 2)] for odd in range(2) for c in range(2)]
 CORE_SWAP = [(i, i ^ 1) for i in range(2 * NZ)]
 
 
@@ -63,13 +63,21 @@
     return lax.dot_general(a, b, (((1,), (1,)), ((), ())), preferred_element_type=F32)
 
 
-def prep_kernel(tok_ref, cot_ref, out_ref):
+def prep_kernel(tok_hbm, cot_hbm, out_ref, tok_ref, cot_ref, sems):
+    copies = [
+        pltpu.make_async_copy(tok_hbm, tok_ref, sems.at[0]),
+        pltpu.make_async_copy(cot_hbm, cot_ref, sems.at[1]),
+    ]
+    for copy in copies:
+        copy.start()
+    for copy in copies:
+        copy.wait()
     for j in range(2):
         tok_t = tok_ref[:, j * BLK : (j + 1) * BLK].T
         cot = cot_ref[:, j * BLK : (j + 1) * BLK]
-        for z in range(NZ):
-            out_ref[z, j] = tok_t
-            out_ref[z, 2 + j] = cot
+        for half in range(NZ // 2):
+            out_ref[half, j] = tok_t
+            out_ref[half, 2 + j] = cot
 
 
 def table_kernel(mask_ref, out_ref, cells):
@@ -89,60 +97,94 @@
         last_row = row
 
 
-def weights_kernel(up_ref, down_ref, up_t_ref, down_t_ref):
-    for s in range(SLOTS):
-        up_t_ref[s] = up_ref[s].T
-        down_t_ref[s] = down_ref[s].T
-
-
-def first_kernel(
-    table_ref, place_ref, own_ref, other_ref, up_t_ref, down_ref, grads_ref, act_ref, pre_ref, panels, hid, dac
-):
+def load_tiles(sources, goals, sems):
+    copies = [
+        [
+            pltpu.make_async_copy(source.at[pl.ds(8 * q, 8)], goal.at[pl.ds(8 * q, 8)], sems.at[q, n])
+            for n, (source, goal) in enumerate(zip(sources, goals))
+        ]
+        for q in range(SLOTS // 8)
+    ]
+    for group in copies:
+        for copy in group:
+            copy.start()
+    return copies
+
+
+def wait_tiles(copies, q):
+    for copy in copies[q]:
+        copy.wait()
+
+
+def first_kernel(table_ref, place_ref, *refs):
+    panel_refs, (up_hbm, down_hbm, grads_hbm, acts_hbm) = refs[:4], refs[4:8]
+    panels, hid, dac, grads, acts, up_ref, down_ref, sems, tile_sems = refs[8:]
+    loads = load_tiles((up_hbm, down_hbm), (up_ref, down_ref), tile_sems)
     core = place_ref[0]
-    panels[0] = own_ref[...]
-    panels[1] = other_ref[...]
+    odd = place_ref[1] & 1
+    for side in range(2):
+        for other in range(2):
+            panels[side, other] = panel_refs[2 * side + other][...]
 
     def place(s):
         col = table_ref[s]
-        return ((col >> 1) & 1) ^ core, col >> 2, col & 1
+        return ((col >> 1) & 1) ^ core, ((col >> 2) & 1) ^ odd, col >> 3, col & 1
 
     hid_sum = jnp.zeros((BLK, BLK), F32)
     dac_sum = jnp.zeros((BLK, BLK), F32)
     for s in range(SLOTS):
-        side, z, j = place(s)
+        if s % 8 == 0:
+            wait_tiles(loads, s // 8)
+        side, other, half, j = place(s)
         row = table_ref[SLOTS + s]
         fresh = table_ref[2 * SLOTS + s] == 1
         used = table_ref[3 * SLOTS + s] == 1
-        hid_part = nn(up_t_ref[s], panels[side, z, j])
-        dac_part = nt(down_ref[s], panels[side, z, 2 + j])
+        hid_part = nn(up_ref[s].T, panels[side, other, half, j])
+        dac_part = nt(down_ref[s], panels[side, other, half, 2 + j])
         hid_sum = jnp.where(fresh, 0.0, hid_sum) + jnp.where(used, hid_part, 0.0)
         dac_sum = jnp.where(fresh, 0.0, dac_sum) + jnp.where(used, dac_part, 0.0)
         hid[row] = hid_sum
         dac[row] = dac_sum
     for r in range(ROWS):
         act, pre = gelu_pair(hid[r], dac[r])
-        act_ref[r] = act
-        pre_ref[r] = pre
+        acts[0, r] = act
+        acts[1, r] = pre
+    copies = [pltpu.make_async_copy(acts, acts_hbm, sems.at[4])]
+    copies[0].start()
     for s in range(SLOTS):
-        side, z, j = place(s)
+        side, other, half, j = place(s)
         row = table_ref[SLOTS + s]
         used = table_ref[3 * SLOTS + s] == 1
-        up_part = nt(panels[side, z, j], pre_ref[row])
-        down_part = nn(act_ref[row], panels[side, z, 2 + j])
-        grads_ref[s // 8, 0, s % 8] = jnp.where(used, up_part, 0.0).astype(BF)
-        grads_ref[s // 8, 1, s % 8] = jnp.where(used, down_part, 0.0).astype(BF)
-
-
-def second_kernel(table_ref, place_ref, act_ref, pre_ref, down_t_ref, up_ref, own_ref, send_ref, out_sum, grad_sum):
+        up_part = nt(panels[side, other, half, j], acts[1, row])
+        down_part = nn(acts[0, row], panels[side, other, half, 2 + j])
+        grads[s // 8, 0, s % 8] = jnp.where(used, up_part, 0.0).astype(BF)
+        grads[s // 8, 1, s % 8] = jnp.where(used, down_part, 0.0).astype(BF)
+        if s % 8 == 7:
+            copies.append(pltpu.make_async_copy(grads.at[s // 8], grads_hbm.at[s // 8], sems.at[s // 8]))
+            copies[-1].start()
+    for copy in copies:
+        copy.wait()
+
+
+def second_kernel(
+    table_ref, place_ref, acts_hbm, up_hbm, down_hbm, own_ref, send_ref, *scratch
+):
+    out_sum, grad_sum, acts_ref, up_ref, down_ref, sem, tile_sems = scratch
     core = place_ref[0]
+    copy = pltpu.make_async_copy(acts_hbm, acts_ref, sem)
+    copy.start()
+    loads = load_tiles((up_hbm, down_hbm), (up_ref, down_ref), tile_sems)
     out_sum[...] = jnp.zeros_like(out_sum)
     grad_sum[...] = jnp.zeros_like(grad_sum)
+    copy.wait()
     for s in range(SLOTS):
+        if s % 8 == 0:
+            wait_tiles(loads, s // 8)
         col = table_ref[s]
         row = table_ref[SLOTS + s]
         used = table_ref[3 * SLOTS + s] == 1
-        out_part = nn(down_t_ref[s], act_ref[row])
-        grad_part = nn(up_ref[s], pre_ref[row])
+        out_part = nn(down_ref[s].T, acts_ref[0, row])
+        grad_part = nn(up_ref[s], acts_ref[1, row])
         out_sum[col] += jnp.where(used, out_part, 0.0)
         grad_sum[col] += jnp.where(used, grad_part, 0.0)
     for z in range(NZ):
@@ -183,18 +225,26 @@
             out_ref[y, k] = total
 
 
-def spread_kernel(in_ref, out_ref):
-    for y in range(NY):
-        for k in range(2):
-            tile = in_ref[y, k]
-            for x in range(NX):
-                out_ref[x, k, y] = tile
-
-
-def split_kernel(in_ref, up_ref, down_ref):
-    for x in range(NX):
-        up_ref[x * 8 : (x + 1) * 8] = in_ref[x, 0]
-        down_ref[x * 8 : (x + 1) * 8] = in_ref[x, 1]
+def spread_kernel(in_ref, out_hbm, sems):
+    copies = [
+        pltpu.make_async_copy(in_ref.at[:, k], out_hbm.at[x, k], sems.at[x, k]) for x in range(NX) for k in range(2)
+    ]
+    for copy in copies:
+        copy.start()
+    for copy in copies:
+        copy.wait()
+
+
+def split_kernel(in_ref, up_hbm, down_hbm, sems):
+    copies = [
+        pltpu.make_async_copy(in_ref.at[x, k], goal.at[pl.ds(x * 8, 8)], sems.at[x, k])
+        for x in range(NX)
+        for k, goal in enumerate((up_hbm, down_hbm))
+    ]
+    for copy in copies:
+        copy.start()
+    for copy in copies:
+        copy.wait()
 
 
 def final_kernel(a_ref, b_ref, out_ref, grad_ref):
@@ -204,26 +254,19 @@
         goal[:, (j % 2) * BLK : (j % 2 + 1) * BLK] = total.T.astype(BF)
 
 
-def whole(count):
-    return [pl.BlockSpec(memory_space=pltpu.VMEM)] * count
-
-
-def smem(count):
-    return [pl.BlockSpec(memory_space=pltpu.SMEM)] * count
-
-
 def shape(*dims, dtype=BF):
     return jax.ShapeDtypeStruct(dims, dtype)
 
 
-def call(kernel, outs, operands, n_smem=0, scratch=(), flops=0, moved=0, out_smem=False):
+def call(kernel, outs, operands, scratch=(), flops=0, moved=0, ins=None, results=None):
     many = isinstance(outs, (list, tuple))
-    n_out = len(outs) if many else 1
-    out_specs = smem(n_out) if out_smem else whole(n_out)
+    ins = ins or [pltpu.VMEM] * len(operands)
+    results = results or [pltpu.VMEM] * (len(outs) if many else 1)
+    out_specs = [pl.BlockSpec(memory_space=space) for space in results]
     return pl.pallas_call(
         kernel,
         out_shape=outs,
-        in_specs=smem(n_smem) + whole(len(operands) - n_smem),
+        in_specs=[pl.BlockSpec(memory_space=space) for space in ins],
         out_specs=out_specs if many else out_specs[0],
         scratch_shapes=list(scratch),
         compiler_params=VM,
@@ -239,45 +282,66 @@
     mib = 1 << 20
     position = lax.axis_index("mp")
     place = jnp.stack([position & 1, position >> 1]).astype(jnp.int32)
-    sent = call(prep_kernel, shape(NZ, 4, BLK, BLK), (tokens, cotangent), moved=mib)
-    own_panels = exchange(sent, "mp", Z_GROUPS)
+    tokens, cotangent, up_tiles, down_tiles = (
+        pltpu.with_memory_space_constraint(x, pltpu.HBM) for x in (tokens, cotangent, up_tiles, down_tiles)
+    )
+    sent = call(
+        prep_kernel,
+        shape(NZ // 2, 4, BLK, BLK),
+        (tokens, cotangent),
+        scratch=[pltpu.VMEM((BLK, 2 * BLK), BF), pltpu.VMEM((BLK, 2 * BLK), BF), pltpu.SemaphoreType.DMA((2,))],
+        ins=[pltpu.HBM] * 2,
+        moved=mib,
+    )
     table = call(
         table_kernel,
         shape(4 * SLOTS, dtype=jnp.int32),
         (block_mask,),
-        n_smem=1,
         scratch=[pltpu.SMEM((ROWS * COLS + 8,), jnp.int32)],
-        out_smem=True,
+        ins=[pltpu.SMEM],
+        results=[pltpu.SMEM],
         flops=mib,
         moved=1024,
     )
-    up_t, down_t = call(
-        weights_kernel,
-        [shape(SLOTS, BLK, BLK), shape(SLOTS, BLK, BLK)],
-        (up_tiles, down_tiles),
-        moved=4 * mib,
-    )
-    other_panels = lax.ppermute(own_panels, "mp", CORE_SWAP)
+    same = exchange(sent, "mp", Z_GROUPS)
+    other = lax.ppermute(same, "mp", z_swap(0))
+    other, table = lax.optimization_barrier((other, table))
+    panels = (same, other, lax.ppermute(same, "mp", CORE_SWAP), lax.ppermute(other, "mp", CORE_SWAP))
     product = 2 * SLOTS * BLK * BLK * BLK
-    grads, act, pre = call(
+    grads, acts = call(
         first_kernel,
-        [shape(NX, 2, 8, BLK, BLK), shape(ROWS, BLK, BLK), shape(ROWS, BLK, BLK)],
-        (table, place, own_panels, other_panels, up_t, down_tiles),
-        n_smem=2,
+        [pltpu.HBM((4, 2, 8, BLK, BLK), BF), pltpu.HBM((2, ROWS, BLK, BLK), BF)],
+        (table, place) + panels + (up_tiles, down_tiles),
         scratch=[
-            pltpu.VMEM((2, NZ, 4, BLK, BLK), BF),
+            pltpu.VMEM((2, 2, NZ // 2, 4, BLK, BLK), BF),
             pltpu.VMEM((ROWS, BLK, BLK), F32),
             pltpu.VMEM((ROWS, BLK, BLK), F32),
+            pltpu.VMEM((4, 2, 8, BLK, BLK), BF),
+            pltpu.VMEM((2, ROWS, BLK, BLK), BF),
+            pltpu.VMEM((SLOTS, BLK, BLK), BF),
+            pltpu.VMEM((SLOTS, BLK, BLK), BF),
+            pltpu.SemaphoreType.DMA((5,)),
+            pltpu.SemaphoreType.DMA((4, 2)),
         ],
+        ins=[pltpu.SMEM] * 2 + [pltpu.VMEM] * 4 + [pltpu.HBM] * 2,
+        results=[pltpu.HBM] * 2,
         flops=4 * product,
         moved=6 * mib,
     )
     own_part, other_part = call(
         second_kernel,
         [shape(NZ, 4, BLK, BLK), shape(NZ, 4, BLK, BLK)],
-        (table, place, act, pre, down_t, up_tiles),
-        n_smem=2,
-        scratch=[pltpu.VMEM((COLS, BLK, BLK), F32), pltpu.VMEM((COLS, BLK, BLK), F32)],
+        (table, place, acts, up_tiles, down_tiles),
+        scratch=[
+            pltpu.VMEM((COLS, BLK, BLK), F32),
+            pltpu.VMEM((COLS, BLK, BLK), F32),
+            pltpu.VMEM((2, ROWS, BLK, BLK), BF),
+            pltpu.VMEM((SLOTS, BLK, BLK), BF),
+            pltpu.VMEM((SLOTS, BLK, BLK), BF),
+            pltpu.SemaphoreType.DMA,
+            pltpu.SemaphoreType.DMA((4, 2)),
+        ],
+        ins=[pltpu.SMEM] * 2 + [pltpu.HBM] * 3,
         flops=2 * product,
         moved=5 * mib,
     )
@@ -289,7 +353,7 @@
             functools.partial(halve_kernel, level),
             [shape(count, 4, BLK, BLK)] * 2,
             (place, a, b),
-            n_smem=1,
+            ins=[pltpu.SMEM] + [pltpu.VMEM] * 2,
             moved=count * mib // 2,
         )
 
@@ -304,7 +368,10 @@
     keep, send = halve(2, keep, lax.ppermute(send, "mp", z_swap(1)))
     all_y = exchange(y_done, ("dp", "mp"), FAR_GROUPS)
     all_y, keep, send = lax.optimization_barrier((all_y, keep, send))
-    spread = call(spread_kernel, shape(NX, 2, NY, BLK, BLK), (all_y,), moved=3 * mib)
+    eight = [pltpu.SemaphoreType.DMA((NX, 2))]
+    spread = call(
+        spread_kernel, shape(NX, 2, NY, BLK, BLK), (all_y,), scratch=eight, results=[pltpu.HBM], moved=3 * mib
+    )
     output, grad_tokens = call(
         final_kernel,
         [shape(BLK, 2 * BLK), shape(BLK, 2 * BLK)],
@@ -313,7 +380,12 @@
     )
     all_x = exchange(spread, ("dp", "mp"), NEAR_GROUPS)
     grad_up, grad_down = call(
-        split_kernel, [shape(SLOTS, BLK, BLK), shape(SLOTS, BLK, BLK)], (all_x,), moved=4 * mib
+        split_kernel,
+        [shape(SLOTS, BLK, BLK), shape(SLOTS, BLK, BLK)],
+        (all_x,),
+        scratch=eight,
+        results=[pltpu.HBM] * 2,
+        moved=4 * mib,
     )
     return output, grad_tokens, grad_up, grad_down
 

time: 146 us -> 142 us (0.973)
  blocking collectives: 38.8 us -> 27.1 us
  waiting for transfers between devices: 43.7 us -> 49.5 us
  starting transfers between devices: 37.3 us -> 42.5 us
  local copies, waits for them, and re-layouts: 5.67 us -> 0.69 us
  Pallas kernels: 17.3 us -> 19.1 us
    all_to_all x1, blocking collectives: 38.8 us -> 27.1 us  [exchange(): return lax.all_to_all(x, axis, 0, 0, tiled=True, axis_index_groups=groups)]
    ppermute x1 -> x3, waiting for transfers between devices: 0.01 us -> 5.6 us  [the longest x1 3.81 us: body(): other = lax.ppermute(same, 'mp', z_swap(0))]
    unnamed x18 -> x4, local copies, waits for them, and re-layouts: 5.67 us -> 0.69 us
    ppermute x1 -> x3, starting transfers between devices: 1.91 us -> 6.8 us  [the longest x1 2.97 us: body(): other = lax.ppermute(same, 'mp', z_swap(0))]
    pallas_call x13 -> x12, Pallas kernels: 17.3 us -> 19.1 us  [call(): pl.pallas_call(kernel, out_shape=outs, in_specs=[pl.BlockSpec(memory_spac...]
  transfers between devices with their start and end apart: 9 -> 11, of which waited for: 7 -> 9; matrix products, arithmetic and copies ran while one was open for 0% -> 0% of each run, Pallas kernels for 5% -> 5%
where the time goes in v4:
time: 142 us; the launch traced here: 140 us
  waiting for transfers between devices  49.5 us (35%)
  starting transfers between devices  42.5 us (30%)
  blocking collectives  27.1 us (19%)
  Pallas kernels  19.1 us (13%)
    all_to_all x1, blocking collectives, exchange(): return lax.all_to_all(x, axis, 0, 0, tiled=True, axis_index_groups=groups)  27.1 us
    all_to_all x4, starting transfers between devices, exchange(): return lax.all_to_all(x, axis, 0, 0, tiled=True, axis_index_groups=groups)  23.9 us
    pallas_call x12, Pallas kernels, call(): pl.pallas_call(kernel, out_shape=outs, in_specs=[pl.BlockSpec(memory_spac...  19.1 us
    all_to_all x4, waiting for transfers between devices, exchange(): return lax.all_to_all(x, axis, 0, 0, tiled=True, axis_index_groups=groups)  11.8 us
    ppermute x1, waiting for transfers between devices, body(): lax.ppermute(send, 'mp', z_swap(2))  11.6 us
    ppermute x1, waiting for transfers between devices, body(): keep, send = halve(2, keep, lax.ppermute(send, 'mp', z_swap(1)))  10 us
    ppermute x1, waiting for transfers between devices, body(): keep, send = halve(1, keep, lax.ppermute(send, 'mp', z_swap(0)))  8.09 us
    ppermute x1, starting transfers between devices, body(): from_other = lax.ppermute(other_part, 'mp', CORE_SWAP)  4.4 us
  transfers between devices with their start and end apart: 11, of which 9 were waited for; matrix products, arithmetic and copies ran while one was open for 0% of the time, Pallas kernels for 5%

profile of v4, /device:TPU:6, one launch (start us, length us, event | category | flops | bytes accessed | tf_op | source)
XLA Modules:
  0.0 139.7 jit_solution(15988604143714734959)
XLA Ops:
  0.6 1.0 shard_map.84
  1.6 27.1 %all_to_all.25.refs_0_ = bf16[4,4,128,128]{3,2,1,0:T(8,128)(2,1)S(1)} all-to-all(bf16[4,4,128,128]{3,2,1,0:T(8,128)(2,1)S(1)} %shard_map.84), channel_id=1, replica_groups={{0,4,8,12},{1,5,9,13},{2,6,10,14},{3,7,11,15},{16,20,24,28},{17,21,25,2..., dimensions={0} | all-to-all | bytes 1048576 | tf_op jit(solution)/shard_map/all_to_all | solution.py:278
  28.7 3.0 %collective-permute-start = (bf16[4,4,128,128]{3,2,1,0:T(8,128)(2,1)S(1)}, bf16[4,4,128,128]{3,2,1,0:T(8,128)(2,1)S(1)}, u32[]{:S(2)}, u32[]{:S(2)}) collective-permute-start(bf16[4,4,128,128]{3,2,1,0:T(8,128)(2,1)S(1)} %all_to_all.25.refs_0_), channel_id=1, source_target_pairs={{0,2},{1,15},{2,0},{3,5},{4,6},{5,3},{6,4},{7,9},{8,10},{9,7},{10,... | collective-permute-start | bytes 1572872 | tf_op jit(solution)/shard_map/ppermute | solution.py:307
  31.7 0.0 copy-start.1
  31.7 0.7 copy-done.1
  32.4 1.6 %shard_map.85.table_ref = s32[128]{0:T(128)S(1)} custom-call(s32[8,32]{1,0:T(8,128)S(1)} %copy-done.1), custom_call_target="tpu_custom_call" | custom-call | flops 1048576 | bytes 1024 | tf_op jit(solution)/shard_map/pallas_call | solution.py:266
  34.0 1.9 %collective-permute-start.1 = (bf16[4,4,128,128]{3,2,1,0:T(8,128)(2,1)S(1)}, bf16[4,4,128,128]{3,2,1,0:T(8,128)(2,1)S(1)}, u32[]{:S(2)}, u32[]{:S(2)}) collective-permute-start(bf16[4,4,128,128]{3,2,1,0:T(8,128)(2,1)S(1)} %all_to_all.25.refs_0_), channel_id=1, source_target_pairs={{0,1},{1,0},{2,3},{3,2},{4,5},{5,4},{6,7},{7,6},{8,9},{9,8},{10,11... | collective-permute-start | bytes 1572872 | tf_op jit(solution)/shard_map/ppermute | solution.py:309
  36.0 3.8 %collective-permute-done.refs_1_ = bf16[4,4,128,128]{3,2,1,0:T(8,128)(2,1)S(1)} collective-permute-done((bf16[4,4,128,128]{3,2,1,0:T(8,128)(2,1)S(1)}, bf16[4,4,128,128]{3,2,1,0:T(8,128)(2,1)S(1)}, u32[]{:S(2)}, u32[]{:S(2)}) %collective-permute-start) | collective-permute-done | bytes 524320 | tf_op jit(solution)/shard_map/ppermute | solution.py:307
  39.8 1.9 %collective-permute-start.2 = (bf16[4,4,128,128]{3,2,1,0:T(8,128)(2,1)S(1)}, bf16[4,4,128,128]{3,2,1,0:T(8,128)(2,1)S(1)}, u32[]{:S(2)}, u32[]{:S(2)}) collective-permute-start(bf16[4,4,128,128]{3,2,1,0:T(8,128)(2,1)S(1)} %collective-permute-done.refs_1_), channel_id=1, source_target_pairs={{0,1},{1,0},{2,3},{3,2},{4,5},{5,4},{6,7},{7,6},{8,9},{9,8},{10,11... | collective-permute-start | bytes 1572872 | tf_op jit(solution)/shard_map/ppermute | solution.py:309
  41.7 0.1 pad_add_fusion.place_ref
  41.8 0.0 collective-permute-done.1.refs_2_
  41.8 1.8 %collective-permute-done.2.refs_3_ = bf16[4,4,128,128]{3,2,1,0:T(8,128)(2,1)S(1)} collective-permute-done((bf16[4,4,128,128]{3,2,1,0:T(8,128)(2,1)S(1)}, bf16[4,4,128,128]{3,2,1,0:T(8,128)(2,1)S(1)}, u32[]{:S(2)}, u32[]{:S(2)}) %collective-permute-start.2) | collective-permute-done | bytes 524320 | tf_op jit(solution)/shard_map/ppermute | solution.py:309
  43.6 5.8 %shard_map.86 = (bf16[4,2,8,128,128]{4,3,2,1,0:T(8,128)(2,1)}, bf16[2,8,128,128]{3,2,1,0:T(8,128)(2,1)}) custom-call(s32[128]{0:T(128)S(1)} %shard_map.85.table_ref, s32[2]{0:T(128)S(1)} %pad_add_fusion.place_ref, bf16[4,4,128,128]{3,2,1,0:T(8,128)(2,1)S(1)} %all_to_all.25.refs_0_, bf16[4,4,128,128]{3,2,1,0:T(8,128)(2,1)S(1)} %collective-permute-done.refs_1_, ...), custom_call_target="tpu_custom_call" | custom-call | flops 536870912 | bytes 6291456 | tf_op jit(solution)/shard_map/pallas_call | solution.py:266
  49.4 0.0 copy-start
  49.4 4.5 %all-to-all-start.1 = ((bf16[4,2,8,128,128]{4,3,2,1,0:T(8,128)(2,1)}), bf16[4,2,8,128,128]{4,3,2,1,0:T(8,128)(2,1)S(1)}, u32[]{:S(2)}, u32[]{:S(2)}) async-start(bf16[4,2,8,128,128]{4,3,2,1,0:T(8,128)(2,1)} %get-tuple-element.31), calls=%async_computation.1 | async-start | bytes 4194304 | tf_op jit(solution)/shard_map/all_to_all | solution.py:278
  54.0 0.0 copy-done
  54.0 3.2 %shard_map.87 = (bf16[8,4,128,128]{3,2,1,0:T(8,128)(2,1)S(1)}, bf16[8,4,128,128]{3,2,1,0:T(8,128)(2,1)S(1)}) custom-call(s32[128]{0:T(128)S(1)} %shard_map.85.table_ref, s32[2]{0:T(128)S(1)} %pad_add_fusion.place_ref, bf16[2,8,128,128]{3,2,1,0:T(8,128)(2,1)S(1)} %copy-done, bf16[32,128,128]{2,1,0:T(8,128)(2,1)} %up_hbm.1, bf16[32,128,128]{2,1,0:T(8,128)(2,1)} %down_hbm.1), custom_call_target="tpu_custom_call" | custom-call | flops 268435456 | bytes 5242880 | tf_op jit(solution)/shard_map/pallas_call | solution.py:266
  57.1 4.4 %collective-permute-start.3 = (bf16[8,4,128,128]{3,2,1,0:T(8,128)(2,1)S(1)}, bf16[8,4,128,128]{3,2,1,0:T(8,128)(2,1)S(1)}, u32[]{:S(2)}, u32[]{:S(2)}) collective-permute-start(bf16[8,4,128,128]{3,2,1,0:T(8,128)(2,1)S(1)} %get-tuple-element.34), channel_id=1, source_target_pairs={{0,1},{1,0},{2,3},{3,2},{4,5},{5,4},{6,7},{7,6},{8,9},{9,8},{10,11... | collective-permute-start | bytes 3145736 | tf_op jit(solution)/shard_map/ppermute | solution.py:348
  61.6 2.3 %collective-permute-done.3.b_ref = bf16[8,4,128,128]{3,2,1,0:T(8,128)(2,1)S(1)} collective-permute-done((bf16[8,4,128,128]{3,2,1,0:T(8,128)(2,1)S(1)}, bf16[8,4,128,128]{3,2,1,0:T(8,128)(2,1)S(1)}, u32[]{:S(2)}, u32[]{:S(2)}) %collective-permute-start.3) | collective-permute-done | bytes 1048608 | tf_op jit(solution)/shard_map/ppermute | solution.py:348
  63.8 0.8 shard_map.88
  64.6 3.9 %all-to-all-done.1.in_ref = bf16[4,2,8,128,128]{4,3,2,1,0:T(8,128)(2,1)S(1)} async-done(((bf16[4,2,8,128,128]{4,3,2,1,0:T(8,128)(2,1)}), bf16[4,2,8,128,128]{4,3,2,1,0:T(8,128)(2,1)S(1)}, u32[]{:S(2)}, u32[]{:S(2)}) %all-to-all-start.1) | async-done | bytes 2097184 | tf_op jit(solution)/shard_map/all_to_all | solution.py:278
  68.5 1.0 shard_map.89
  69.5 10.1 %all-to-all-start.2 = ((bf16[8,2,128,128]{3,2,1,0:T(8,128)(2,1)}), bf16[8,2,128,128]{3,2,1,0:T(8,128)(2,1)S(1)}, u32[]{:S(2)}, u32[]{:S(2)}) async-start(bf16[8,2,128,128]{3,2,1,0:T(8,128)(2,1)} %shard_map.89), calls=%async_computation.2 | async-start | bytes 1048576 | tf_op jit(solution)/shard_map/all_to_all | solution.py:278
  79.6 3.0 %collective-permute-start.4 = (bf16[4,4,128,128]{3,2,1,0:T(8,128)(2,1)S(1)}, bf16[4,4,128,128]{3,2,1,0:T(8,128)(2,1)S(1)}, u32[]{:S(2)}, u32[]{:S(2)}) collective-permute-start(bf16[4,4,128,128]{3,2,1,0:T(8,128)(2,1)S(1)} %get-tuple-element.39), channel_id=1, source_target_pairs={{0,2},{1,15},{2,0},{3,5},{4,6},{5,3},{6,4},{7,9},{8,10},{9,7},{10,... | collective-permute-start | bytes 1572872 | tf_op jit(solution)/shard_map/ppermute | solution.py:364
  82.6 8.1 %collective-permute-done.4.b_ref = bf16[4,4,128,128]{3,2,1,0:T(8,128)(2,1)S(1)} collective-permute-done((bf16[4,4,128,128]{3,2,1,0:T(8,128)(2,1)S(1)}, bf16[4,4,128,128]{3,2,1,0:T(8,128)(2,1)S(1)}, u32[]{:S(2)}, u32[]{:S(2)}) %collective-permute-start.4) | collective-permute-done | bytes 524320 | tf_op jit(solution)/shard_map/ppermute | solution.py:364
  90.6 0.7 shard_map.90
  91.3 4.5 %all-to-all-done.2.in_ref = bf16[8,2,128,128]{3,2,1,0:T(8,128)(2,1)S(1)} async-done(((bf16[8,2,128,128]{3,2,1,0:T(8,128)(2,1)}), bf16[8,2,128,128]{3,2,1,0:T(8,128)(2,1)S(1)}, u32[]{:S(2)}, u32[]{:S(2)}) %all-to-all-start.2) | async-done | bytes 524320 | tf_op jit(solution)/shard_map/all_to_all | solution.py:278
  95.8 0.9 shard_map.91
  96.7 5.7 %all-to-all-start.3 = ((bf16[8,2,128,128]{3,2,1,0:T(8,128)(2,1)}), bf16[8,2,128,128]{3,2,1,0:T(8,128)(2,1)S(1)}, u32[]{:S(2)}, u32[]{:S(2)}) async-start(bf16[8,2,128,128]{3,2,1,0:T(8,128)(2,1)} %shard_map.91), calls=%async_computation.3 | async-start | bytes 1048576 | tf_op jit(solution)/shard_map/all_to_all | solution.py:278
  102.4 1.9 %collective-permute-start.5 = (bf16[2,4,128,128]{3,2,1,0:T(8,128)(2,1)S(1)}, bf16[2,4,128,128]{3,2,1,0:T(8,128)(2,1)S(1)}, u32[]{:S(2)}, u32[]{:S(2)}) collective-permute-start(bf16[2,4,128,128]{3,2,1,0:T(8,128)(2,1)S(1)} %get-tuple-element.44), channel_id=1, source_target_pairs={{0,4},{1,13},{2,6},{3,15},{4,0},{5,9},{6,2},{7,11},{8,12},{9,5},{1... | collective-permute-start | bytes 786440 | tf_op jit(solution)/shard_map/ppermute | solution.py:368
  104.3 10.0 %collective-permute-done.5.b_ref = bf16[2,4,128,128]{3,2,1,0:T(8,128)(2,1)S(1)} collective-permute-done((bf16[2,4,128,128]{3,2,1,0:T(8,128)(2,1)S(1)}, bf16[2,4,128,128]{3,2,1,0:T(8,128)(2,1)S(1)}, u32[]{:S(2)}, u32[]{:S(2)}) %collective-permute-start.5) | collective-permute-done | bytes 262176 | tf_op jit(solution)/shard_map/ppermute | solution.py:368
  114.3 0.6 shard_map.92
  114.9 3.5 %all-to-all-done.3.in_ref = bf16[8,2,128,128]{3,2,1,0:T(8,128)(2,1)S(1)} async-done(((bf16[8,2,128,128]{3,2,1,0:T(8,128)(2,1)}), bf16[8,2,128,128]{3,2,1,0:T(8,128)(2,1)S(1)}, u32[]{:S(2)}, u32[]{:S(2)}) %all-to-all-start.3) | async-done | bytes 524320 | tf_op jit(solution)/shard_map/all_to_all | solution.py:278
  118.4 1.4 shard_map.94
  119.8 3.6 %all-to-all-start.4 = ((bf16[4,2,8,128,128]{4,3,2,1,0:T(8,128)(2,1)}), bf16[4,2,8,128,128]{4,3,2,1,0:T(8,128)(2,1)S(1)}, u32[]{:S(2)}, u32[]{:S(2)}) async-start(bf16[4,2,8,128,128]{4,3,2,1,0:T(8,128)(2,1)} %shard_map.94), calls=%async_computation.4 | async-start | bytes 4194304 | tf_op jit(solution)/shard_map/all_to_all | solution.py:278
  123.4 2.5 %collective-permute-start.6 = (bf16[1,4,128,128]{3,2,1,0:T(8,128)(2,1)S(1)}, bf16[1,4,128,128]{3,2,1,0:T(8,128)(2,1)S(1)}, u32[]{:S(2)}, u32[]{:S(2)}) collective-permute-start(bf16[1,4,128,128]{3,2,1,0:T(8,128)(2,1)S(1)} %get-tuple-element.48), channel_id=1, source_target_pairs={{0,8},{1,9},{2,10},{3,11},{4,12},{5,13},{6,14},{7,15},{8,0},{9,1},... | collective-permute-start | bytes 393224 | tf_op jit(solution)/shard_map/ppermute | solution.py:378
  125.9 11.6 %collective-permute-done.6.b_ref = bf16[1,4,128,128]{3,2,1,0:T(8,128)(2,1)S(1)} collective-permute-done((bf16[1,4,128,128]{3,2,1,0:T(8,128)(2,1)S(1)}, bf16[1,4,128,128]{3,2,1,0:T(8,128)(2,1)S(1)}, u32[]{:S(2)}, u32[]{:S(2)}) %collective-permute-start.6) | collective-permute-done | bytes 131104 | tf_op jit(solution)/shard_map/ppermute | solution.py:378
  137.6 0.8 shard_map.93
  138.3 0.0 all-to-all-done.4.in_ref
  138.3 1.4 shard_map.95
Async XLA Ops:
  28.7 11.1 %collective-permute-start = (bf16[4,4,128,128]{3,2,1,0:T(8,128)(2,1)S(1)}, bf16[4,4,128,128]{3,2,1,0:T(8,128)(2,1)S(1)}, u32[]{:S(2)}, u32[]{:S(2)}) collective-permute-start(bf16[4,4,128,128]{3,2,1,0:T(8,128)(2,1)S(1)} %all_to_all.25.refs_0_), channel_id=1, source_target_pairs={{0,2},{1,15},{2,0},{3,5},{4,6},{5,3},{6,4},{7,9},{8,10},{9,7},{10,... | collective-permute-start | bytes 1572872 | tf_op jit(solution)/shard_map/ppermute | solution.py:307
  31.7 0.7 copy-start.1
  34.0 7.7 %collective-permute-start.1 = (bf16[4,4,128,128]{3,2,1,0:T(8,128)(2,1)S(1)}, bf16[4,4,128,128]{3,2,1,0:T(8,128)(2,1)S(1)}, u32[]{:S(2)}, u32[]{:S(2)}) collective-permute-start(bf16[4,4,128,128]{3,2,1,0:T(8,128)(2,1)S(1)} %all_to_all.25.refs_0_), channel_id=1, source_target_pairs={{0,1},{1,0},{2,3},{3,2},{4,5},{5,4},{6,7},{7,6},{8,9},{9,8},{10,11... | collective-permute-start | bytes 1572872 | tf_op jit(solution)/shard_map/ppermute | solution.py:309
  39.8 3.8 %collective-permute-start.2 = (bf16[4,4,128,128]{3,2,1,0:T(8,128)(2,1)S(1)}, bf16[4,4,128,128]{3,2,1,0:T(8,128)(2,1)S(1)}, u32[]{:S(2)}, u32[]{:S(2)}) collective-permute-start(bf16[4,4,128,128]{3,2,1,0:T(8,128)(2,1)S(1)} %collective-permute-done.refs_1_), channel_id=1, source_target_pairs={{0,1},{1,0},{2,3},{3,2},{4,5},{5,4},{6,7},{7,6},{8,9},{9,8},{10,11... | collective-permute-start | bytes 1572872 | tf_op jit(solution)/shard_map/ppermute | solution.py:309
  49.4 4.6 %copy-start = (bf16[2,8,128,128]{3,2,1,0:T(8,128)(2,1)S(1)}, bf16[2,8,128,128]{3,2,1,0:T(8,128)(2,1)}, u32[]{:S(2)}) copy-start(bf16[2,8,128,128]{3,2,1,0:T(8,128)(2,1)} %get-tuple-element.32.acts_hbm) | copy-start | bytes 1572868
  49.4 19.0 %all-to-all-start.1 = ((bf16[4,2,8,128,128]{4,3,2,1,0:T(8,128)(2,1)}), bf16[4,2,8,128,128]{4,3,2,1,0:T(8,128)(2,1)S(1)}, u32[]{:S(2)}, u32[]{:S(2)}) async-start(bf16[4,2,8,128,128]{4,3,2,1,0:T(8,128)(2,1)} %get-tuple-element.31), calls=%async_computation.1 | async-start | bytes 4194304 | tf_op jit(solution)/shard_map/all_to_all | solution.py:278
  57.1 6.7 %collective-permute-start.3 = (bf16[8,4,128,128]{3,2,1,0:T(8,128)(2,1)S(1)}, bf16[8,4,128,128]{3,2,1,0:T(8,128)(2,1)S(1)}, u32[]{:S(2)}, u32[]{:S(2)}) collective-permute-start(bf16[8,4,128,128]{3,2,1,0:T(8,128)(2,1)S(1)} %get-tuple-element.34), channel_id=1, source_target_pairs={{0,1},{1,0},{2,3},{3,2},{4,5},{5,4},{6,7},{7,6},{8,9},{9,8},{10,11... | collective-permute-start | bytes 3145736 | tf_op jit(solution)/shard_map/ppermute | solution.py:348
  69.5 26.3 %all-to-all-start.2 = ((bf16[8,2,128,128]{3,2,1,0:T(8,128)(2,1)}), bf16[8,2,128,128]{3,2,1,0:T(8,128)(2,1)S(1)}, u32[]{:S(2)}, u32[]{:S(2)}) async-start(bf16[8,2,128,128]{3,2,1,0:T(8,128)(2,1)} %shard_map.89), calls=%async_computation.2 | async-start | bytes 1048576 | tf_op jit(solution)/shard_map/all_to_all | solution.py:278
  79.6 11.1 %collective-permute-start.4 = (bf16[4,4,128,128]{3,2,1,0:T(8,128)(2,1)S(1)}, bf16[4,4,128,128]{3,2,1,0:T(8,128)(2,1)S(1)}, u32[]{:S(2)}, u32[]{:S(2)}) collective-permute-start(bf16[4,4,128,128]{3,2,1,0:T(8,128)(2,1)S(1)} %get-tuple-element.39), channel_id=1, source_target_pairs={{0,2},{1,15},{2,0},{3,5},{4,6},{5,3},{6,4},{7,9},{8,10},{9,7},{10,... | collective-permute-start | bytes 1572872 | tf_op jit(solution)/shard_map/ppermute | solution.py:364
  96.7 21.7 %all-to-all-start.3 = ((bf16[8,2,128,128]{3,2,1,0:T(8,128)(2,1)}), bf16[8,2,128,128]{3,2,1,0:T(8,128)(2,1)S(1)}, u32[]{:S(2)}, u32[]{:S(2)}) async-start(bf16[8,2,128,128]{3,2,1,0:T(8,128)(2,1)} %shard_map.91), calls=%async_computation.3 | async-start | bytes 1048576 | tf_op jit(solution)/shard_map/all_to_all | solution.py:278
  102.4 12.0 %collective-permute-start.5 = (bf16[2,4,128,128]{3,2,1,0:T(8,128)(2,1)S(1)}, bf16[2,4,128,128]{3,2,1,0:T(8,128)(2,1)S(1)}, u32[]{:S(2)}, u32[]{:S(2)}) collective-permute-start(bf16[2,4,128,128]{3,2,1,0:T(8,128)(2,1)S(1)} %get-tuple-element.44), channel_id=1, source_target_pairs={{0,4},{1,13},{2,6},{3,15},{4,0},{5,9},{6,2},{7,11},{8,12},{9,5},{1... | collective-permute-start | bytes 786440 | tf_op jit(solution)/shard_map/ppermute | solution.py:368
  119.8 18.5 %all-to-all-start.4 = ((bf16[4,2,8,128,128]{4,3,2,1,0:T(8,128)(2,1)}), bf16[4,2,8,128,128]{4,3,2,1,0:T(8,128)(2,1)S(1)}, u32[]{:S(2)}, u32[]{:S(2)}) async-start(bf16[4,2,8,128,128]{4,3,2,1,0:T(8,128)(2,1)} %shard_map.94), calls=%async_computation.4 | async-start | bytes 4194304 | tf_op jit(solution)/shard_map/all_to_all | solution.py:278
  123.4 14.1 %collective-permute-start.6 = (bf16[1,4,128,128]{3,2,1,0:T(8,128)(2,1)S(1)}, bf16[1,4,128,128]{3,2,1,0:T(8,128)(2,1)S(1)}, u32[]{:S(2)}, u32[]{:S(2)}) collective-permute-start(bf16[1,4,128,128]{3,2,1,0:T(8,128)(2,1)S(1)} %get-tuple-element.48), channel_id=1, source_target_pairs={{0,8},{1,9},{2,10},{3,11},{4,12},{5,13},{6,14},{7,15},{8,0},{9,1},... | collective-permute-start | bytes 393224 | tf_op jit(solution)/shard_map/ppermute | solution.py:378

commit v5 on v4

--- a/solution.py
+++ b/solution.py
@@ -80,7 +80,13 @@
             out_ref[half, 2 + j] = cot
 
 
-def table_kernel(mask_ref, out_ref, cells):
+def table_kernel(mask_ref, up_hbm, down_hbm, out_ref, up_ref, down_ref, cells, sems):
+    copies = [
+        pltpu.make_async_copy(up_hbm, up_ref, sems.at[0]),
+        pltpu.make_async_copy(down_hbm, down_ref, sems.at[1]),
+    ]
+    for copy in copies:
+        copy.start()
     count = jnp.int32(0)
     for cell in range(ROWS * COLS):
         cells[count] = jnp.int32(cell)
@@ -95,31 +101,13 @@
         out_ref[2 * SLOTS + s] = jnp.where(row == last_row, 0, 1)
         out_ref[3 * SLOTS + s] = jnp.where(used, 1, 0)
         last_row = row
-
-
-def load_tiles(sources, goals, sems):
-    copies = [
-        [
-            pltpu.make_async_copy(source.at[pl.ds(8 * q, 8)], goal.at[pl.ds(8 * q, 8)], sems.at[q, n])
-            for n, (source, goal) in enumerate(zip(sources, goals))
-        ]
-        for q in range(SLOTS // 8)
-    ]
-    for group in copies:
-        for copy in group:
-            copy.start()
-    return copies
-
-
-def wait_tiles(copies, q):
-    for copy in copies[q]:
+    for copy in copies:
         copy.wait()
 
 
 def first_kernel(table_ref, place_ref, *refs):
-    panel_refs, (up_hbm, down_hbm, grads_hbm, acts_hbm) = refs[:4], refs[4:8]
-    panels, hid, dac, grads, acts, up_ref, down_ref, sems, tile_sems = refs[8:]
-    loads = load_tiles((up_hbm, down_hbm), (up_ref, down_ref), tile_sems)
+    panel_refs, (up_ref, down_ref, grads_hbm, acts_hbm) = refs[:4], refs[4:8]
+    panels, hid, dac, grads, acts, sems, act_sem = refs[8:]
     core = place_ref[0]
     odd = place_ref[1] & 1
     for side in range(2):
@@ -133,8 +121,6 @@
     hid_sum = jnp.zeros((BLK, BLK), F32)
     dac_sum = jnp.zeros((BLK, BLK), F32)
     for s in range(SLOTS):
-        if s % 8 == 0:
-            wait_tiles(loads, s // 8)
         side, other, half, j = place(s)
         row = table_ref[SLOTS + s]
         fresh = table_ref[2 * SLOTS + s] == 1
@@ -149,7 +135,7 @@
         act, pre = gelu_pair(hid[r], dac[r])
         acts[0, r] = act
         acts[1, r] = pre
-    copies = [pltpu.make_async_copy(acts, acts_hbm, sems.at[4])]
+    copies = [pltpu.make_async_copy(acts, acts_hbm, act_sem)]
     copies[0].start()
     for s in range(SLOTS):
         side, other, half, j = place(s)
@@ -159,27 +145,24 @@
         down_part = nn(acts[0, row], panels[side, other, half, 2 + j])
         grads[s // 8, 0, s % 8] = jnp.where(used, up_part, 0.0).astype(BF)
         grads[s // 8, 1, s % 8] = jnp.where(used, down_part, 0.0).astype(BF)
-        if s % 8 == 7:
-            copies.append(pltpu.make_async_copy(grads.at[s // 8], grads_hbm.at[s // 8], sems.at[s // 8]))
+        if s % 4 == 3:
+            ready = (s // 8, slice(None), pl.ds(s % 8 - 3, 4))
+            copies.append(pltpu.make_async_copy(grads.at[ready], grads_hbm.at[ready], sems.at[s // 4]))
             copies[-1].start()
     for copy in copies:
         copy.wait()
 
 
 def second_kernel(
-    table_ref, place_ref, acts_hbm, up_hbm, down_hbm, own_ref, send_ref, *scratch
+    table_ref, place_ref, acts_hbm, up_ref, down_ref, own_ref, send_ref, out_sum, grad_sum, acts_ref, sem
 ):
-    out_sum, grad_sum, acts_ref, up_ref, down_ref, sem, tile_sems = scratch
     core = place_ref[0]
     copy = pltpu.make_async_copy(acts_hbm, acts_ref, sem)
     copy.start()
-    loads = load_tiles((up_hbm, down_hbm), (up_ref, down_ref), tile_sems)
     out_sum[...] = jnp.zeros_like(out_sum)
     grad_sum[...] = jnp.zeros_like(grad_sum)
     copy.wait()
     for s in range(SLOTS):
-        if s % 8 == 0:
-            wait_tiles(loads, s // 8)
         col = table_ref[s]
         row = table_ref[SLOTS + s]
         used = table_ref[3 * SLOTS + s] == 1
@@ -278,37 +261,8 @@
     return lax.all_to_all(x, axis, 0, 0, tiled=True, axis_index_groups=groups)
 
 
-def body(tokens, cotangent, block_mask, up_tiles, down_tiles):
-    mib = 1 << 20
-    position = lax.axis_index("mp")
-    place = jnp.stack([position & 1, position >> 1]).astype(jnp.int32)
-    tokens, cotangent, up_tiles, down_tiles = (
-        pltpu.with_memory_space_constraint(x, pltpu.HBM) for x in (tokens, cotangent, up_tiles, down_tiles)
-    )
-    sent = call(
-        prep_kernel,
-        shape(NZ // 2, 4, BLK, BLK),
-        (tokens, cotangent),
-        scratch=[pltpu.VMEM((BLK, 2 * BLK), BF), pltpu.VMEM((BLK, 2 * BLK), BF), pltpu.SemaphoreType.DMA((2,))],
-        ins=[pltpu.HBM] * 2,
-        moved=mib,
-    )
-    table = call(
-        table_kernel,
-        shape(4 * SLOTS, dtype=jnp.int32),
-        (block_mask,),
-        scratch=[pltpu.SMEM((ROWS * COLS + 8,), jnp.int32)],
-        ins=[pltpu.SMEM],
-        results=[pltpu.SMEM],
-        flops=mib,
-        moved=1024,
-    )
-    same = exchange(sent, "mp", Z_GROUPS)
-    other = lax.ppermute(same, "mp", z_swap(0))
-    other, table = lax.optimization_barrier((other, table))
-    panels = (same, other, lax.ppermute(same, "mp", CORE_SWAP), lax.ppermute(other, "mp", CORE_SWAP))
-    product = 2 * SLOTS * BLK * BLK * BLK
-    grads, acts = call(
+def run_first(table, place, panels, up_tiles, down_tiles):
+    return call(
         first_kernel,
         [pltpu.HBM((4, 2, 8, BLK, BLK), BF), pltpu.HBM((2, ROWS, BLK, BLK), BF)],
         (table, place) + panels + (up_tiles, down_tiles),
@@ -318,17 +272,18 @@
             pltpu.VMEM((ROWS, BLK, BLK), F32),
             pltpu.VMEM((4, 2, 8, BLK, BLK), BF),
             pltpu.VMEM((2, ROWS, BLK, BLK), BF),
-            pltpu.VMEM((SLOTS, BLK, BLK), BF),
-            pltpu.VMEM((SLOTS, BLK, BLK), BF),
-            pltpu.SemaphoreType.DMA((5,)),
-            pltpu.SemaphoreType.DMA((4, 2)),
+            pltpu.SemaphoreType.DMA((8,)),
+            pltpu.SemaphoreType.DMA,
         ],
-        ins=[pltpu.SMEM] * 2 + [pltpu.VMEM] * 4 + [pltpu.HBM] * 2,
+        ins=[pltpu.SMEM] * 2 + [pltpu.VMEM] * 6,
         results=[pltpu.HBM] * 2,
-        flops=4 * product,
-        moved=6 * mib,
-    )
-    own_part, other_part = call(
+        flops=8 * SLOTS * BLK**3,
+        moved=6 << 20,
+    )
+
+
+def run_second(table, place, acts, up_tiles, down_tiles):
+    return call(
         second_kernel,
         [shape(NZ, 4, BLK, BLK), shape(NZ, 4, BLK, BLK)],
         (table, place, acts, up_tiles, down_tiles),
@@ -336,15 +291,45 @@
             pltpu.VMEM((COLS, BLK, BLK), F32),
             pltpu.VMEM((COLS, BLK, BLK), F32),
             pltpu.VMEM((2, ROWS, BLK, BLK), BF),
-            pltpu.VMEM((SLOTS, BLK, BLK), BF),
-            pltpu.VMEM((SLOTS, BLK, BLK), BF),
             pltpu.SemaphoreType.DMA,
-            pltpu.SemaphoreType.DMA((4, 2)),
         ],
-        ins=[pltpu.SMEM] * 2 + [pltpu.HBM] * 3,
-        flops=2 * product,
-        moved=5 * mib,
-    )
+        ins=[pltpu.SMEM] * 2 + [pltpu.HBM] + [pltpu.VMEM] * 2,
+        flops=4 * SLOTS * BLK**3,
+        moved=5 << 20,
+    )
+
+
+def body(tokens, cotangent, block_mask, up_tiles, down_tiles):
+    mib = 1 << 20
+    position = lax.axis_index("mp")
+    place = jnp.stack([position & 1, position >> 1]).astype(jnp.int32)
+    tokens, cotangent, up_tiles, down_tiles = (
+        pltpu.with_memory_space_constraint(x, pltpu.HBM) for x in (tokens, cotangent, up_tiles, down_tiles)
+    )
+    sent = call(
+        prep_kernel,
+        shape(NZ // 2, 4, BLK, BLK),
+        (tokens, cotangent),
+        scratch=[pltpu.VMEM((BLK, 2 * BLK), BF), pltpu.VMEM((BLK, 2 * BLK), BF), pltpu.SemaphoreType.DMA((2,))],
+        ins=[pltpu.HBM] * 2,
+        moved=mib,
+    )
+    table, up_tiles, down_tiles = call(
+        table_kernel,
+        [shape(4 * SLOTS, dtype=jnp.int32), pltpu.VMEM((SLOTS, BLK, BLK), BF), pltpu.VMEM((SLOTS, BLK, BLK), BF)],
+        (block_mask, up_tiles, down_tiles),
+        scratch=[pltpu.SMEM((ROWS * COLS + 8,), jnp.int32), pltpu.SemaphoreType.DMA((2,))],
+        ins=[pltpu.SMEM] + [pltpu.HBM] * 2,
+        results=[pltpu.SMEM] + [pltpu.VMEM] * 2,
+        flops=mib,
+        moved=4 * mib,
+    )
+    same = exchange(sent, "mp", Z_GROUPS)
+    other = lax.ppermute(same, "mp", z_swap(0))
+    other, table, up_tiles, down_tiles = lax.optimization_barrier((other, table, up_tiles, down_tiles))
+    panels = (same, other, lax.ppermute(same, "mp", CORE_SWAP), lax.ppermute(other, "mp", CORE_SWAP))
+    grads, acts = run_first(table, place, panels, up_tiles, down_tiles)
+    own_part, other_part = run_second(table, place, acts, up_tiles, down_tiles)
     from_other = lax.ppermute(other_part, "mp", CORE_SWAP)
 
     def halve(level, a, b):

time: 142 us -> 141 us (level)
  local copies, waits for them, and re-layouts: 0.69 us -> 2.95 us
  waiting for transfers between devices: 49.5 us -> 47.5 us
    unnamed x4 -> x8, local copies, waits for them, and re-layouts: 0.69 us -> 2.95 us
where the time goes in v5:
time: 141 us; the launch traced here: 139 us
  waiting for transfers between devices  47.5 us (34%)
  starting transfers between devices  42.4 us (30%)
  blocking collectives  27.1 us (19%)
  Pallas kernels  18 us (13%)
  local copies, waits for them, and re-layouts  2.95 us (2%)
    all_to_all x1, blocking collectives, exchange(): return lax.all_to_all(x, axis, 0, 0, tiled=True, axis_index_groups=groups)  27.1 us
    all_to_all x4, starting transfers between devices, exchange(): return lax.all_to_all(x, axis, 0, 0, tiled=True, axis_index_groups=groups)  23.8 us
    pallas_call x12, Pallas kernels, call(): pl.pallas_call(kernel, out_shape=outs, in_specs=[pl.BlockSpec(memory_spac...  18 us
    ppermute x1, waiting for transfers between devices, body(): lax.ppermute(send, 'mp', z_swap(2))  11.7 us
    all_to_all x4, waiting for transfers between devices, exchange(): return lax.all_to_all(x, axis, 0, 0, tiled=True, axis_index_groups=groups)  10.9 us
    ppermute x1, waiting for transfers between devices, body(): keep, send = halve(2, keep, lax.ppermute(send, 'mp', z_swap(1)))  10.1 us
    ppermute x1, waiting for transfers between devices, body(): keep, send = halve(1, keep, lax.ppermute(send, 'mp', z_swap(0)))  8.07 us
    ppermute x1, starting transfers between devices, body(): from_other = lax.ppermute(other_part, 'mp', CORE_SWAP)  4.42 us
  transfers between devices with their start and end apart: 11, of which 9 were waited for; matrix products, arithmetic and copies ran while one was open for 0% of the time, Pallas kernels for 5%

profile of v5, /device:TPU:6, one launch (start us, length us, event | category | flops | bytes accessed | tf_op | source)
XLA Modules:
  0.0 138.8 jit_solution(4005968057586580288)
XLA Ops:
  0.6 1.0 shard_map.84
  1.6 27.1 %all_to_all.25.refs_0_ = bf16[4,4,128,128]{3,2,1,0:T(8,128)(2,1)S(1)} all-to-all(bf16[4,4,128,128]{3,2,1,0:T(8,128)(2,1)S(1)} %shard_map.84), channel_id=1, replica_groups={{0,4,8,12},{1,5,9,13},{2,6,10,14},{3,7,11,15},{16,20,24,28},{17,21,25,2..., dimensions={0} | all-to-all | bytes 1048576 | tf_op jit(solution)/shard_map/all_to_all | solution.py:261
  28.7 3.0 %collective-permute-start = (bf16[4,4,128,128]{3,2,1,0:T(8,128)(2,1)S(1)}, bf16[4,4,128,128]{3,2,1,0:T(8,128)(2,1)S(1)}, u32[]{:S(2)}, u32[]{:S(2)}) collective-permute-start(bf16[4,4,128,128]{3,2,1,0:T(8,128)(2,1)S(1)} %all_to_all.25.refs_0_), channel_id=1, source_target_pairs={{0,2},{1,15},{2,0},{3,5},{4,6},{5,3},{6,4},{7,9},{8,10},{9,7},{10,... | collective-permute-start | bytes 1572872 | tf_op jit(solution)/shard_map/ppermute | solution.py:328
  31.7 0.0 copy-start.3
  31.7 0.7 copy-done.3
  32.4 2.7 %shard_map.85 = (s32[128]{0:T(128)S(1)}, bf16[32,128,128]{2,1,0:T(8,128)(2,1)S(1)}, bf16[32,128,128]{2,1,0:T(8,128)(2,1)S(1)}) custom-call(s32[8,32]{1,0:T(8,128)S(1)} %copy-done.3, bf16[32,128,128]{2,1,0:T(8,128)(2,1)} %up_hbm.1, bf16[32,128,128]{2,1,0:T(8,128)(2,1)} %down_hbm.1), custom_call_target="tpu_custom_call" | custom-call | flops 1048576 | bytes 4194304 | tf_op jit(solution)/shard_map/pallas_call | solution.py:249
  35.1 0.0 copy-start
  35.2 1.9 %collective-permute-start.1 = (bf16[4,4,128,128]{3,2,1,0:T(8,128)(2,1)S(1)}, bf16[4,4,128,128]{3,2,1,0:T(8,128)(2,1)}, u32[]{:S(2)}, u32[]{:S(2)}) collective-permute-start(bf16[4,4,128,128]{3,2,1,0:T(8,128)(2,1)S(1)} %all_to_all.25.refs_0_), channel_id=1, source_target_pairs={{0,1},{1,0},{2,3},{3,2},{4,5},{5,4},{6,7},{7,6},{8,9},{9,8},{10,11... | collective-permute-start | bytes 1572872 | tf_op jit(solution)/shard_map/ppermute | solution.py:330
  37.1 2.7 %collective-permute-done.refs_1_ = bf16[4,4,128,128]{3,2,1,0:T(8,128)(2,1)S(1)} collective-permute-done((bf16[4,4,128,128]{3,2,1,0:T(8,128)(2,1)S(1)}, bf16[4,4,128,128]{3,2,1,0:T(8,128)(2,1)S(1)}, u32[]{:S(2)}, u32[]{:S(2)}) %collective-permute-start) | collective-permute-done | bytes 524320 | tf_op jit(solution)/shard_map/ppermute | solution.py:328
  39.8 1.9 %collective-permute-start.2 = (bf16[4,4,128,128]{3,2,1,0:T(8,128)(2,1)S(1)}, bf16[4,4,128,128]{3,2,1,0:T(8,128)(2,1)}, u32[]{:S(2)}, u32[]{:S(2)}) collective-permute-start(bf16[4,4,128,128]{3,2,1,0:T(8,128)(2,1)S(1)} %collective-permute-done.refs_1_), channel_id=1, source_target_pairs={{0,1},{1,0},{2,3},{3,2},{4,5},{5,4},{6,7},{7,6},{8,9},{9,8},{10,11... | collective-permute-start | bytes 1572872 | tf_op jit(solution)/shard_map/ppermute | solution.py:330
  41.7 0.1 pad_add_fusion.place_ref
  41.8 0.0 collective-permute-done.1.refs_2_
  41.8 1.9 %collective-permute-done.2.refs_3_ = bf16[4,4,128,128]{3,2,1,0:T(8,128)(2,1)} collective-permute-done((bf16[4,4,128,128]{3,2,1,0:T(8,128)(2,1)S(1)}, bf16[4,4,128,128]{3,2,1,0:T(8,128)(2,1)}, u32[]{:S(2)}, u32[]{:S(2)}) %collective-permute-start.2) | collective-permute-done | bytes 524320 | tf_op jit(solution)/shard_map/ppermute | solution.py:330
  43.7 4.9 %shard_map.86 = (bf16[4,2,8,128,128]{4,3,2,1,0:T(8,128)(2,1)}, bf16[2,8,128,128]{3,2,1,0:T(8,128)(2,1)}) custom-call(s32[128]{0:T(128)S(1)} %get-tuple-element.37.table_ref, s32[2]{0:T(128)S(1)} %pad_add_fusion.place_ref, bf16[4,4,128,128]{3,2,1,0:T(8,128)(2,1)S(1)} %all_to_all.25.refs_0_, bf16[4,4,128,128]{3,2,1,0:T(8,128)(2,1)S(1)} %collective-permute-done.refs_1_, ...), custom_call_target="tpu_custom_call" | custom-call | flops 536870912 | bytes 6291456 | tf_op jit(solution)/shard_map/pallas_call | solution.py:249
  48.7 0.0 copy-done
  48.7 4.4 %all-to-all-start.1 = ((bf16[4,2,8,128,128]{4,3,2,1,0:T(8,128)(2,1)}), bf16[4,2,8,128,128]{4,3,2,1,0:T(8,128)(2,1)S(1)}, u32[]{:S(2)}, u32[]{:S(2)}) async-start(bf16[4,2,8,128,128]{4,3,2,1,0:T(8,128)(2,1)} %get-tuple-element.41), calls=%async_computation.1 | async-start | bytes 4194304 | tf_op jit(solution)/shard_map/all_to_all | solution.py:261
  53.1 0.0 copy-start.1
  53.1 1.2 copy-done.1
  54.3 0.0 copy-start.2
  54.3 1.0 copy-done.2
  55.3 1.9 %shard_map.87 = (bf16[8,4,128,128]{3,2,1,0:T(8,128)(2,1)S(1)}, bf16[8,4,128,128]{3,2,1,0:T(8,128)(2,1)S(1)}) custom-call(s32[128]{0:T(128)S(1)} %get-tuple-element.37.table_ref, s32[2]{0:T(128)S(1)} %pad_add_fusion.place_ref, bf16[2,8,128,128]{3,2,1,0:T(8,128)(2,1)S(1)} %copy-done.2, bf16[32,128,128]{2,1,0:T(8,128)(2,1)S(1)} %get-tuple-element.39.refs_4_.up_ref, ...), custom_call_target="tpu_custom_call" | custom-call | flops 268435456 | bytes 5242880 | tf_op jit(solution)/shard_map/pallas_call | solution.py:249
  57.2 4.4 %collective-permute-start.3 = (bf16[8,4,128,128]{3,2,1,0:T(8,128)(2,1)S(1)}, bf16[8,4,128,128]{3,2,1,0:T(8,128)(2,1)S(1)}, u32[]{:S(2)}, u32[]{:S(2)}) collective-permute-start(bf16[8,4,128,128]{3,2,1,0:T(8,128)(2,1)S(1)} %get-tuple-element.44), channel_id=1, source_target_pairs={{0,1},{1,0},{2,3},{3,2},{4,5},{5,4},{6,7},{7,6},{8,9},{9,8},{10,11... | collective-permute-start | bytes 3145736 | tf_op jit(solution)/shard_map/ppermute | solution.py:333
  61.6 2.3 %collective-permute-done.3.b_ref = bf16[8,4,128,128]{3,2,1,0:T(8,128)(2,1)S(1)} collective-permute-done((bf16[8,4,128,128]{3,2,1,0:T(8,128)(2,1)S(1)}, bf16[8,4,128,128]{3,2,1,0:T(8,128)(2,1)S(1)}, u32[]{:S(2)}, u32[]{:S(2)}) %collective-permute-start.3) | collective-permute-done | bytes 1048608 | tf_op jit(solution)/shard_map/ppermute | solution.py:333
  63.9 0.8 shard_map.88
  64.7 2.9 %all-to-all-done.1.in_ref = bf16[4,2,8,128,128]{4,3,2,1,0:T(8,128)(2,1)S(1)} async-done(((bf16[4,2,8,128,128]{4,3,2,1,0:T(8,128)(2,1)}), bf16[4,2,8,128,128]{4,3,2,1,0:T(8,128)(2,1)S(1)}, u32[]{:S(2)}, u32[]{:S(2)}) %all-to-all-start.1) | async-done | bytes 2097184 | tf_op jit(solution)/shard_map/all_to_all | solution.py:261
  67.6 1.0 shard_map.89
  68.6 10.1 %all-to-all-start.2 = ((bf16[8,2,128,128]{3,2,1,0:T(8,128)(2,1)}), bf16[8,2,128,128]{3,2,1,0:T(8,128)(2,1)S(1)}, u32[]{:S(2)}, u32[]{:S(2)}) async-start(bf16[8,2,128,128]{3,2,1,0:T(8,128)(2,1)} %shard_map.89), calls=%async_computation.2 | async-start | bytes 1048576 | tf_op jit(solution)/shard_map/all_to_all | solution.py:261
  78.7 3.0 %collective-permute-start.4 = (bf16[4,4,128,128]{3,2,1,0:T(8,128)(2,1)S(1)}, bf16[4,4,128,128]{3,2,1,0:T(8,128)(2,1)S(1)}, u32[]{:S(2)}, u32[]{:S(2)}) collective-permute-start(bf16[4,4,128,128]{3,2,1,0:T(8,128)(2,1)S(1)} %get-tuple-element.49), channel_id=1, source_target_pairs={{0,2},{1,15},{2,0},{3,5},{4,6},{5,3},{6,4},{7,9},{8,10},{9,7},{10,... | collective-permute-start | bytes 1572872 | tf_op jit(solution)/shard_map/ppermute | solution.py:349
  81.7 8.1 %collective-permute-done.4.b_ref = bf16[4,4,128,128]{3,2,1,0:T(8,128)(2,1)S(1)} collective-permute-done((bf16[4,4,128,128]{3,2,1,0:T(8,128)(2,1)S(1)}, bf16[4,4,128,128]{3,2,1,0:T(8,128)(2,1)S(1)}, u32[]{:S(2)}, u32[]{:S(2)}) %collective-permute-start.4) | collective-permute-done | bytes 524320 | tf_op jit(solution)/shard_map/ppermute | solution.py:349
  89.7 0.7 shard_map.90
  90.4 4.5 %all-to-all-done.2.in_ref = bf16[8,2,128,128]{3,2,1,0:T(8,128)(2,1)S(1)} async-done(((bf16[8,2,128,128]{3,2,1,0:T(8,128)(2,1)}), bf16[8,2,128,128]{3,2,1,0:T(8,128)(2,1)S(1)}, u32[]{:S(2)}, u32[]{:S(2)}) %all-to-all-start.2) | async-done | bytes 524320 | tf_op jit(solution)/shard_map/all_to_all | solution.py:261
  94.9 0.9 shard_map.91
  95.8 5.7 %all-to-all-start.3 = ((bf16[8,2,128,128]{3,2,1,0:T(8,128)(2,1)}), bf16[8,2,128,128]{3,2,1,0:T(8,128)(2,1)S(1)}, u32[]{:S(2)}, u32[]{:S(2)}) async-start(bf16[8,2,128,128]{3,2,1,0:T(8,128)(2,1)} %shard_map.91), calls=%async_computation.3 | async-start | bytes 1048576 | tf_op jit(solution)/shard_map/all_to_all | solution.py:261
  101.5 1.9 %collective-permute-start.5 = (bf16[2,4,128,128]{3,2,1,0:T(8,128)(2,1)S(1)}, bf16[2,4,128,128]{3,2,1,0:T(8,128)(2,1)S(1)}, u32[]{:S(2)}, u32[]{:S(2)}) collective-permute-start(bf16[2,4,128,128]{3,2,1,0:T(8,128)(2,1)S(1)} %get-tuple-element.54), channel_id=1, source_target_pairs={{0,4},{1,13},{2,6},{3,15},{4,0},{5,9},{6,2},{7,11},{8,12},{9,5},{1... | collective-permute-start | bytes 786440 | tf_op jit(solution)/shard_map/ppermute | solution.py:353
  103.4 10.1 %collective-permute-done.5.b_ref = bf16[2,4,128,128]{3,2,1,0:T(8,128)(2,1)S(1)} collective-permute-done((bf16[2,4,128,128]{3,2,1,0:T(8,128)(2,1)S(1)}, bf16[2,4,128,128]{3,2,1,0:T(8,128)(2,1)S(1)}, u32[]{:S(2)}, u32[]{:S(2)}) %collective-permute-start.5) | collective-permute-done | bytes 262176 | tf_op jit(solution)/shard_map/ppermute | solution.py:353
  113.4 0.6 shard_map.92
  114.1 3.5 %all-to-all-done.3.in_ref = bf16[8,2,128,128]{3,2,1,0:T(8,128)(2,1)S(1)} async-done(((bf16[8,2,128,128]{3,2,1,0:T(8,128)(2,1)}), bf16[8,2,128,128]{3,2,1,0:T(8,128)(2,1)S(1)}, u32[]{:S(2)}, u32[]{:S(2)}) %all-to-all-start.3) | async-done | bytes 524320 | tf_op jit(solution)/shard_map/all_to_all | solution.py:261
  117.5 1.4 %shard_map.94 = bf16[4,2,8,128,128]{4,3,2,1,0:T(8,128)(2,1)} custom-call(bf16[8,2,128,128]{3,2,1,0:T(8,128)(2,1)S(1)} %all-to-all-done.3.in_ref), custom_call_target="tpu_custom_call" | custom-call | bytes 3145728 | tf_op jit(solution)/shard_map/pallas_call | solution.py:249
  118.9 3.6 %all-to-all-start.4 = ((bf16[4,2,8,128,128]{4,3,2,1,0:T(8,128)(2,1)}), bf16[4,2,8,128,128]{4,3,2,1,0:T(8,128)(2,1)S(1)}, u32[]{:S(2)}, u32[]{:S(2)}) async-start(bf16[4,2,8,128,128]{4,3,2,1,0:T(8,128)(2,1)} %shard_map.94), calls=%async_computation.4 | async-start | bytes 4194304 | tf_op jit(solution)/shard_map/all_to_all | solution.py:261
  122.5 2.5 %collective-permute-start.6 = (bf16[1,4,128,128]{3,2,1,0:T(8,128)(2,1)S(1)}, bf16[1,4,128,128]{3,2,1,0:T(8,128)(2,1)S(1)}, u32[]{:S(2)}, u32[]{:S(2)}) collective-permute-start(bf16[1,4,128,128]{3,2,1,0:T(8,128)(2,1)S(1)} %get-tuple-element.58), channel_id=1, source_target_pairs={{0,8},{1,9},{2,10},{3,11},{4,12},{5,13},{6,14},{7,15},{8,0},{9,1},... | collective-permute-start | bytes 393224 | tf_op jit(solution)/shard_map/ppermute | solution.py:363
  125.0 11.7 %collective-permute-done.6.b_ref = bf16[1,4,128,128]{3,2,1,0:T(8,128)(2,1)S(1)} collective-permute-done((bf16[1,4,128,128]{3,2,1,0:T(8,128)(2,1)S(1)}, bf16[1,4,128,128]{3,2,1,0:T(8,128)(2,1)S(1)}, u32[]{:S(2)}, u32[]{:S(2)}) %collective-permute-start.6) | collective-permute-done | bytes 131104 | tf_op jit(solution)/shard_map/ppermute | solution.py:363
  136.7 0.8 shard_map.93
  137.4 0.0 all-to-all-done.4.in_ref
  137.4 1.4 shard_map.95
Async XLA Ops:
  28.7 11.1 %collective-permute-start = (bf16[4,4,128,128]{3,2,1,0:T(8,128)(2,1)S(1)}, bf16[4,4,128,128]{3,2,1,0:T(8,128)(2,1)S(1)}, u32[]{:S(2)}, u32[]{:S(2)}) collective-permute-start(bf16[4,4,128,128]{3,2,1,0:T(8,128)(2,1)S(1)} %all_to_all.25.refs_0_), channel_id=1, source_target_pairs={{0,2},{1,15},{2,0},{3,5},{4,6},{5,3},{6,4},{7,9},{8,10},{9,7},{10,... | collective-permute-start | bytes 1572872 | tf_op jit(solution)/shard_map/ppermute | solution.py:328
  31.7 0.7 copy-start.3
  35.1 13.5 %copy-start = (bf16[32,128,128]{2,1,0:T(8,128)(2,1)}, bf16[32,128,128]{2,1,0:T(8,128)(2,1)S(1)}, u32[]{:S(2)}) copy-start(bf16[32,128,128]{2,1,0:T(8,128)(2,1)S(1)} %get-tuple-element.40.refs_5_.down_ref) | copy-start | bytes 3145732
  35.2 6.6 %collective-permute-start.1 = (bf16[4,4,128,128]{3,2,1,0:T(8,128)(2,1)S(1)}, bf16[4,4,128,128]{3,2,1,0:T(8,128)(2,1)}, u32[]{:S(2)}, u32[]{:S(2)}) collective-permute-start(bf16[4,4,128,128]{3,2,1,0:T(8,128)(2,1)S(1)} %all_to_all.25.refs_0_), channel_id=1, source_target_pairs={{0,1},{1,0},{2,3},{3,2},{4,5},{5,4},{6,7},{7,6},{8,9},{9,8},{10,11... | collective-permute-start | bytes 1572872 | tf_op jit(solution)/shard_map/ppermute | solution.py:330
  39.8 3.9 %collective-permute-start.2 = (bf16[4,4,128,128]{3,2,1,0:T(8,128)(2,1)S(1)}, bf16[4,4,128,128]{3,2,1,0:T(8,128)(2,1)}, u32[]{:S(2)}, u32[]{:S(2)}) collective-permute-start(bf16[4,4,128,128]{3,2,1,0:T(8,128)(2,1)S(1)} %collective-permute-done.refs_1_), channel_id=1, source_target_pairs={{0,1},{1,0},{2,3},{3,2},{4,5},{5,4},{6,7},{7,6},{8,9},{9,8},{10,11... | collective-permute-start | bytes 1572872 | tf_op jit(solution)/shard_map/ppermute | solution.py:330
  48.7 18.9 %all-to-all-start.1 = ((bf16[4,2,8,128,128]{4,3,2,1,0:T(8,128)(2,1)}), bf16[4,2,8,128,128]{4,3,2,1,0:T(8,128)(2,1)S(1)}, u32[]{:S(2)}, u32[]{:S(2)}) async-start(bf16[4,2,8,128,128]{4,3,2,1,0:T(8,128)(2,1)} %get-tuple-element.41), calls=%async_computation.1 | async-start | bytes 4194304 | tf_op jit(solution)/shard_map/all_to_all | solution.py:261
  53.1 1.2 copy-start.1
  54.3 1.0 copy-start.2
  57.2 6.7 %collective-permute-start.3 = (bf16[8,4,128,128]{3,2,1,0:T(8,128)(2,1)S(1)}, bf16[8,4,128,128]{3,2,1,0:T(8,128)(2,1)S(1)}, u32[]{:S(2)}, u32[]{:S(2)}) collective-permute-start(bf16[8,4,128,128]{3,2,1,0:T(8,128)(2,1)S(1)} %get-tuple-element.44), channel_id=1, source_target_pairs={{0,1},{1,0},{2,3},{3,2},{4,5},{5,4},{6,7},{7,6},{8,9},{9,8},{10,11... | collective-permute-start | bytes 3145736 | tf_op jit(solution)/shard_map/ppermute | solution.py:333
  68.6 26.3 %all-to-all-start.2 = ((bf16[8,2,128,128]{3,2,1,0:T(8,128)(2,1)}), bf16[8,2,128,128]{3,2,1,0:T(8,128)(2,1)S(1)}, u32[]{:S(2)}, u32[]{:S(2)}) async-start(bf16[8,2,128,128]{3,2,1,0:T(8,128)(2,1)} %shard_map.89), calls=%async_computation.2 | async-start | bytes 1048576 | tf_op jit(solution)/shard_map/all_to_all | solution.py:261
  78.7 11.1 %collective-permute-start.4 = (bf16[4,4,128,128]{3,2,1,0:T(8,128)(2,1)S(1)}, bf16[4,4,128,128]{3,2,1,0:T(8,128)(2,1)S(1)}, u32[]{:S(2)}, u32[]{:S(2)}) collective-permute-start(bf16[4,4,128,128]{3,2,1,0:T(8,128)(2,1)S(1)} %get-tuple-element.49), channel_id=1, source_target_pairs={{0,2},{1,15},{2,0},{3,5},{4,6},{5,3},{6,4},{7,9},{8,10},{9,7},{10,... | collective-permute-start | bytes 1572872 | tf_op jit(solution)/shard_map/ppermute | solution.py:349
  95.8 21.7 %all-to-all-start.3 = ((bf16[8,2,128,128]{3,2,1,0:T(8,128)(2,1)}), bf16[8,2,128,128]{3,2,1,0:T(8,128)(2,1)S(1)}, u32[]{:S(2)}, u32[]{:S(2)}) async-start(bf16[8,2,128,128]{3,2,1,0:T(8,128)(2,1)} %shard_map.91), calls=%async_computation.3 | async-start | bytes 1048576 | tf_op jit(solution)/shard_map/all_to_all | solution.py:261
  101.5 12.0 %collective-permute-start.5 = (bf16[2,4,128,128]{3,2,1,0:T(8,128)(2,1)S(1)}, bf16[2,4,128,128]{3,2,1,0:T(8,128)(2,1)S(1)}, u32[]{:S(2)}, u32[]{:S(2)}) collective-permute-start(bf16[2,4,128,128]{3,2,1,0:T(8,128)(2,1)S(1)} %get-tuple-element.54), channel_id=1, source_target_pairs={{0,4},{1,13},{2,6},{3,15},{4,0},{5,9},{6,2},{7,11},{8,12},{9,5},{1... | collective-permute-start | bytes 786440 | tf_op jit(solution)/shard_map/ppermute | solution.py:353
  118.9 18.5 %all-to-all-start.4 = ((bf16[4,2,8,128,128]{4,3,2,1,0:T(8,128)(2,1)}), bf16[4,2,8,128,128]{4,3,2,1,0:T(8,128)(2,1)S(1)}, u32[]{:S(2)}, u32[]{:S(2)}) async-start(bf16[4,2,8,128,128]{4,3,2,1,0:T(8,128)(2,1)} %shard_map.94), calls=%async_computation.4 | async-start | bytes 4194304 | tf_op jit(solution)/shard_map/all_to_all | solution.py:261
  122.5 14.1 %collective-permute-start.6 = (bf16[1,4,128,128]{3,2,1,0:T(8,128)(2,1)S(1)}, bf16[1,4,128,128]{3,2,1,0:T(8,128)(2,1)S(1)}, u32[]{:S(2)}, u32[]{:S(2)}) collective-permute-start(bf16[1,4,128,128]{3,2,1,0:T(8,128)(2,1)S(1)} %get-tuple-element.58), channel_id=1, source_target_pairs={{0,8},{1,9},{2,10},{3,11},{4,12},{5,13},{6,14},{7,15},{8,0},{9,1},... | collective-permute-start | bytes 393224 | tf_op jit(solution)/shard_map/ppermute | solution.py:363

commit v6 on v5

--- a/solution.py
+++ b/solution.py
@@ -9,7 +9,7 @@
 
 BF = jnp.bfloat16
 F32 = jnp.float32
-VM = pltpu.CompilerParams(vmem_limit_bytes=48 * 1024 * 1024)
+VM = pltpu.CompilerParams(vmem_limit_bytes=32 * 1024 * 1024)
 NX, NY, NZ = 4, 8, 8
 N_MP = 2 * NZ
 
@@ -189,23 +189,31 @@
         send_ref[half] = (a_ref[far].astype(F32) + b_ref[far].astype(F32)).astype(BF)
 
 
-def x_sum_kernel(in_ref, out_ref):
+def x_sum_kernel(in_ref, out_hbm, sums, sems):
+    copies = []
     for y in range(NY):
         for k in range(2):
             total = in_ref[0, k, y].astype(F32)
             for x in range(1, NX):
                 total = total + in_ref[x, k, y].astype(F32)
-            out_ref[y, k] = total.astype(BF)
-
-
-def y_sum_kernel(in_ref, out_ref):
+            sums[y, k] = total.astype(BF)
+        copies.append(pltpu.make_async_copy(sums.at[y], out_hbm.at[y], sems.at[y]))
+        copies[-1].start()
+    for copy in copies:
+        copy.wait()
+
+
+def y_sum_kernel(in_ref, out_hbm, sums, sems):
     for k in range(2):
         total = in_ref[0, k].astype(F32)
         for y in range(1, NY):
             total = total + in_ref[y, k].astype(F32)
-        total = total.astype(BF)
-        for y in range(NY):
-            out_ref[y, k] = total
+        sums[k] = total.astype(BF)
+    copies = [pltpu.make_async_copy(sums, out_hbm.at[y], sems.at[y]) for y in range(NY)]
+    for copy in copies:
+        copy.start()
+    for copy in copies:
+        copy.wait()
 
 
 def spread_kernel(in_ref, out_hbm, sems):
@@ -345,11 +353,25 @@
     keep, send = halve(0, own_part, from_other)
     by_x = exchange(grads, ("dp", "mp"), NEAR_GROUPS)
     by_x, keep, send = lax.optimization_barrier((by_x, keep, send))
-    x_done = call(x_sum_kernel, shape(NY, 2, BLK, BLK), (by_x,), moved=3 * mib)
+    x_done = call(
+        x_sum_kernel,
+        pltpu.HBM((NY, 2, BLK, BLK), BF),
+        (by_x,),
+        scratch=[pltpu.VMEM((NY, 2, BLK, BLK), BF), pltpu.SemaphoreType.DMA((NY,))],
+        results=[pltpu.HBM],
+        moved=3 * mib,
+    )
     keep, send = halve(1, keep, lax.ppermute(send, "mp", z_swap(0)))
     by_y = exchange(x_done, ("dp", "mp"), FAR_GROUPS)
     by_y, keep, send = lax.optimization_barrier((by_y, keep, send))
-    y_done = call(y_sum_kernel, shape(NY, 2, BLK, BLK), (by_y,), moved=mib)
+    y_done = call(
+        y_sum_kernel,
+        pltpu.HBM((NY, 2, BLK, BLK), BF),
+        (by_y,),
+        scratch=[pltpu.VMEM((2, BLK, BLK), BF), pltpu.SemaphoreType.DMA((NY,))],
+        results=[pltpu.HBM],
+        moved=mib,
+    )
     keep, send = halve(2, keep, lax.ppermute(send, "mp", z_swap(1)))
     all_y = exchange(y_done, ("dp", "mp"), FAR_GROUPS)
     all_y, keep, send = lax.optimization_barrier((all_y, keep, send))

time: 141 us -> 141 us (level)
  no operation moved by 1% of the time
where the time goes in v6:
time: 141 us; the launch traced here: 139 us
  waiting for transfers between devices  47.5 us (34%)
  starting transfers between devices  42.4 us (30%)
  blocking collectives  27.1 us (19%)
  Pallas kernels  18 us (13%)
  local copies, waits for them, and re-layouts  2.95 us (2%)
    all_to_all x1, blocking collectives, exchange(): return lax.all_to_all(x, axis, 0, 0, tiled=True, axis_index_groups=groups)  27.1 us
    all_to_all x4, starting transfers between devices, exchange(): return lax.all_to_all(x, axis, 0, 0, tiled=True, axis_index_groups=groups)  23.8 us
    pallas_call x12, Pallas kernels, call(): pl.pallas_call(kernel, out_shape=outs, in_specs=[pl.BlockSpec(memory_spac...  18 us
    ppermute x1, waiting for transfers between devices, body(): lax.ppermute(send, 'mp', z_swap(2))  11.7 us
    all_to_all x4, waiting for transfers between devices, exchange(): return lax.all_to_all(x, axis, 0, 0, tiled=True, axis_index_groups=groups)  10.9 us
    ppermute x1, waiting for transfers between devices, body(): keep, send = halve(2, keep, lax.ppermute(send, 'mp', z_swap(1)))  10.1 us
    ppermute x1, waiting for transfers between devices, body(): keep, send = halve(1, keep, lax.ppermute(send, 'mp', z_swap(0)))  8.07 us
    ppermute x1, starting transfers between devices, body(): from_other = lax.ppermute(other_part, 'mp', CORE_SWAP)  4.42 us
  transfers between devices with their start and end apart: 11, of which 9 were waited for; matrix products, arithmetic and copies ran while one was open for 0% of the time, Pallas kernels for 5%

profile of v6, /device:TPU:6, one launch (start us, length us, event | category | flops | bytes accessed | tf_op | source)
XLA Modules:
  0.0 138.8 jit_solution(15850197515096238406)
XLA Ops:
  0.6 1.0 shard_map.84
  1.6 27.1 %all_to_all.25.refs_0_ = bf16[4,4,128,128]{3,2,1,0:T(8,128)(2,1)S(1)} all-to-all(bf16[4,4,128,128]{3,2,1,0:T(8,128)(2,1)S(1)} %shard_map.84), channel_id=1, replica_groups={{0,4,8,12},{1,5,9,13},{2,6,10,14},{3,7,11,15},{16,20,24,28},{17,21,25,2..., dimensions={0} | all-to-all | bytes 1048576 | tf_op jit(solution)/shard_map/all_to_all | solution.py:269
  28.7 3.0 %collective-permute-start = (bf16[4,4,128,128]{3,2,1,0:T(8,128)(2,1)S(1)}, bf16[4,4,128,128]{3,2,1,0:T(8,128)(2,1)S(1)}, u32[]{:S(2)}, u32[]{:S(2)}) collective-permute-start(bf16[4,4,128,128]{3,2,1,0:T(8,128)(2,1)S(1)} %all_to_all.25.refs_0_), channel_id=1, source_target_pairs={{0,2},{1,15},{2,0},{3,5},{4,6},{5,3},{6,4},{7,9},{8,10},{9,7},{10,... | collective-permute-start | bytes 1572872 | tf_op jit(solution)/shard_map/ppermute | solution.py:336
  31.7 0.0 copy-start.3
  31.7 0.7 copy-done.3
  32.4 2.7 %shard_map.85 = (s32[128]{0:T(128)S(1)}, bf16[32,128,128]{2,1,0:T(8,128)(2,1)S(1)}, bf16[32,128,128]{2,1,0:T(8,128)(2,1)S(1)}) custom-call(s32[8,32]{1,0:T(8,128)S(1)} %copy-done.3, bf16[32,128,128]{2,1,0:T(8,128)(2,1)} %up_hbm.1, bf16[32,128,128]{2,1,0:T(8,128)(2,1)} %down_hbm.1), custom_call_target="tpu_custom_call" | custom-call | flops 1048576 | bytes 4194304 | tf_op jit(solution)/shard_map/pallas_call | solution.py:257
  35.1 0.0 copy-start
  35.2 1.9 %collective-permute-start.1 = (bf16[4,4,128,128]{3,2,1,0:T(8,128)(2,1)S(1)}, bf16[4,4,128,128]{3,2,1,0:T(8,128)(2,1)}, u32[]{:S(2)}, u32[]{:S(2)}) collective-permute-start(bf16[4,4,128,128]{3,2,1,0:T(8,128)(2,1)S(1)} %all_to_all.25.refs_0_), channel_id=1, source_target_pairs={{0,1},{1,0},{2,3},{3,2},{4,5},{5,4},{6,7},{7,6},{8,9},{9,8},{10,11... | collective-permute-start | bytes 1572872 | tf_op jit(solution)/shard_map/ppermute | solution.py:338
  37.1 2.7 %collective-permute-done.refs_1_ = bf16[4,4,128,128]{3,2,1,0:T(8,128)(2,1)S(1)} collective-permute-done((bf16[4,4,128,128]{3,2,1,0:T(8,128)(2,1)S(1)}, bf16[4,4,128,128]{3,2,1,0:T(8,128)(2,1)S(1)}, u32[]{:S(2)}, u32[]{:S(2)}) %collective-permute-start) | collective-permute-done | bytes 524320 | tf_op jit(solution)/shard_map/ppermute | solution.py:336
  39.8 1.9 %collective-permute-start.2 = (bf16[4,4,128,128]{3,2,1,0:T(8,128)(2,1)S(1)}, bf16[4,4,128,128]{3,2,1,0:T(8,128)(2,1)}, u32[]{:S(2)}, u32[]{:S(2)}) collective-permute-start(bf16[4,4,128,128]{3,2,1,0:T(8,128)(2,1)S(1)} %collective-permute-done.refs_1_), channel_id=1, source_target_pairs={{0,1},{1,0},{2,3},{3,2},{4,5},{5,4},{6,7},{7,6},{8,9},{9,8},{10,11... | collective-permute-start | bytes 1572872 | tf_op jit(solution)/shard_map/ppermute | solution.py:338
  41.7 0.1 pad_add_fusion.place_ref
  41.8 0.0 collective-permute-done.1.refs_2_
  41.8 1.9 %collective-permute-done.2.refs_3_ = bf16[4,4,128,128]{3,2,1,0:T(8,128)(2,1)} collective-permute-done((bf16[4,4,128,128]{3,2,1,0:T(8,128)(2,1)S(1)}, bf16[4,4,128,128]{3,2,1,0:T(8,128)(2,1)}, u32[]{:S(2)}, u32[]{:S(2)}) %collective-permute-start.2) | collective-permute-done | bytes 524320 | tf_op jit(solution)/shard_map/ppermute | solution.py:338
  43.7 4.9 %shard_map.86 = (bf16[4,2,8,128,128]{4,3,2,1,0:T(8,128)(2,1)}, bf16[2,8,128,128]{3,2,1,0:T(8,128)(2,1)}) custom-call(s32[128]{0:T(128)S(1)} %get-tuple-element.37.table_ref, s32[2]{0:T(128)S(1)} %pad_add_fusion.place_ref, bf16[4,4,128,128]{3,2,1,0:T(8,128)(2,1)S(1)} %all_to_all.25.refs_0_, bf16[4,4,128,128]{3,2,1,0:T(8,128)(2,1)S(1)} %collective-permute-done.refs_1_, ...), custom_call_target="tpu_custom_call" | custom-call | flops 536870912 | bytes 6291456 | tf_op jit(solution)/shard_map/pallas_call | solution.py:257
  48.7 0.0 copy-done
  48.7 4.4 %all-to-all-start.1 = ((bf16[4,2,8,128,128]{4,3,2,1,0:T(8,128)(2,1)}), bf16[4,2,8,128,128]{4,3,2,1,0:T(8,128)(2,1)S(1)}, u32[]{:S(2)}, u32[]{:S(2)}) async-start(bf16[4,2,8,128,128]{4,3,2,1,0:T(8,128)(2,1)} %get-tuple-element.41), calls=%async_computation.1 | async-start | bytes 4194304 | tf_op jit(solution)/shard_map/all_to_all | solution.py:269
  53.1 0.0 copy-start.1
  53.1 1.2 copy-done.1
  54.3 0.0 copy-start.2
  54.3 1.0 copy-done.2
  55.3 1.9 %shard_map.87 = (bf16[8,4,128,128]{3,2,1,0:T(8,128)(2,1)S(1)}, bf16[8,4,128,128]{3,2,1,0:T(8,128)(2,1)S(1)}) custom-call(s32[128]{0:T(128)S(1)} %get-tuple-element.37.table_ref, s32[2]{0:T(128)S(1)} %pad_add_fusion.place_ref, bf16[2,8,128,128]{3,2,1,0:T(8,128)(2,1)S(1)} %copy-done.2, bf16[32,128,128]{2,1,0:T(8,128)(2,1)S(1)} %get-tuple-element.39.refs_4_.up_ref, ...), custom_call_target="tpu_custom_call" | custom-call | flops 268435456 | bytes 5242880 | tf_op jit(solution)/shard_map/pallas_call | solution.py:257
  57.2 4.4 %collective-permute-start.3 = (bf16[8,4,128,128]{3,2,1,0:T(8,128)(2,1)S(1)}, bf16[8,4,128,128]{3,2,1,0:T(8,128)(2,1)S(1)}, u32[]{:S(2)}, u32[]{:S(2)}) collective-permute-start(bf16[8,4,128,128]{3,2,1,0:T(8,128)(2,1)S(1)} %get-tuple-element.44), channel_id=1, source_target_pairs={{0,1},{1,0},{2,3},{3,2},{4,5},{5,4},{6,7},{7,6},{8,9},{9,8},{10,11... | collective-permute-start | bytes 3145736 | tf_op jit(solution)/shard_map/ppermute | solution.py:341
  61.6 2.3 %collective-permute-done.3.b_ref = bf16[8,4,128,128]{3,2,1,0:T(8,128)(2,1)S(1)} collective-permute-done((bf16[8,4,128,128]{3,2,1,0:T(8,128)(2,1)S(1)}, bf16[8,4,128,128]{3,2,1,0:T(8,128)(2,1)S(1)}, u32[]{:S(2)}, u32[]{:S(2)}) %collective-permute-start.3) | collective-permute-done | bytes 1048608 | tf_op jit(solution)/shard_map/ppermute | solution.py:341
  63.9 0.8 shard_map.88
  64.7 2.9 %all-to-all-done.1.in_ref = bf16[4,2,8,128,128]{4,3,2,1,0:T(8,128)(2,1)S(1)} async-done(((bf16[4,2,8,128,128]{4,3,2,1,0:T(8,128)(2,1)}), bf16[4,2,8,128,128]{4,3,2,1,0:T(8,128)(2,1)S(1)}, u32[]{:S(2)}, u32[]{:S(2)}) %all-to-all-start.1) | async-done | bytes 2097184 | tf_op jit(solution)/shard_map/all_to_all | solution.py:269
  67.6 1.0 shard_map.89
  68.5 10.1 %all-to-all-start.2 = ((bf16[8,2,128,128]{3,2,1,0:T(8,128)(2,1)}), bf16[8,2,128,128]{3,2,1,0:T(8,128)(2,1)S(1)}, u32[]{:S(2)}, u32[]{:S(2)}) async-start(bf16[8,2,128,128]{3,2,1,0:T(8,128)(2,1)} %shard_map.89), calls=%async_computation.2 | async-start | bytes 1048576 | tf_op jit(solution)/shard_map/all_to_all | solution.py:269
  78.6 3.0 %collective-permute-start.4 = (bf16[4,4,128,128]{3,2,1,0:T(8,128)(2,1)S(1)}, bf16[4,4,128,128]{3,2,1,0:T(8,128)(2,1)S(1)}, u32[]{:S(2)}, u32[]{:S(2)}) collective-permute-start(bf16[4,4,128,128]{3,2,1,0:T(8,128)(2,1)S(1)} %get-tuple-element.49), channel_id=1, source_target_pairs={{0,2},{1,15},{2,0},{3,5},{4,6},{5,3},{6,4},{7,9},{8,10},{9,7},{10,... | collective-permute-start | bytes 1572872 | tf_op jit(solution)/shard_map/ppermute | solution.py:364
  81.6 8.1 %collective-permute-done.4.b_ref = bf16[4,4,128,128]{3,2,1,0:T(8,128)(2,1)S(1)} collective-permute-done((bf16[4,4,128,128]{3,2,1,0:T(8,128)(2,1)S(1)}, bf16[4,4,128,128]{3,2,1,0:T(8,128)(2,1)S(1)}, u32[]{:S(2)}, u32[]{:S(2)}) %collective-permute-start.4) | collective-permute-done | bytes 524320 | tf_op jit(solution)/shard_map/ppermute | solution.py:364
  89.7 0.7 shard_map.90
  90.3 4.5 %all-to-all-done.2.in_ref = bf16[8,2,128,128]{3,2,1,0:T(8,128)(2,1)S(1)} async-done(((bf16[8,2,128,128]{3,2,1,0:T(8,128)(2,1)}), bf16[8,2,128,128]{3,2,1,0:T(8,128)(2,1)S(1)}, u32[]{:S(2)}, u32[]{:S(2)}) %all-to-all-start.2) | async-done | bytes 524320 | tf_op jit(solution)/shard_map/all_to_all | solution.py:269
  94.9 0.9 shard_map.91
  95.8 5.7 %all-to-all-start.3 = ((bf16[8,2,128,128]{3,2,1,0:T(8,128)(2,1)}), bf16[8,2,128,128]{3,2,1,0:T(8,128)(2,1)S(1)}, u32[]{:S(2)}, u32[]{:S(2)}) async-start(bf16[8,2,128,128]{3,2,1,0:T(8,128)(2,1)} %shard_map.91), calls=%async_computation.3 | async-start | bytes 1048576 | tf_op jit(solution)/shard_map/all_to_all | solution.py:269
  101.5 1.9 %collective-permute-start.5 = (bf16[2,4,128,128]{3,2,1,0:T(8,128)(2,1)S(1)}, bf16[2,4,128,128]{3,2,1,0:T(8,128)(2,1)S(1)}, u32[]{:S(2)}, u32[]{:S(2)}) collective-permute-start(bf16[2,4,128,128]{3,2,1,0:T(8,128)(2,1)S(1)} %get-tuple-element.54), channel_id=1, source_target_pairs={{0,4},{1,13},{2,6},{3,15},{4,0},{5,9},{6,2},{7,11},{8,12},{9,5},{1... | collective-permute-start | bytes 786440 | tf_op jit(solution)/shard_map/ppermute | solution.py:375
  103.4 10.1 %collective-permute-done.5.b_ref = bf16[2,4,128,128]{3,2,1,0:T(8,128)(2,1)S(1)} collective-permute-done((bf16[2,4,128,128]{3,2,1,0:T(8,128)(2,1)S(1)}, bf16[2,4,128,128]{3,2,1,0:T(8,128)(2,1)S(1)}, u32[]{:S(2)}, u32[]{:S(2)}) %collective-permute-start.5) | collective-permute-done | bytes 262176 | tf_op jit(solution)/shard_map/ppermute | solution.py:375
  113.4 0.6 shard_map.92
  114.0 3.5 %all-to-all-done.3.in_ref = bf16[8,2,128,128]{3,2,1,0:T(8,128)(2,1)S(1)} async-done(((bf16[8,2,128,128]{3,2,1,0:T(8,128)(2,1)}), bf16[8,2,128,128]{3,2,1,0:T(8,128)(2,1)S(1)}, u32[]{:S(2)}, u32[]{:S(2)}) %all-to-all-start.3) | async-done | bytes 524320 | tf_op jit(solution)/shard_map/all_to_all | solution.py:269
  117.5 1.4 %shard_map.94 = bf16[4,2,8,128,128]{4,3,2,1,0:T(8,128)(2,1)} custom-call(bf16[8,2,128,128]{3,2,1,0:T(8,128)(2,1)S(1)} %all-to-all-done.3.in_ref), custom_call_target="tpu_custom_call" | custom-call | bytes 3145728 | tf_op jit(solution)/shard_map/pallas_call | solution.py:257
  118.9 3.6 %all-to-all-start.4 = ((bf16[4,2,8,128,128]{4,3,2,1,0:T(8,128)(2,1)}), bf16[4,2,8,128,128]{4,3,2,1,0:T(8,128)(2,1)S(1)}, u32[]{:S(2)}, u32[]{:S(2)}) async-start(bf16[4,2,8,128,128]{4,3,2,1,0:T(8,128)(2,1)} %shard_map.94), calls=%async_computation.4 | async-start | bytes 4194304 | tf_op jit(solution)/shard_map/all_to_all | solution.py:269
  122.5 2.5 %collective-permute-start.6 = (bf16[1,4,128,128]{3,2,1,0:T(8,128)(2,1)S(1)}, bf16[1,4,128,128]{3,2,1,0:T(8,128)(2,1)S(1)}, u32[]{:S(2)}, u32[]{:S(2)}) collective-permute-start(bf16[1,4,128,128]{3,2,1,0:T(8,128)(2,1)S(1)} %get-tuple-element.58), channel_id=1, source_target_pairs={{0,8},{1,9},{2,10},{3,11},{4,12},{5,13},{6,14},{7,15},{8,0},{9,1},... | collective-permute-start | bytes 393224 | tf_op jit(solution)/shard_map/ppermute | solution.py:385
  125.0 11.7 %collective-permute-done.6.b_ref = bf16[1,4,128,128]{3,2,1,0:T(8,128)(2,1)S(1)} collective-permute-done((bf16[1,4,128,128]{3,2,1,0:T(8,128)(2,1)S(1)}, bf16[1,4,128,128]{3,2,1,0:T(8,128)(2,1)S(1)}, u32[]{:S(2)}, u32[]{:S(2)}) %collective-permute-start.6) | collective-permute-done | bytes 131104 | tf_op jit(solution)/shard_map/ppermute | solution.py:385
  136.7 0.8 shard_map.93
  137.4 0.0 all-to-all-done.4.in_ref
  137.4 1.4 shard_map.95
Async XLA Ops:
  28.7 11.1 %collective-permute-start = (bf16[4,4,128,128]{3,2,1,0:T(8,128)(2,1)S(1)}, bf16[4,4,128,128]{3,2,1,0:T(8,128)(2,1)S(1)}, u32[]{:S(2)}, u32[]{:S(2)}) collective-permute-start(bf16[4,4,128,128]{3,2,1,0:T(8,128)(2,1)S(1)} %all_to_all.25.refs_0_), channel_id=1, source_target_pairs={{0,2},{1,15},{2,0},{3,5},{4,6},{5,3},{6,4},{7,9},{8,10},{9,7},{10,... | collective-permute-start | bytes 1572872 | tf_op jit(solution)/shard_map/ppermute | solution.py:336
  31.7 0.7 copy-start.3
  35.1 13.5 %copy-start = (bf16[32,128,128]{2,1,0:T(8,128)(2,1)}, bf16[32,128,128]{2,1,0:T(8,128)(2,1)S(1)}, u32[]{:S(2)}) copy-start(bf16[32,128,128]{2,1,0:T(8,128)(2,1)S(1)} %get-tuple-element.40.refs_5_.down_ref) | copy-start | bytes 3145732
  35.2 6.6 %collective-permute-start.1 = (bf16[4,4,128,128]{3,2,1,0:T(8,128)(2,1)S(1)}, bf16[4,4,128,128]{3,2,1,0:T(8,128)(2,1)}, u32[]{:S(2)}, u32[]{:S(2)}) collective-permute-start(bf16[4,4,128,128]{3,2,1,0:T(8,128)(2,1)S(1)} %all_to_all.25.refs_0_), channel_id=1, source_target_pairs={{0,1},{1,0},{2,3},{3,2},{4,5},{5,4},{6,7},{7,6},{8,9},{9,8},{10,11... | collective-permute-start | bytes 1572872 | tf_op jit(solution)/shard_map/ppermute | solution.py:338
  39.8 3.9 %collective-permute-start.2 = (bf16[4,4,128,128]{3,2,1,0:T(8,128)(2,1)S(1)}, bf16[4,4,128,128]{3,2,1,0:T(8,128)(2,1)}, u32[]{:S(2)}, u32[]{:S(2)}) collective-permute-start(bf16[4,4,128,128]{3,2,1,0:T(8,128)(2,1)S(1)} %collective-permute-done.refs_1_), channel_id=1, source_target_pairs={{0,1},{1,0},{2,3},{3,2},{4,5},{5,4},{6,7},{7,6},{8,9},{9,8},{10,11... | collective-permute-start | bytes 1572872 | tf_op jit(solution)/shard_map/ppermute | solution.py:338
  48.7 18.9 %all-to-all-start.1 = ((bf16[4,2,8,128,128]{4,3,2,1,0:T(8,128)(2,1)}), bf16[4,2,8,128,128]{4,3,2,1,0:T(8,128)(2,1)S(1)}, u32[]{:S(2)}, u32[]{:S(2)}) async-start(bf16[4,2,8,128,128]{4,3,2,1,0:T(8,128)(2,1)} %get-tuple-element.41), calls=%async_computation.1 | async-start | bytes 4194304 | tf_op jit(solution)/shard_map/all_to_all | solution.py:269
  53.1 1.2 copy-start.1
  54.3 1.0 copy-start.2
  57.2 6.7 %collective-permute-start.3 = (bf16[8,4,128,128]{3,2,1,0:T(8,128)(2,1)S(1)}, bf16[8,4,128,128]{3,2,1,0:T(8,128)(2,1)S(1)}, u32[]{:S(2)}, u32[]{:S(2)}) collective-permute-start(bf16[8,4,128,128]{3,2,1,0:T(8,128)(2,1)S(1)} %get-tuple-element.44), channel_id=1, source_target_pairs={{0,1},{1,0},{2,3},{3,2},{4,5},{5,4},{6,7},{7,6},{8,9},{9,8},{10,11... | collective-permute-start | bytes 3145736 | tf_op jit(solution)/shard_map/ppermute | solution.py:341
  68.5 26.3 %all-to-all-start.2 = ((bf16[8,2,128,128]{3,2,1,0:T(8,128)(2,1)}), bf16[8,2,128,128]{3,2,1,0:T(8,128)(2,1)S(1)}, u32[]{:S(2)}, u32[]{:S(2)}) async-start(bf16[8,2,128,128]{3,2,1,0:T(8,128)(2,1)} %shard_map.89), calls=%async_computation.2 | async-start | bytes 1048576 | tf_op jit(solution)/shard_map/all_to_all | solution.py:269
  78.6 11.1 %collective-permute-start.4 = (bf16[4,4,128,128]{3,2,1,0:T(8,128)(2,1)S(1)}, bf16[4,4,128,128]{3,2,1,0:T(8,128)(2,1)S(1)}, u32[]{:S(2)}, u32[]{:S(2)}) collective-permute-start(bf16[4,4,128,128]{3,2,1,0:T(8,128)(2,1)S(1)} %get-tuple-element.49), channel_id=1, source_target_pairs={{0,2},{1,15},{2,0},{3,5},{4,6},{5,3},{6,4},{7,9},{8,10},{9,7},{10,... | collective-permute-start | bytes 1572872 | tf_op jit(solution)/shard_map/ppermute | solution.py:364
  95.8 21.7 %all-to-all-start.3 = ((bf16[8,2,128,128]{3,2,1,0:T(8,128)(2,1)}), bf16[8,2,128,128]{3,2,1,0:T(8,128)(2,1)S(1)}, u32[]{:S(2)}, u32[]{:S(2)}) async-start(bf16[8,2,128,128]{3,2,1,0:T(8,128)(2,1)} %shard_map.91), calls=%async_computation.3 | async-start | bytes 1048576 | tf_op jit(solution)/shard_map/all_to_all | solution.py:269
  101.5 12.0 %collective-permute-start.5 = (bf16[2,4,128,128]{3,2,1,0:T(8,128)(2,1)S(1)}, bf16[2,4,128,128]{3,2,1,0:T(8,128)(2,1)S(1)}, u32[]{:S(2)}, u32[]{:S(2)}) collective-permute-start(bf16[2,4,128,128]{3,2,1,0:T(8,128)(2,1)S(1)} %get-tuple-element.54), channel_id=1, source_target_pairs={{0,4},{1,13},{2,6},{3,15},{4,0},{5,9},{6,2},{7,11},{8,12},{9,5},{1... | collective-permute-start | bytes 786440 | tf_op jit(solution)/shard_map/ppermute | solution.py:375
  118.9 18.5 %all-to-all-start.4 = ((bf16[4,2,8,128,128]{4,3,2,1,0:T(8,128)(2,1)}), bf16[4,2,8,128,128]{4,3,2,1,0:T(8,128)(2,1)S(1)}, u32[]{:S(2)}, u32[]{:S(2)}) async-start(bf16[4,2,8,128,128]{4,3,2,1,0:T(8,128)(2,1)} %shard_map.94), calls=%async_computation.4 | async-start | bytes 4194304 | tf_op jit(solution)/shard_map/all_to_all | solution.py:269
  122.5 14.1 %collective-permute-start.6 = (bf16[1,4,128,128]{3,2,1,0:T(8,128)(2,1)S(1)}, bf16[1,4,128,128]{3,2,1,0:T(8,128)(2,1)S(1)}, u32[]{:S(2)}, u32[]{:S(2)}) collective-permute-start(bf16[1,4,128,128]{3,2,1,0:T(8,128)(2,1)S(1)} %get-tuple-element.58), channel_id=1, source_target_pairs={{0,8},{1,9},{2,10},{3,11},{4,12},{5,13},{6,14},{7,15},{8,0},{9,1},... | collective-permute-start | bytes 393224 | tf_op jit(solution)/shard_map/ppermute | solution.py:385

commit v7 on v6

--- a/solution.py
+++ b/solution.py
@@ -30,7 +30,7 @@
     for j in range(2)
     for i in range(2)
 ]
-Z_GROUPS = [[2 * (2 * half + odd) + c for half in range(NZ // 2)] for odd in range(2) for c in range(2)]
+Z_GROUPS = [[2 * (2 * half + odd) + c for half in (0, 2, 1, 3)] for odd in range(2) for c in range(2)]
 CORE_SWAP = [(i, i ^ 1) for i in range(2 * NZ)]
 
 
@@ -116,7 +116,8 @@
 
     def place(s):
         col = table_ref[s]
-        return ((col >> 1) & 1) ^ core, ((col >> 2) & 1) ^ odd, col >> 3, col & 1
+        half = 2 * ((col >> 3) & 1) + (col >> 4)
+        return ((col >> 1) & 1) ^ core, ((col >> 2) & 1) ^ odd, half, col & 1
 
     hid_sum = jnp.zeros((BLK, BLK), F32)
     dac_sum = jnp.zeros((BLK, BLK), F32)

time: 141 us -> 141 us (level)
  no operation moved by 1% of the time
where the time goes in v7:
time: 141 us; the launch traced here: 139 us
  waiting for transfers between devices  47 us (33%)
  starting transfers between devices  42.8 us (30%)
  blocking collectives  27.2 us (19%)
  Pallas kernels  18 us (13%)
  local copies, waits for them, and re-layouts  2.95 us (2%)
    all_to_all x1, blocking collectives, exchange(): return lax.all_to_all(x, axis, 0, 0, tiled=True, axis_index_groups=groups)  27.2 us
    all_to_all x4, starting transfers between devices, exchange(): return lax.all_to_all(x, axis, 0, 0, tiled=True, axis_index_groups=groups)  23.8 us
    pallas_call x12, Pallas kernels, call(): pl.pallas_call(kernel, out_shape=outs, in_specs=[pl.BlockSpec(memory_spac...  18 us
    ppermute x1, waiting for transfers between devices, body(): lax.ppermute(send, 'mp', z_swap(2))  11.2 us
    all_to_all x4, waiting for transfers between devices, exchange(): return lax.all_to_all(x, axis, 0, 0, tiled=True, axis_index_groups=groups)  10.9 us
    ppermute x1, waiting for transfers between devices, body(): keep, send = halve(2, keep, lax.ppermute(send, 'mp', z_swap(1)))  10 us
    ppermute x1, waiting for transfers between devices, body(): keep, send = halve(1, keep, lax.ppermute(send, 'mp', z_swap(0)))  8.06 us
    ppermute x1, starting transfers between devices, body(): from_other = lax.ppermute(other_part, 'mp', CORE_SWAP)  4.4 us
  transfers between devices with their start and end apart: 11, of which 9 were waited for; matrix products, arithmetic and copies ran while one was open for 0% of the time, Pallas kernels for 5%

profile of v7, /device:TPU:6, one launch (start us, length us, event | category | flops | bytes accessed | tf_op | source)
XLA Modules:
  0.0 139.0 jit_solution(15560882971582549731)
XLA Ops:
  0.6 1.0 shard_map.84
  1.6 27.2 %all_to_all.25.refs_0_ = bf16[4,4,128,128]{3,2,1,0:T(8,128)(2,1)S(1)} all-to-all(bf16[4,4,128,128]{3,2,1,0:T(8,128)(2,1)S(1)} %shard_map.84), channel_id=1, replica_groups={{0,8,4,12},{1,9,5,13},{2,10,6,14},{3,11,7,15},{16,24,20,28},{17,25,21,2..., dimensions={0} | all-to-all | bytes 1048576 | tf_op jit(solution)/shard_map/all_to_all | solution.py:270
  28.9 3.0 %collective-permute-start = (bf16[4,4,128,128]{3,2,1,0:T(8,128)(2,1)S(1)}, bf16[4,4,128,128]{3,2,1,0:T(8,128)(2,1)S(1)}, u32[]{:S(2)}, u32[]{:S(2)}) collective-permute-start(bf16[4,4,128,128]{3,2,1,0:T(8,128)(2,1)S(1)} %all_to_all.25.refs_0_), channel_id=1, source_target_pairs={{0,2},{1,15},{2,0},{3,5},{4,6},{5,3},{6,4},{7,9},{8,10},{9,7},{10,... | collective-permute-start | bytes 1572872 | tf_op jit(solution)/shard_map/ppermute | solution.py:337
  31.9 0.0 copy-start.3
  31.9 0.7 copy-done.3
  32.6 2.7 %shard_map.85 = (s32[128]{0:T(128)S(1)}, bf16[32,128,128]{2,1,0:T(8,128)(2,1)S(1)}, bf16[32,128,128]{2,1,0:T(8,128)(2,1)S(1)}) custom-call(s32[8,32]{1,0:T(8,128)S(1)} %copy-done.3, bf16[32,128,128]{2,1,0:T(8,128)(2,1)} %up_hbm.1, bf16[32,128,128]{2,1,0:T(8,128)(2,1)} %down_hbm.1), custom_call_target="tpu_custom_call" | custom-call | flops 1048576 | bytes 4194304 | tf_op jit(solution)/shard_map/pallas_call | solution.py:258
  35.3 0.0 copy-start
  35.3 1.9 %collective-permute-start.1 = (bf16[4,4,128,128]{3,2,1,0:T(8,128)(2,1)S(1)}, bf16[4,4,128,128]{3,2,1,0:T(8,128)(2,1)}, u32[]{:S(2)}, u32[]{:S(2)}) collective-permute-start(bf16[4,4,128,128]{3,2,1,0:T(8,128)(2,1)S(1)} %all_to_all.25.refs_0_), channel_id=1, source_target_pairs={{0,1},{1,0},{2,3},{3,2},{4,5},{5,4},{6,7},{7,6},{8,9},{9,8},{10,11... | collective-permute-start | bytes 1572872 | tf_op jit(solution)/shard_map/ppermute | solution.py:339
  37.3 2.7 %collective-permute-done.refs_1_ = bf16[4,4,128,128]{3,2,1,0:T(8,128)(2,1)S(1)} collective-permute-done((bf16[4,4,128,128]{3,2,1,0:T(8,128)(2,1)S(1)}, bf16[4,4,128,128]{3,2,1,0:T(8,128)(2,1)S(1)}, u32[]{:S(2)}, u32[]{:S(2)}) %collective-permute-start) | collective-permute-done | bytes 524320 | tf_op jit(solution)/shard_map/ppermute | solution.py:337
  39.9 1.9 %collective-permute-start.2 = (bf16[4,4,128,128]{3,2,1,0:T(8,128)(2,1)S(1)}, bf16[4,4,128,128]{3,2,1,0:T(8,128)(2,1)}, u32[]{:S(2)}, u32[]{:S(2)}) collective-permute-start(bf16[4,4,128,128]{3,2,1,0:T(8,128)(2,1)S(1)} %collective-permute-done.refs_1_), channel_id=1, source_target_pairs={{0,1},{1,0},{2,3},{3,2},{4,5},{5,4},{6,7},{7,6},{8,9},{9,8},{10,11... | collective-permute-start | bytes 1572872 | tf_op jit(solution)/shard_map/ppermute | solution.py:339
  41.9 0.1 pad_add_fusion.place_ref
  41.9 0.0 collective-permute-done.1.refs_2_
  41.9 1.9 %collective-permute-done.2.refs_3_ = bf16[4,4,128,128]{3,2,1,0:T(8,128)(2,1)} collective-permute-done((bf16[4,4,128,128]{3,2,1,0:T(8,128)(2,1)S(1)}, bf16[4,4,128,128]{3,2,1,0:T(8,128)(2,1)}, u32[]{:S(2)}, u32[]{:S(2)}) %collective-permute-start.2) | collective-permute-done | bytes 524320 | tf_op jit(solution)/shard_map/ppermute | solution.py:339
  43.9 5.0 %shard_map.86 = (bf16[4,2,8,128,128]{4,3,2,1,0:T(8,128)(2,1)}, bf16[2,8,128,128]{3,2,1,0:T(8,128)(2,1)}) custom-call(s32[128]{0:T(128)S(1)} %get-tuple-element.37.table_ref, s32[2]{0:T(128)S(1)} %pad_add_fusion.place_ref, bf16[4,4,128,128]{3,2,1,0:T(8,128)(2,1)S(1)} %all_to_all.25.refs_0_, bf16[4,4,128,128]{3,2,1,0:T(8,128)(2,1)S(1)} %collective-permute-done.refs_1_, ...), custom_call_target="tpu_custom_call" | custom-call | flops 536870912 | bytes 6291456 | tf_op jit(solution)/shard_map/pallas_call | solution.py:258
  48.8 0.0 copy-done
  48.9 4.4 %all-to-all-start.1 = ((bf16[4,2,8,128,128]{4,3,2,1,0:T(8,128)(2,1)}), bf16[4,2,8,128,128]{4,3,2,1,0:T(8,128)(2,1)S(1)}, u32[]{:S(2)}, u32[]{:S(2)}) async-start(bf16[4,2,8,128,128]{4,3,2,1,0:T(8,128)(2,1)} %get-tuple-element.41), calls=%async_computation.1 | async-start | bytes 4194304 | tf_op jit(solution)/shard_map/all_to_all | solution.py:270
  53.3 0.0 copy-start.1
  53.3 1.2 copy-done.1
  54.5 0.0 copy-start.2
  54.5 1.0 copy-done.2
  55.5 1.9 %shard_map.87 = (bf16[8,4,128,128]{3,2,1,0:T(8,128)(2,1)S(1)}, bf16[8,4,128,128]{3,2,1,0:T(8,128)(2,1)S(1)}) custom-call(s32[128]{0:T(128)S(1)} %get-tuple-element.37.table_ref, s32[2]{0:T(128)S(1)} %pad_add_fusion.place_ref, bf16[2,8,128,128]{3,2,1,0:T(8,128)(2,1)S(1)} %copy-done.2, bf16[32,128,128]{2,1,0:T(8,128)(2,1)S(1)} %get-tuple-element.39.refs_4_.up_ref, ...), custom_call_target="tpu_custom_call" | custom-call | flops 268435456 | bytes 5242880 | tf_op jit(solution)/shard_map/pallas_call | solution.py:258
  57.4 4.4 %collective-permute-start.3 = (bf16[8,4,128,128]{3,2,1,0:T(8,128)(2,1)S(1)}, bf16[8,4,128,128]{3,2,1,0:T(8,128)(2,1)S(1)}, u32[]{:S(2)}, u32[]{:S(2)}) collective-permute-start(bf16[8,4,128,128]{3,2,1,0:T(8,128)(2,1)S(1)} %get-tuple-element.44), channel_id=1, source_target_pairs={{0,1},{1,0},{2,3},{3,2},{4,5},{5,4},{6,7},{7,6},{8,9},{9,8},{10,11... | collective-permute-start | bytes 3145736 | tf_op jit(solution)/shard_map/ppermute | solution.py:342
  61.8 2.3 %collective-permute-done.3.b_ref = bf16[8,4,128,128]{3,2,1,0:T(8,128)(2,1)S(1)} collective-permute-done((bf16[8,4,128,128]{3,2,1,0:T(8,128)(2,1)S(1)}, bf16[8,4,128,128]{3,2,1,0:T(8,128)(2,1)S(1)}, u32[]{:S(2)}, u32[]{:S(2)}) %collective-permute-start.3) | collective-permute-done | bytes 1048608 | tf_op jit(solution)/shard_map/ppermute | solution.py:342
  64.1 0.8 shard_map.88
  64.9 2.9 %all-to-all-done.1.in_ref = bf16[4,2,8,128,128]{4,3,2,1,0:T(8,128)(2,1)S(1)} async-done(((bf16[4,2,8,128,128]{4,3,2,1,0:T(8,128)(2,1)}), bf16[4,2,8,128,128]{4,3,2,1,0:T(8,128)(2,1)S(1)}, u32[]{:S(2)}, u32[]{:S(2)}) %all-to-all-start.1) | async-done | bytes 2097184 | tf_op jit(solution)/shard_map/all_to_all | solution.py:270
  67.8 1.0 shard_map.89
  68.7 10.1 %all-to-all-start.2 = ((bf16[8,2,128,128]{3,2,1,0:T(8,128)(2,1)}), bf16[8,2,128,128]{3,2,1,0:T(8,128)(2,1)S(1)}, u32[]{:S(2)}, u32[]{:S(2)}) async-start(bf16[8,2,128,128]{3,2,1,0:T(8,128)(2,1)} %shard_map.89), calls=%async_computation.2 | async-start | bytes 1048576 | tf_op jit(solution)/shard_map/all_to_all | solution.py:270
  78.8 3.0 %collective-permute-start.4 = (bf16[4,4,128,128]{3,2,1,0:T(8,128)(2,1)S(1)}, bf16[4,4,128,128]{3,2,1,0:T(8,128)(2,1)S(1)}, u32[]{:S(2)}, u32[]{:S(2)}) collective-permute-start(bf16[4,4,128,128]{3,2,1,0:T(8,128)(2,1)S(1)} %get-tuple-element.49), channel_id=1, source_target_pairs={{0,2},{1,15},{2,0},{3,5},{4,6},{5,3},{6,4},{7,9},{8,10},{9,7},{10,... | collective-permute-start | bytes 1572872 | tf_op jit(solution)/shard_map/ppermute | solution.py:365
  81.8 8.1 %collective-permute-done.4.b_ref = bf16[4,4,128,128]{3,2,1,0:T(8,128)(2,1)S(1)} collective-permute-done((bf16[4,4,128,128]{3,2,1,0:T(8,128)(2,1)S(1)}, bf16[4,4,128,128]{3,2,1,0:T(8,128)(2,1)S(1)}, u32[]{:S(2)}, u32[]{:S(2)}) %collective-permute-start.4) | collective-permute-done | bytes 524320 | tf_op jit(solution)/shard_map/ppermute | solution.py:365
  89.9 0.7 shard_map.90
  90.5 4.5 %all-to-all-done.2.in_ref = bf16[8,2,128,128]{3,2,1,0:T(8,128)(2,1)S(1)} async-done(((bf16[8,2,128,128]{3,2,1,0:T(8,128)(2,1)}), bf16[8,2,128,128]{3,2,1,0:T(8,128)(2,1)S(1)}, u32[]{:S(2)}, u32[]{:S(2)}) %all-to-all-start.2) | async-done | bytes 524320 | tf_op jit(solution)/shard_map/all_to_all | solution.py:270
  95.0 0.9 shard_map.91
  96.0 5.7 %all-to-all-start.3 = ((bf16[8,2,128,128]{3,2,1,0:T(8,128)(2,1)}), bf16[8,2,128,128]{3,2,1,0:T(8,128)(2,1)S(1)}, u32[]{:S(2)}, u32[]{:S(2)}) async-start(bf16[8,2,128,128]{3,2,1,0:T(8,128)(2,1)} %shard_map.91), calls=%async_computation.3 | async-start | bytes 1048576 | tf_op jit(solution)/shard_map/all_to_all | solution.py:270
  101.7 1.9 %collective-permute-start.5 = (bf16[2,4,128,128]{3,2,1,0:T(8,128)(2,1)S(1)}, bf16[2,4,128,128]{3,2,1,0:T(8,128)(2,1)S(1)}, u32[]{:S(2)}, u32[]{:S(2)}) collective-permute-start(bf16[2,4,128,128]{3,2,1,0:T(8,128)(2,1)S(1)} %get-tuple-element.54), channel_id=1, source_target_pairs={{0,4},{1,13},{2,6},{3,15},{4,0},{5,9},{6,2},{7,11},{8,12},{9,5},{1... | collective-permute-start | bytes 786440 | tf_op jit(solution)/shard_map/ppermute | solution.py:376
  103.6 10.0 %collective-permute-done.5.b_ref = bf16[2,4,128,128]{3,2,1,0:T(8,128)(2,1)S(1)} collective-permute-done((bf16[2,4,128,128]{3,2,1,0:T(8,128)(2,1)S(1)}, bf16[2,4,128,128]{3,2,1,0:T(8,128)(2,1)S(1)}, u32[]{:S(2)}, u32[]{:S(2)}) %collective-permute-start.5) | collective-permute-done | bytes 262176 | tf_op jit(solution)/shard_map/ppermute | solution.py:376
  113.6 0.6 shard_map.92
  114.2 3.5 %all-to-all-done.3.in_ref = bf16[8,2,128,128]{3,2,1,0:T(8,128)(2,1)S(1)} async-done(((bf16[8,2,128,128]{3,2,1,0:T(8,128)(2,1)}), bf16[8,2,128,128]{3,2,1,0:T(8,128)(2,1)S(1)}, u32[]{:S(2)}, u32[]{:S(2)}) %all-to-all-start.3) | async-done | bytes 524320 | tf_op jit(solution)/shard_map/all_to_all | solution.py:270
  117.7 1.4 %shard_map.94 = bf16[4,2,8,128,128]{4,3,2,1,0:T(8,128)(2,1)} custom-call(bf16[8,2,128,128]{3,2,1,0:T(8,128)(2,1)S(1)} %all-to-all-done.3.in_ref), custom_call_target="tpu_custom_call" | custom-call | bytes 3145728 | tf_op jit(solution)/shard_map/pallas_call | solution.py:258
  119.1 3.6 %all-to-all-start.4 = ((bf16[4,2,8,128,128]{4,3,2,1,0:T(8,128)(2,1)}), bf16[4,2,8,128,128]{4,3,2,1,0:T(8,128)(2,1)S(1)}, u32[]{:S(2)}, u32[]{:S(2)}) async-start(bf16[4,2,8,128,128]{4,3,2,1,0:T(8,128)(2,1)} %shard_map.94), calls=%async_computation.4 | async-start | bytes 4194304 | tf_op jit(solution)/shard_map/all_to_all | solution.py:270
  122.7 2.9 %collective-permute-start.6 = (bf16[1,4,128,128]{3,2,1,0:T(8,128)(2,1)S(1)}, bf16[1,4,128,128]{3,2,1,0:T(8,128)(2,1)S(1)}, u32[]{:S(2)}, u32[]{:S(2)}) collective-permute-start(bf16[1,4,128,128]{3,2,1,0:T(8,128)(2,1)S(1)} %get-tuple-element.58), channel_id=1, source_target_pairs={{0,8},{1,9},{2,10},{3,11},{4,12},{5,13},{6,14},{7,15},{8,0},{9,1},... | collective-permute-start | bytes 393224 | tf_op jit(solution)/shard_map/ppermute | solution.py:386
  125.7 11.2 %collective-permute-done.6.b_ref = bf16[1,4,128,128]{3,2,1,0:T(8,128)(2,1)S(1)} collective-permute-done((bf16[1,4,128,128]{3,2,1,0:T(8,128)(2,1)S(1)}, bf16[1,4,128,128]{3,2,1,0:T(8,128)(2,1)S(1)}, u32[]{:S(2)}, u32[]{:S(2)}) %collective-permute-start.6) | collective-permute-done | bytes 131104 | tf_op jit(solution)/shard_map/ppermute | solution.py:386
  136.9 0.8 shard_map.93
  137.6 0.0 all-to-all-done.4.in_ref
  137.6 1.4 shard_map.95
Async XLA Ops:
  28.9 11.1 %collective-permute-start = (bf16[4,4,128,128]{3,2,1,0:T(8,128)(2,1)S(1)}, bf16[4,4,128,128]{3,2,1,0:T(8,128)(2,1)S(1)}, u32[]{:S(2)}, u32[]{:S(2)}) collective-permute-start(bf16[4,4,128,128]{3,2,1,0:T(8,128)(2,1)S(1)} %all_to_all.25.refs_0_), channel_id=1, source_target_pairs={{0,2},{1,15},{2,0},{3,5},{4,6},{5,3},{6,4},{7,9},{8,10},{9,7},{10,... | collective-permute-start | bytes 1572872 | tf_op jit(solution)/shard_map/ppermute | solution.py:337
  31.9 0.7 copy-start.3
  35.3 13.5 %copy-start = (bf16[32,128,128]{2,1,0:T(8,128)(2,1)}, bf16[32,128,128]{2,1,0:T(8,128)(2,1)S(1)}, u32[]{:S(2)}) copy-start(bf16[32,128,128]{2,1,0:T(8,128)(2,1)S(1)} %get-tuple-element.40.refs_5_.down_ref) | copy-start | bytes 3145732
  35.3 6.6 %collective-permute-start.1 = (bf16[4,4,128,128]{3,2,1,0:T(8,128)(2,1)S(1)}, bf16[4,4,128,128]{3,2,1,0:T(8,128)(2,1)}, u32[]{:S(2)}, u32[]{:S(2)}) collective-permute-start(bf16[4,4,128,128]{3,2,1,0:T(8,128)(2,1)S(1)} %all_to_all.25.refs_0_), channel_id=1, source_target_pairs={{0,1},{1,0},{2,3},{3,2},{4,5},{5,4},{6,7},{7,6},{8,9},{9,8},{10,11... | collective-permute-start | bytes 1572872 | tf_op jit(solution)/shard_map/ppermute | solution.py:339
  39.9 3.9 %collective-permute-start.2 = (bf16[4,4,128,128]{3,2,1,0:T(8,128)(2,1)S(1)}, bf16[4,4,128,128]{3,2,1,0:T(8,128)(2,1)}, u32[]{:S(2)}, u32[]{:S(2)}) collective-permute-start(bf16[4,4,128,128]{3,2,1,0:T(8,128)(2,1)S(1)} %collective-permute-done.refs_1_), channel_id=1, source_target_pairs={{0,1},{1,0},{2,3},{3,2},{4,5},{5,4},{6,7},{7,6},{8,9},{9,8},{10,11... | collective-permute-start | bytes 1572872 | tf_op jit(solution)/shard_map/ppermute | solution.py:339
  48.9 18.9 %all-to-all-start.1 = ((bf16[4,2,8,128,128]{4,3,2,1,0:T(8,128)(2,1)}), bf16[4,2,8,128,128]{4,3,2,1,0:T(8,128)(2,1)S(1)}, u32[]{:S(2)}, u32[]{:S(2)}) async-start(bf16[4,2,8,128,128]{4,3,2,1,0:T(8,128)(2,1)} %get-tuple-element.41), calls=%async_computation.1 | async-start | bytes 4194304 | tf_op jit(solution)/shard_map/all_to_all | solution.py:270
  53.3 1.2 copy-start.1
  54.5 1.0 copy-start.2
  57.4 6.7 %collective-permute-start.3 = (bf16[8,4,128,128]{3,2,1,0:T(8,128)(2,1)S(1)}, bf16[8,4,128,128]{3,2,1,0:T(8,128)(2,1)S(1)}, u32[]{:S(2)}, u32[]{:S(2)}) collective-permute-start(bf16[8,4,128,128]{3,2,1,0:T(8,128)(2,1)S(1)} %get-tuple-element.44), channel_id=1, source_target_pairs={{0,1},{1,0},{2,3},{3,2},{4,5},{5,4},{6,7},{7,6},{8,9},{9,8},{10,11... | collective-permute-start | bytes 3145736 | tf_op jit(solution)/shard_map/ppermute | solution.py:342
  68.7 26.3 %all-to-all-start.2 = ((bf16[8,2,128,128]{3,2,1,0:T(8,128)(2,1)}), bf16[8,2,128,128]{3,2,1,0:T(8,128)(2,1)S(1)}, u32[]{:S(2)}, u32[]{:S(2)}) async-start(bf16[8,2,128,128]{3,2,1,0:T(8,128)(2,1)} %shard_map.89), calls=%async_computation.2 | async-start | bytes 1048576 | tf_op jit(solution)/shard_map/all_to_all | solution.py:270
  78.8 11.1 %collective-permute-start.4 = (bf16[4,4,128,128]{3,2,1,0:T(8,128)(2,1)S(1)}, bf16[4,4,128,128]{3,2,1,0:T(8,128)(2,1)S(1)}, u32[]{:S(2)}, u32[]{:S(2)}) collective-permute-start(bf16[4,4,128,128]{3,2,1,0:T(8,128)(2,1)S(1)} %get-tuple-element.49), channel_id=1, source_target_pairs={{0,2},{1,15},{2,0},{3,5},{4,6},{5,3},{6,4},{7,9},{8,10},{9,7},{10,... | collective-permute-start | bytes 1572872 | tf_op jit(solution)/shard_map/ppermute | solution.py:365
  96.0 21.7 %all-to-all-start.3 = ((bf16[8,2,128,128]{3,2,1,0:T(8,128)(2,1)}), bf16[8,2,128,128]{3,2,1,0:T(8,128)(2,1)S(1)}, u32[]{:S(2)}, u32[]{:S(2)}) async-start(bf16[8,2,128,128]{3,2,1,0:T(8,128)(2,1)} %shard_map.91), calls=%async_computation.3 | async-start | bytes 1048576 | tf_op jit(solution)/shard_map/all_to_all | solution.py:270
  101.7 12.0 %collective-permute-start.5 = (bf16[2,4,128,128]{3,2,1,0:T(8,128)(2,1)S(1)}, bf16[2,4,128,128]{3,2,1,0:T(8,128)(2,1)S(1)}, u32[]{:S(2)}, u32[]{:S(2)}) collective-permute-start(bf16[2,4,128,128]{3,2,1,0:T(8,128)(2,1)S(1)} %get-tuple-element.54), channel_id=1, source_target_pairs={{0,4},{1,13},{2,6},{3,15},{4,0},{5,9},{6,2},{7,11},{8,12},{9,5},{1... | collective-permute-start | bytes 786440 | tf_op jit(solution)/shard_map/ppermute | solution.py:376
  119.1 18.5 %all-to-all-start.4 = ((bf16[4,2,8,128,128]{4,3,2,1,0:T(8,128)(2,1)}), bf16[4,2,8,128,128]{4,3,2,1,0:T(8,128)(2,1)S(1)}, u32[]{:S(2)}, u32[]{:S(2)}) async-start(bf16[4,2,8,128,128]{4,3,2,1,0:T(8,128)(2,1)} %shard_map.94), calls=%async_computation.4 | async-start | bytes 4194304 | tf_op jit(solution)/shard_map/all_to_all | solution.py:270
  122.7 14.1 %collective-permute-start.6 = (bf16[1,4,128,128]{3,2,1,0:T(8,128)(2,1)S(1)}, bf16[1,4,128,128]{3,2,1,0:T(8,128)(2,1)S(1)}, u32[]{:S(2)}, u32[]{:S(2)}) collective-permute-start(bf16[1,4,128,128]{3,2,1,0:T(8,128)(2,1)S(1)} %get-tuple-element.58), channel_id=1, source_target_pairs={{0,8},{1,9},{2,10},{3,11},{4,12},{5,13},{6,14},{7,15},{8,0},{9,1},... | collective-permute-start | bytes 393224 | tf_op jit(solution)/shard_map/ppermute | solution.py:386

commit v8 on v5

--- a/solution.py
+++ b/solution.py
@@ -145,9 +145,8 @@
         down_part = nn(acts[0, row], panels[side, other, half, 2 + j])
         grads[s // 8, 0, s % 8] = jnp.where(used, up_part, 0.0).astype(BF)
         grads[s // 8, 1, s % 8] = jnp.where(used, down_part, 0.0).astype(BF)
-        if s % 4 == 3:
-            ready = (s // 8, slice(None), pl.ds(s % 8 - 3, 4))
-            copies.append(pltpu.make_async_copy(grads.at[ready], grads_hbm.at[ready], sems.at[s // 4]))
+        if s % 8 == 7:
+            copies.append(pltpu.make_async_copy(grads.at[s // 8], grads_hbm.at[s // 8], sems.at[s // 8]))
             copies[-1].start()
     for copy in copies:
         copy.wait()
@@ -272,7 +271,7 @@
             pltpu.VMEM((ROWS, BLK, BLK), F32),
             pltpu.VMEM((4, 2, 8, BLK, BLK), BF),
             pltpu.VMEM((2, ROWS, BLK, BLK), BF),
-            pltpu.SemaphoreType.DMA((8,)),
+            pltpu.SemaphoreType.DMA((4,)),
             pltpu.SemaphoreType.DMA,
         ],
         ins=[pltpu.SMEM] * 2 + [pltpu.VMEM] * 6,

time: 141 us -> 141 us (level)
  no operation moved by 1% of the time
where the time goes in v8:
time: 141 us; the launch traced here: 139 us
  waiting for transfers between devices  47.5 us (34%)
  starting transfers between devices  42.4 us (30%)
  blocking collectives  27.1 us (19%)
  Pallas kernels  18.1 us (13%)
  local copies, waits for them, and re-layouts  2.95 us (2%)
    all_to_all x1, blocking collectives, exchange(): return lax.all_to_all(x, axis, 0, 0, tiled=True, axis_index_groups=groups)  27.1 us
    all_to_all x4, starting transfers between devices, exchange(): return lax.all_to_all(x, axis, 0, 0, tiled=True, axis_index_groups=groups)  23.8 us
    pallas_call x12, Pallas kernels, call(): pl.pallas_call(kernel, out_shape=outs, in_specs=[pl.BlockSpec(memory_spac...  18.1 us
    ppermute x1, waiting for transfers between devices, body(): lax.ppermute(send, 'mp', z_swap(2))  11.7 us
    all_to_all x4, waiting for transfers between devices, exchange(): return lax.all_to_all(x, axis, 0, 0, tiled=True, axis_index_groups=groups)  10.9 us
    ppermute x1, waiting for transfers between devices, body(): keep, send = halve(2, keep, lax.ppermute(send, 'mp', z_swap(1)))  10.1 us
    ppermute x1, waiting for transfers between devices, body(): keep, send = halve(1, keep, lax.ppermute(send, 'mp', z_swap(0)))  8.07 us
    ppermute x1, starting transfers between devices, body(): from_other = lax.ppermute(other_part, 'mp', CORE_SWAP)  4.42 us
  transfers between devices with their start and end apart: 11, of which 9 were waited for; matrix products, arithmetic and copies ran while one was open for 0% of the time, Pallas kernels for 5%

profile of v8, /device:TPU:6, one launch (start us, length us, event | category | flops | bytes accessed | tf_op | source)
XLA Modules:
  0.0 138.9 jit_solution(12357088637065778701)
XLA Ops:
  0.6 1.0 shard_map.84
  1.6 27.1 %all_to_all.25.refs_0_ = bf16[4,4,128,128]{3,2,1,0:T(8,128)(2,1)S(1)} all-to-all(bf16[4,4,128,128]{3,2,1,0:T(8,128)(2,1)S(1)} %shard_map.84), channel_id=1, replica_groups={{0,4,8,12},{1,5,9,13},{2,6,10,14},{3,7,11,15},{16,20,24,28},{17,21,25,2..., dimensions={0} | all-to-all | bytes 1048576 | tf_op jit(solution)/shard_map/all_to_all | solution.py:260
  28.7 3.0 %collective-permute-start = (bf16[4,4,128,128]{3,2,1,0:T(8,128)(2,1)S(1)}, bf16[4,4,128,128]{3,2,1,0:T(8,128)(2,1)S(1)}, u32[]{:S(2)}, u32[]{:S(2)}) collective-permute-start(bf16[4,4,128,128]{3,2,1,0:T(8,128)(2,1)S(1)} %all_to_all.25.refs_0_), channel_id=1, source_target_pairs={{0,2},{1,15},{2,0},{3,5},{4,6},{5,3},{6,4},{7,9},{8,10},{9,7},{10,... | collective-permute-start | bytes 1572872 | tf_op jit(solution)/shard_map/ppermute | solution.py:327
  31.7 0.0 copy-start.3
  31.7 0.7 copy-done.3
  32.4 2.7 %shard_map.85 = (s32[128]{0:T(128)S(1)}, bf16[32,128,128]{2,1,0:T(8,128)(2,1)S(1)}, bf16[32,128,128]{2,1,0:T(8,128)(2,1)S(1)}) custom-call(s32[8,32]{1,0:T(8,128)S(1)} %copy-done.3, bf16[32,128,128]{2,1,0:T(8,128)(2,1)} %up_hbm.1, bf16[32,128,128]{2,1,0:T(8,128)(2,1)} %down_hbm.1), custom_call_target="tpu_custom_call" | custom-call | flops 1048576 | bytes 4194304 | tf_op jit(solution)/shard_map/pallas_call | solution.py:248
  35.1 0.0 copy-start
  35.2 1.9 %collective-permute-start.1 = (bf16[4,4,128,128]{3,2,1,0:T(8,128)(2,1)S(1)}, bf16[4,4,128,128]{3,2,1,0:T(8,128)(2,1)}, u32[]{:S(2)}, u32[]{:S(2)}) collective-permute-start(bf16[4,4,128,128]{3,2,1,0:T(8,128)(2,1)S(1)} %all_to_all.25.refs_0_), channel_id=1, source_target_pairs={{0,1},{1,0},{2,3},{3,2},{4,5},{5,4},{6,7},{7,6},{8,9},{9,8},{10,11... | collective-permute-start | bytes 1572872 | tf_op jit(solution)/shard_map/ppermute | solution.py:329
  37.1 2.7 %collective-permute-done.refs_1_ = bf16[4,4,128,128]{3,2,1,0:T(8,128)(2,1)S(1)} collective-permute-done((bf16[4,4,128,128]{3,2,1,0:T(8,128)(2,1)S(1)}, bf16[4,4,128,128]{3,2,1,0:T(8,128)(2,1)S(1)}, u32[]{:S(2)}, u32[]{:S(2)}) %collective-permute-start) | collective-permute-done | bytes 524320 | tf_op jit(solution)/shard_map/ppermute | solution.py:327
  39.8 1.9 %collective-permute-start.2 = (bf16[4,4,128,128]{3,2,1,0:T(8,128)(2,1)S(1)}, bf16[4,4,128,128]{3,2,1,0:T(8,128)(2,1)}, u32[]{:S(2)}, u32[]{:S(2)}) collective-permute-start(bf16[4,4,128,128]{3,2,1,0:T(8,128)(2,1)S(1)} %collective-permute-done.refs_1_), channel_id=1, source_target_pairs={{0,1},{1,0},{2,3},{3,2},{4,5},{5,4},{6,7},{7,6},{8,9},{9,8},{10,11... | collective-permute-start | bytes 1572872 | tf_op jit(solution)/shard_map/ppermute | solution.py:329
  41.7 0.1 pad_add_fusion.place_ref
  41.8 0.0 collective-permute-done.1.refs_2_
  41.8 1.9 %collective-permute-done.2.refs_3_ = bf16[4,4,128,128]{3,2,1,0:T(8,128)(2,1)} collective-permute-done((bf16[4,4,128,128]{3,2,1,0:T(8,128)(2,1)S(1)}, bf16[4,4,128,128]{3,2,1,0:T(8,128)(2,1)}, u32[]{:S(2)}, u32[]{:S(2)}) %collective-permute-start.2) | collective-permute-done | bytes 524320 | tf_op jit(solution)/shard_map/ppermute | solution.py:329
  43.7 5.0 %shard_map.86 = (bf16[4,2,8,128,128]{4,3,2,1,0:T(8,128)(2,1)}, bf16[2,8,128,128]{3,2,1,0:T(8,128)(2,1)}) custom-call(s32[128]{0:T(128)S(1)} %get-tuple-element.37.table_ref, s32[2]{0:T(128)S(1)} %pad_add_fusion.place_ref, bf16[4,4,128,128]{3,2,1,0:T(8,128)(2,1)S(1)} %all_to_all.25.refs_0_, bf16[4,4,128,128]{3,2,1,0:T(8,128)(2,1)S(1)} %collective-permute-done.refs_1_, ...), custom_call_target="tpu_custom_call" | custom-call | flops 536870912 | bytes 6291456 | tf_op jit(solution)/shard_map/pallas_call | solution.py:248
  48.7 0.0 copy-done
  48.7 4.4 %all-to-all-start.1 = ((bf16[4,2,8,128,128]{4,3,2,1,0:T(8,128)(2,1)}), bf16[4,2,8,128,128]{4,3,2,1,0:T(8,128)(2,1)S(1)}, u32[]{:S(2)}, u32[]{:S(2)}) async-start(bf16[4,2,8,128,128]{4,3,2,1,0:T(8,128)(2,1)} %get-tuple-element.41), calls=%async_computation.1 | async-start | bytes 4194304 | tf_op jit(solution)/shard_map/all_to_all | solution.py:260
  53.1 0.0 copy-start.1
  53.1 1.2 copy-done.1
  54.3 0.0 copy-start.2
  54.3 1.0 copy-done.2
  55.4 1.9 %shard_map.87 = (bf16[8,4,128,128]{3,2,1,0:T(8,128)(2,1)S(1)}, bf16[8,4,128,128]{3,2,1,0:T(8,128)(2,1)S(1)}) custom-call(s32[128]{0:T(128)S(1)} %get-tuple-element.37.table_ref, s32[2]{0:T(128)S(1)} %pad_add_fusion.place_ref, bf16[2,8,128,128]{3,2,1,0:T(8,128)(2,1)S(1)} %copy-done.2, bf16[32,128,128]{2,1,0:T(8,128)(2,1)S(1)} %get-tuple-element.39.refs_4_.up_ref, ...), custom_call_target="tpu_custom_call" | custom-call | flops 268435456 | bytes 5242880 | tf_op jit(solution)/shard_map/pallas_call | solution.py:248
  57.2 4.4 %collective-permute-start.3 = (bf16[8,4,128,128]{3,2,1,0:T(8,128)(2,1)S(1)}, bf16[8,4,128,128]{3,2,1,0:T(8,128)(2,1)S(1)}, u32[]{:S(2)}, u32[]{:S(2)}) collective-permute-start(bf16[8,4,128,128]{3,2,1,0:T(8,128)(2,1)S(1)} %get-tuple-element.44), channel_id=1, source_target_pairs={{0,1},{1,0},{2,3},{3,2},{4,5},{5,4},{6,7},{7,6},{8,9},{9,8},{10,11... | collective-permute-start | bytes 3145736 | tf_op jit(solution)/shard_map/ppermute | solution.py:332
  61.7 2.3 %collective-permute-done.3.b_ref = bf16[8,4,128,128]{3,2,1,0:T(8,128)(2,1)S(1)} collective-permute-done((bf16[8,4,128,128]{3,2,1,0:T(8,128)(2,1)S(1)}, bf16[8,4,128,128]{3,2,1,0:T(8,128)(2,1)S(1)}, u32[]{:S(2)}, u32[]{:S(2)}) %collective-permute-start.3) | collective-permute-done | bytes 1048608 | tf_op jit(solution)/shard_map/ppermute | solution.py:332
  63.9 0.8 shard_map.88
  64.7 2.9 %all-to-all-done.1.in_ref = bf16[4,2,8,128,128]{4,3,2,1,0:T(8,128)(2,1)S(1)} async-done(((bf16[4,2,8,128,128]{4,3,2,1,0:T(8,128)(2,1)}), bf16[4,2,8,128,128]{4,3,2,1,0:T(8,128)(2,1)S(1)}, u32[]{:S(2)}, u32[]{:S(2)}) %all-to-all-start.1) | async-done | bytes 2097184 | tf_op jit(solution)/shard_map/all_to_all | solution.py:260
  67.6 1.0 shard_map.89
  68.7 10.1 %all-to-all-start.2 = ((bf16[8,2,128,128]{3,2,1,0:T(8,128)(2,1)}), bf16[8,2,128,128]{3,2,1,0:T(8,128)(2,1)S(1)}, u32[]{:S(2)}, u32[]{:S(2)}) async-start(bf16[8,2,128,128]{3,2,1,0:T(8,128)(2,1)} %shard_map.89), calls=%async_computation.2 | async-start | bytes 1048576 | tf_op jit(solution)/shard_map/all_to_all | solution.py:260
  78.7 3.0 %collective-permute-start.4 = (bf16[4,4,128,128]{3,2,1,0:T(8,128)(2,1)S(1)}, bf16[4,4,128,128]{3,2,1,0:T(8,128)(2,1)S(1)}, u32[]{:S(2)}, u32[]{:S(2)}) collective-permute-start(bf16[4,4,128,128]{3,2,1,0:T(8,128)(2,1)S(1)} %get-tuple-element.49), channel_id=1, source_target_pairs={{0,2},{1,15},{2,0},{3,5},{4,6},{5,3},{6,4},{7,9},{8,10},{9,7},{10,... | collective-permute-start | bytes 1572872 | tf_op jit(solution)/shard_map/ppermute | solution.py:348
  81.7 8.1 %collective-permute-done.4.b_ref = bf16[4,4,128,128]{3,2,1,0:T(8,128)(2,1)S(1)} collective-permute-done((bf16[4,4,128,128]{3,2,1,0:T(8,128)(2,1)S(1)}, bf16[4,4,128,128]{3,2,1,0:T(8,128)(2,1)S(1)}, u32[]{:S(2)}, u32[]{:S(2)}) %collective-permute-start.4) | collective-permute-done | bytes 524320 | tf_op jit(solution)/shard_map/ppermute | solution.py:348
  89.8 0.7 shard_map.90
  90.5 4.5 %all-to-all-done.2.in_ref = bf16[8,2,128,128]{3,2,1,0:T(8,128)(2,1)S(1)} async-done(((bf16[8,2,128,128]{3,2,1,0:T(8,128)(2,1)}), bf16[8,2,128,128]{3,2,1,0:T(8,128)(2,1)S(1)}, u32[]{:S(2)}, u32[]{:S(2)}) %all-to-all-start.2) | async-done | bytes 524320 | tf_op jit(solution)/shard_map/all_to_all | solution.py:260
  95.0 0.9 shard_map.91
  95.8 5.7 %all-to-all-start.3 = ((bf16[8,2,128,128]{3,2,1,0:T(8,128)(2,1)}), bf16[8,2,128,128]{3,2,1,0:T(8,128)(2,1)S(1)}, u32[]{:S(2)}, u32[]{:S(2)}) async-start(bf16[8,2,128,128]{3,2,1,0:T(8,128)(2,1)} %shard_map.91), calls=%async_computation.3 | async-start | bytes 1048576 | tf_op jit(solution)/shard_map/all_to_all | solution.py:260
  101.5 1.9 %collective-permute-start.5 = (bf16[2,4,128,128]{3,2,1,0:T(8,128)(2,1)S(1)}, bf16[2,4,128,128]{3,2,1,0:T(8,128)(2,1)S(1)}, u32[]{:S(2)}, u32[]{:S(2)}) collective-permute-start(bf16[2,4,128,128]{3,2,1,0:T(8,128)(2,1)S(1)} %get-tuple-element.54), channel_id=1, source_target_pairs={{0,4},{1,13},{2,6},{3,15},{4,0},{5,9},{6,2},{7,11},{8,12},{9,5},{1... | collective-permute-start | bytes 786440 | tf_op jit(solution)/shard_map/ppermute | solution.py:352
  103.4 10.1 %collective-permute-done.5.b_ref = bf16[2,4,128,128]{3,2,1,0:T(8,128)(2,1)S(1)} collective-permute-done((bf16[2,4,128,128]{3,2,1,0:T(8,128)(2,1)S(1)}, bf16[2,4,128,128]{3,2,1,0:T(8,128)(2,1)S(1)}, u32[]{:S(2)}, u32[]{:S(2)}) %collective-permute-start.5) | collective-permute-done | bytes 262176 | tf_op jit(solution)/shard_map/ppermute | solution.py:352
  113.5 0.6 shard_map.92
  114.1 3.5 %all-to-all-done.3.in_ref = bf16[8,2,128,128]{3,2,1,0:T(8,128)(2,1)S(1)} async-done(((bf16[8,2,128,128]{3,2,1,0:T(8,128)(2,1)}), bf16[8,2,128,128]{3,2,1,0:T(8,128)(2,1)S(1)}, u32[]{:S(2)}, u32[]{:S(2)}) %all-to-all-start.3) | async-done | bytes 524320 | tf_op jit(solution)/shard_map/all_to_all | solution.py:260
  117.6 1.4 %shard_map.94 = bf16[4,2,8,128,128]{4,3,2,1,0:T(8,128)(2,1)} custom-call(bf16[8,2,128,128]{3,2,1,0:T(8,128)(2,1)S(1)} %all-to-all-done.3.in_ref), custom_call_target="tpu_custom_call" | custom-call | bytes 3145728 | tf_op jit(solution)/shard_map/pallas_call | solution.py:248
  119.0 3.6 %all-to-all-start.4 = ((bf16[4,2,8,128,128]{4,3,2,1,0:T(8,128)(2,1)}), bf16[4,2,8,128,128]{4,3,2,1,0:T(8,128)(2,1)S(1)}, u32[]{:S(2)}, u32[]{:S(2)}) async-start(bf16[4,2,8,128,128]{4,3,2,1,0:T(8,128)(2,1)} %shard_map.94), calls=%async_computation.4 | async-start | bytes 4194304 | tf_op jit(solution)/shard_map/all_to_all | solution.py:260
  122.6 2.5 %collective-permute-start.6 = (bf16[1,4,128,128]{3,2,1,0:T(8,128)(2,1)S(1)}, bf16[1,4,128,128]{3,2,1,0:T(8,128)(2,1)S(1)}, u32[]{:S(2)}, u32[]{:S(2)}) collective-permute-start(bf16[1,4,128,128]{3,2,1,0:T(8,128)(2,1)S(1)} %get-tuple-element.58), channel_id=1, source_target_pairs={{0,8},{1,9},{2,10},{3,11},{4,12},{5,13},{6,14},{7,15},{8,0},{9,1},... | collective-permute-start | bytes 393224 | tf_op jit(solution)/shard_map/ppermute | solution.py:362
  125.1 11.7 %collective-permute-done.6.b_ref = bf16[1,4,128,128]{3,2,1,0:T(8,128)(2,1)S(1)} collective-permute-done((bf16[1,4,128,128]{3,2,1,0:T(8,128)(2,1)S(1)}, bf16[1,4,128,128]{3,2,1,0:T(8,128)(2,1)S(1)}, u32[]{:S(2)}, u32[]{:S(2)}) %collective-permute-start.6) | collective-permute-done | bytes 131104 | tf_op jit(solution)/shard_map/ppermute | solution.py:362
  136.7 0.8 shard_map.93
  137.5 0.0 all-to-all-done.4.in_ref
  137.5 1.4 shard_map.95
Async XLA Ops:
  28.7 11.1 %collective-permute-start = (bf16[4,4,128,128]{3,2,1,0:T(8,128)(2,1)S(1)}, bf16[4,4,128,128]{3,2,1,0:T(8,128)(2,1)S(1)}, u32[]{:S(2)}, u32[]{:S(2)}) collective-permute-start(bf16[4,4,128,128]{3,2,1,0:T(8,128)(2,1)S(1)} %all_to_all.25.refs_0_), channel_id=1, source_target_pairs={{0,2},{1,15},{2,0},{3,5},{4,6},{5,3},{6,4},{7,9},{8,10},{9,7},{10,... | collective-permute-start | bytes 1572872 | tf_op jit(solution)/shard_map/ppermute | solution.py:327
  31.7 0.7 copy-start.3
  35.1 13.6 %copy-start = (bf16[32,128,128]{2,1,0:T(8,128)(2,1)}, bf16[32,128,128]{2,1,0:T(8,128)(2,1)S(1)}, u32[]{:S(2)}) copy-start(bf16[32,128,128]{2,1,0:T(8,128)(2,1)S(1)} %get-tuple-element.40.refs_5_.down_ref) | copy-start | bytes 3145732
  35.2 6.6 %collective-permute-start.1 = (bf16[4,4,128,128]{3,2,1,0:T(8,128)(2,1)S(1)}, bf16[4,4,128,128]{3,2,1,0:T(8,128)(2,1)}, u32[]{:S(2)}, u32[]{:S(2)}) collective-permute-start(bf16[4,4,128,128]{3,2,1,0:T(8,128)(2,1)S(1)} %all_to_all.25.refs_0_), channel_id=1, source_target_pairs={{0,1},{1,0},{2,3},{3,2},{4,5},{5,4},{6,7},{7,6},{8,9},{9,8},{10,11... | collective-permute-start | bytes 1572872 | tf_op jit(solution)/shard_map/ppermute | solution.py:329
  39.8 3.9 %collective-permute-start.2 = (bf16[4,4,128,128]{3,2,1,0:T(8,128)(2,1)S(1)}, bf16[4,4,128,128]{3,2,1,0:T(8,128)(2,1)}, u32[]{:S(2)}, u32[]{:S(2)}) collective-permute-start(bf16[4,4,128,128]{3,2,1,0:T(8,128)(2,1)S(1)} %collective-permute-done.refs_1_), channel_id=1, source_target_pairs={{0,1},{1,0},{2,3},{3,2},{4,5},{5,4},{6,7},{7,6},{8,9},{9,8},{10,11... | collective-permute-start | bytes 1572872 | tf_op jit(solution)/shard_map/ppermute | solution.py:329
  48.7 18.9 %all-to-all-start.1 = ((bf16[4,2,8,128,128]{4,3,2,1,0:T(8,128)(2,1)}), bf16[4,2,8,128,128]{4,3,2,1,0:T(8,128)(2,1)S(1)}, u32[]{:S(2)}, u32[]{:S(2)}) async-start(bf16[4,2,8,128,128]{4,3,2,1,0:T(8,128)(2,1)} %get-tuple-element.41), calls=%async_computation.1 | async-start | bytes 4194304 | tf_op jit(solution)/shard_map/all_to_all | solution.py:260
  53.1 1.2 copy-start.1
  54.3 1.0 copy-start.2
  57.2 6.7 %collective-permute-start.3 = (bf16[8,4,128,128]{3,2,1,0:T(8,128)(2,1)S(1)}, bf16[8,4,128,128]{3,2,1,0:T(8,128)(2,1)S(1)}, u32[]{:S(2)}, u32[]{:S(2)}) collective-permute-start(bf16[8,4,128,128]{3,2,1,0:T(8,128)(2,1)S(1)} %get-tuple-element.44), channel_id=1, source_target_pairs={{0,1},{1,0},{2,3},{3,2},{4,5},{5,4},{6,7},{7,6},{8,9},{9,8},{10,11... | collective-permute-start | bytes 3145736 | tf_op jit(solution)/shard_map/ppermute | solution.py:332
  68.7 26.3 %all-to-all-start.2 = ((bf16[8,2,128,128]{3,2,1,0:T(8,128)(2,1)}), bf16[8,2,128,128]{3,2,1,0:T(8,128)(2,1)S(1)}, u32[]{:S(2)}, u32[]{:S(2)}) async-start(bf16[8,2,128,128]{3,2,1,0:T(8,128)(2,1)} %shard_map.89), calls=%async_computation.2 | async-start | bytes 1048576 | tf_op jit(solution)/shard_map/all_to_all | solution.py:260
  78.7 11.1 %collective-permute-start.4 = (bf16[4,4,128,128]{3,2,1,0:T(8,128)(2,1)S(1)}, bf16[4,4,128,128]{3,2,1,0:T(8,128)(2,1)S(1)}, u32[]{:S(2)}, u32[]{:S(2)}) collective-permute-start(bf16[4,4,128,128]{3,2,1,0:T(8,128)(2,1)S(1)} %get-tuple-element.49), channel_id=1, source_target_pairs={{0,2},{1,15},{2,0},{3,5},{4,6},{5,3},{6,4},{7,9},{8,10},{9,7},{10,... | collective-permute-start | bytes 1572872 | tf_op jit(solution)/shard_map/ppermute | solution.py:348
  95.8 21.7 %all-to-all-start.3 = ((bf16[8,2,128,128]{3,2,1,0:T(8,128)(2,1)}), bf16[8,2,128,128]{3,2,1,0:T(8,128)(2,1)S(1)}, u32[]{:S(2)}, u32[]{:S(2)}) async-start(bf16[8,2,128,128]{3,2,1,0:T(8,128)(2,1)} %shard_map.91), calls=%async_computation.3 | async-start | bytes 1048576 | tf_op jit(solution)/shard_map/all_to_all | solution.py:260
  101.5 12.0 %collective-permute-start.5 = (bf16[2,4,128,128]{3,2,1,0:T(8,128)(2,1)S(1)}, bf16[2,4,128,128]{3,2,1,0:T(8,128)(2,1)S(1)}, u32[]{:S(2)}, u32[]{:S(2)}) collective-permute-start(bf16[2,4,128,128]{3,2,1,0:T(8,128)(2,1)S(1)} %get-tuple-element.54), channel_id=1, source_target_pairs={{0,4},{1,13},{2,6},{3,15},{4,0},{5,9},{6,2},{7,11},{8,12},{9,5},{1... | collective-permute-start | bytes 786440 | tf_op jit(solution)/shard_map/ppermute | solution.py:352
  119.0 18.5 %all-to-all-start.4 = ((bf16[4,2,8,128,128]{4,3,2,1,0:T(8,128)(2,1)}), bf16[4,2,8,128,128]{4,3,2,1,0:T(8,128)(2,1)S(1)}, u32[]{:S(2)}, u32[]{:S(2)}) async-start(bf16[4,2,8,128,128]{4,3,2,1,0:T(8,128)(2,1)} %shard_map.94), calls=%async_computation.4 | async-start | bytes 4194304 | tf_op jit(solution)/shard_map/all_to_all | solution.py:260
  122.6 14.1 %collective-permute-start.6 = (bf16[1,4,128,128]{3,2,1,0:T(8,128)(2,1)S(1)}, bf16[1,4,128,128]{3,2,1,0:T(8,128)(2,1)S(1)}, u32[]{:S(2)}, u32[]{:S(2)}) collective-permute-start(bf16[1,4,128,128]{3,2,1,0:T(8,128)(2,1)S(1)} %get-tuple-element.58), channel_id=1, source_target_pairs={{0,8},{1,9},{2,10},{3,11},{4,12},{5,13},{6,14},{7,15},{8,0},{9,1},... | collective-permute-start | bytes 393224 | tf_op jit(solution)/shard_map/ppermute | solution.py:362
